TPU v7x, 32 devices: a whole 2x2x4 slice. The times are simulated.
32 devices in a mesh: dp: 8 (over z, core), tensor: 4 (over y, x).
Axes of the slice: x: 2, y: 2, z: 4, core: 2. Of those that a mesh axis runs over, the one named last changes fastest.
Arguments:
- tokens: bfloat16 [8, 2048, 2048], P('dp', 'tensor'), may hold values from -6 to 6
- in_weight: bfloat16 [3, 2048, 2048], P(None, 'dp', 'tensor'), may hold values from -0.125 to 0.125
- conv_taps: float32 [3, 2048], replicated, may hold values from -3.5 to 3.5
- out_weight: bfloat16 [2048, 2048], P('tensor', 'dp'), may hold values from -0.125 to 0.125
- gate_weight: bfloat16 [2048, 8192], P('dp', 'tensor'), may hold values from -0.125 to 0.125
- up_weight: bfloat16 [2048, 8192], P('dp', 'tensor'), may hold values from -0.125 to 0.125
- down_weight: bfloat16 [8192, 2048], P('tensor', 'dp'), may hold values from -0.125 to 0.125
- norm_gain1: float32 [2048], replicated, may hold values from 0.1 to 1.9
- norm_gain2: float32 [2048], replicated, may hold values from 0.1 to 1.9
- out_grad: bfloat16 [8, 2048, 2048], P('dp', 'tensor'), may hold values from -6 to 6
Outputs:
- block_out: bfloat16 [8, 2048, 2048], P('dp', 'tensor')
- tokens_grad: float32 [8, 2048, 2048], P('dp', 'tensor')
- in_weight_grad: float32 [3, 2048, 2048], P(None, 'dp', 'tensor')
- conv_taps_grad: float32 [3, 2048], replicated
- out_weight_grad: float32 [2048, 2048], P('tensor', 'dp')
- gate_weight_grad: float32 [2048, 8192], P('dp', 'tensor')
- up_weight_grad: float32 [2048, 8192], P('dp', 'tensor')
- down_weight_grad: float32 [8192, 2048], P('tensor', 'dp')
- gain1_grad: float32 [2048], replicated
- gain2_grad: float32 [2048], replicated
All inputs are finite; a program needn't handle non-finite values.
Results may differ from a plain program's by a relative error of at most 0.015.
Values may be sent and summed in bfloat16 or wider, within the bound.
No kernel may reach another device: no remote copies, remote signals or barrier semaphores. Data moves between devices by JAX's collectives and lax.ppermute only.
A program may use at most 256 MiB of HBM per device.

v0:
```python
import jax
import jax.numpy as jnp
from jax import lax
from jax.sharding import PartitionSpec as P

EPS = 1e-05


def rms_scale(values):
    return lax.rsqrt(jnp.mean(values * values, axis=-1, keepdims=True) + EPS)


def causal_conv(values, taps):
    padded = jnp.pad(values, ((0, 0), (2, 0), (0, 0)))
    return taps[0] * padded[:, :-2] + taps[1] * padded[:, 1:-1] + taps[2] * padded[:, 2:]


def conv_back(grad, values, taps):
    length = grad.shape[1]
    after = jnp.pad(grad, ((0, 0), (0, 2), (0, 0)))
    back = taps[2] * after[:, :-2] + taps[1] * after[:, 1:-1] + taps[0] * after[:, 2:]
    before = jnp.pad(values, ((0, 0), (2, 0), (0, 0)))
    tap_grads = jnp.stack(
        [jnp.sum(grad * before[:, j : j + length], axis=(0, 1)) for j in range(3)]
    )
    return (back, tap_grads)


def norm_back(hidden, scale, gain, grad):
    scaled = gain * grad
    back = scale * scaled - hidden * scale**3 * jnp.mean(scaled * hidden, axis=-1, keepdims=True)
    return (back, jnp.sum(grad * hidden * scale, axis=(0, 1)))


def local(
    tokens,
    in_weight,
    conv_taps,
    out_weight,
    gate_weight,
    up_weight,
    down_weight,
    norm_gain1,
    norm_gain2,
    out_grad,
):
    single_float32 = jnp.float32
    bf16 = jnp.bfloat16
    chans = out_weight.shape[0]
    width = conv_taps.shape[1]
    offset = lax.axis_index("tensor") * chans
    taps = lax.dynamic_slice_in_dim(conv_taps, offset, chans, 1)
    input_weight_complete, output_weight_complete = (
        lax.all_gather(in_weight, "dp", axis=1, tiled=True),
        lax.all_gather(out_weight, "dp", axis=1, tiled=True),
    )
    hidden = tokens.astype(single_float32)
    scale1 = rms_scale(hidden)
    normed = (hidden * scale1 * norm_gain1).astype(bf16)
    first_normed_total = lax.all_gather(normed, "tensor", axis=1, tiled=True)
    projection_rows = jnp.einsum(
        "hpt,vtx->vhpx",
        first_normed_total,
        input_weight_complete,
        preferred_element_type=single_float32,
    )
    bgate, cgate, xgate = (projection_rows[0], projection_rows[1], projection_rows[2])
    mixed_in = bgate * xgate
    conv = causal_conv(mixed_in, taps)
    output_gate = (cgate * conv).astype(bf16)
    branch_partial = jnp.einsum(
        "xbu,um->xbm", output_gate, output_weight_complete, preferred_element_type=single_float32
    )
    branch = lax.psum_scatter(branch_partial, "tensor", scatter_dimension=1, tiled=True)
    second = hidden + branch
    scale2 = rms_scale(second)
    normed2 = (second * scale2 * norm_gain2).astype(bf16)
    second_normed_total = lax.all_gather(normed2, "tensor", axis=1, tiled=True)
    gate_weight_complete, upward_weight_complete, down_weight_complete = (
        lax.all_gather(gate_weight, "dp", axis=0, tiled=True),
        lax.all_gather(up_weight, "dp", axis=0, tiled=True),
        lax.all_gather(down_weight, "dp", axis=1, tiled=True),
    )
    gate_rows = jnp.einsum(
        "gta,am->gtm",
        second_normed_total,
        gate_weight_complete,
        preferred_element_type=single_float32,
    )
    upward_rows = jnp.einsum(
        "gta,am->gtm",
        second_normed_total,
        upward_weight_complete,
        preferred_element_type=single_float32,
    )
    sigma = jax.nn.sigmoid(gate_rows)
    silu_gate = gate_rows * sigma
    activation_rows = (silu_gate * upward_rows).astype(bf16)
    feedforward_partial = jnp.einsum(
        "naw,wx->nax", activation_rows, down_weight_complete, preferred_element_type=single_float32
    )
    ffn = lax.psum_scatter(
        feedforward_partial.astype(jnp.bfloat16), "tensor", scatter_dimension=1, tiled=True
    ).astype(jnp.float32)
    block_out = (second + ffn).astype(bf16)
    (
        input_weight_backward,
        output_weight_backward,
        gate_weight_backward,
        upward_weight_backward,
        down_weight_backward,
    ) = (
        input_weight_complete,
        output_weight_complete,
        gate_weight_complete,
        upward_weight_complete,
        down_weight_complete,
    )
    gradient_total = lax.all_gather(out_grad, "tensor", axis=1, tiled=True)
    down_gradient_rows = jnp.einsum(
        "cxu,cxr->ur", activation_rows, gradient_total, preferred_element_type=single_float32
    )
    activation_gradient = jnp.einsum(
        "bqw,rw->bqr", gradient_total, down_weight_backward, preferred_element_type=single_float32
    )
    gate_gradient = (
        activation_gradient * upward_rows * sigma * (1.0 + gate_rows * (1.0 - sigma))
    ).astype(bf16)
    upper_gradient = (activation_gradient * silu_gate).astype(bf16)
    gate_gradient_rows = jnp.einsum(
        "bkr,bki->ri", second_normed_total, gate_gradient, preferred_element_type=single_float32
    )
    upward_gradient_rows = jnp.einsum(
        "bkr,bki->ri", second_normed_total, upper_gradient, preferred_element_type=single_float32
    )
    second_normed_gradient_partial = jnp.einsum(
        "ovx,ix->ovi", gate_gradient, gate_weight_backward, preferred_element_type=single_float32
    )
    second_normed_gradient_partial = second_normed_gradient_partial + jnp.einsum(
        "ovx,ix->ovi", upper_gradient, upward_weight_backward, preferred_element_type=single_float32
    )
    gate_owned, up_owned, down_owned = (
        lax.psum_scatter(
            gate_gradient_rows.astype(jnp.bfloat16), "dp", scatter_dimension=0, tiled=True
        ).astype(jnp.float32),
        lax.psum_scatter(
            upward_gradient_rows.astype(jnp.bfloat16), "dp", scatter_dimension=0, tiled=True
        ).astype(jnp.float32),
        lax.psum_scatter(
            down_gradient_rows.astype(jnp.bfloat16), "dp", scatter_dimension=1, tiled=True
        ).astype(jnp.float32),
    )
    dnormed2 = lax.psum_scatter(
        second_normed_gradient_partial, "tensor", scatter_dimension=1, tiled=True
    )
    dsecond_norm, gain2_part = norm_back(second, scale2, norm_gain2, dnormed2)
    dsecond = out_grad.astype(single_float32) + dsecond_norm
    branch_gradient_total = lax.all_gather(dsecond.astype(bf16), "tensor", axis=1, tiled=True)
    output_weight_gradient = jnp.einsum(
        "jez,jeb->zb", output_gate, branch_gradient_total, preferred_element_type=single_float32
    )
    output_gate_gradient = jnp.einsum(
        "abk,fk->abf",
        branch_gradient_total,
        output_weight_backward,
        preferred_element_type=single_float32,
    )
    dcgate = output_gate_gradient * conv
    dconv = output_gate_gradient * cgate
    dmixed, tap_part = conv_back(dconv, mixed_in, taps)
    projection_gradient = jnp.stack([dmixed * xgate, dcgate, dmixed * bgate]).astype(bf16)
    input_weight_gradient = jnp.einsum(
        "htz,mhtg->mzg",
        first_normed_total,
        projection_gradient,
        preferred_element_type=single_float32,
    )
    first_normed_gradient_partial = jnp.einsum(
        "ohrs,ons->hrn",
        projection_gradient,
        input_weight_backward,
        preferred_element_type=single_float32,
    )
    in_owned, out_owned = (
        lax.psum_scatter(
            input_weight_gradient.astype(jnp.bfloat16), "dp", scatter_dimension=1, tiled=True
        ).astype(jnp.float32),
        lax.psum_scatter(
            output_weight_gradient.astype(jnp.bfloat16), "dp", scatter_dimension=1, tiled=True
        ).astype(jnp.float32),
    )
    dnormed = lax.psum_scatter(
        first_normed_gradient_partial.astype(jnp.bfloat16),
        "tensor",
        scatter_dimension=1,
        tiled=True,
    ).astype(jnp.float32)
    dhidden_norm, gain1_part = norm_back(hidden, scale1, norm_gain1, dnormed)
    tokens_grad = dsecond + dhidden_norm
    tap_wide = lax.dynamic_update_slice_in_dim(
        jnp.zeros((3, width), single_float32), tap_part, offset, 1
    )
    tap_total, gain1_total, gain2_total = lax.psum(
        (tap_wide, gain1_part, gain2_part), ("dp", "tensor")
    )
    return (
        block_out,
        tokens_grad,
        in_owned,
        tap_total,
        out_owned,
        gate_owned,
        up_owned,
        down_owned,
        gain1_total,
        gain2_total,
    )


def solution(mesh):
    in_specs = (
        P("dp", "tensor", None),
        P(None, "dp", "tensor"),
        P(),
        P("tensor", "dp"),
        P("dp", "tensor"),
        P("dp", "tensor"),
        P("tensor", "dp"),
        P(),
        P(),
        P("dp", "tensor", None),
    )
    out_specs = (
        P("dp", "tensor", None),
        P("dp", "tensor", None),
        P(None, "dp", "tensor"),
        P(),
        P("tensor", "dp"),
        P("dp", "tensor"),
        P("dp", "tensor"),
        P("tensor", "dp"),
        P(),
        P(),
    )
    return jax.shard_map(local, mesh=mesh, in_specs=in_specs, out_specs=out_specs, check_vma=False)
```

profile of v0, /device:TPU:0, one launch (start us, length us, event | category | flops | bytes accessed | tf_op | source)
XLA Modules:
  0.0 1739.9 jit_solution(10525292303862076047)
XLA Ops:
  15.5 61.6 %all-gather.12.cloned.1.call-done = bf16[3,2048,512]{2,1,0:T(8,128)(2,1)} async-done(((bf16[3,256,512]{2,1,0:T(8,128)(2,1)}), bf16[3,2048,512]{2,1,0:T(8,128)(2,1)}) %all-gather.12.cloned.1.call-update) | async-done | bytes 6291472 | tf_op jit(solution)/shard_map/all_gather | solution.py:54
  77.1 88.7 %all-gather.10.cloned.1.call-done = bf16[1,2048,2048]{2,1,0:T(8,128)(2,1)} async-done(((bf16[1,512,2048]{2,1,0:T(8,128)(2,1)}), bf16[1,2048,2048]{2,1,0:T(8,128)(2,1)}) %all-gather.10.cloned.1.call-update) | async-done | bytes 8388624 | tf_op jit(solution)/shard_map/all_gather | solution.py:60
  165.8 17.4 fusion.19
  198.3 12.5 convolution_bitcast_fusion
  211.9 151.9 %reduce-scatter.10.cloned.1.call-done = f32[1,512,2048]{2,1,0:T(8,128)} async-done(((f32[1,2048,2048]{2,1,0:T(8,128)}), f32[1,512,2048]{2,1,0:T(8,128)}) %reduce-scatter.10.cloned.1.call-update) | async-done | bytes 4194320 | tf_op jit(solution)/shard_map/reduce_scatter | solution.py:74
  372.7 74.7 %all-gather.20.cloned.1.call-done = bf16[2048,2048]{1,0:T(8,128)(2,1)} async-done(((bf16[256,2048]{1,0:T(8,128)(2,1)}), bf16[2048,2048]{1,0:T(8,128)(2,1)}) %all-gather.20.cloned.1.call-update) | async-done | bytes 8388624 | tf_op jit(solution)/shard_map/all_gather | solution.py:81
  447.4 88.4 %all-gather.16.cloned.1.call-done = bf16[1,2048,2048]{2,1,0:T(8,128)(2,1)} async-done(((bf16[1,512,2048]{2,1,0:T(8,128)(2,1)}), bf16[1,2048,2048]{2,1,0:T(8,128)(2,1)}) %all-gather.16.cloned.1.call-update) | async-done | bytes 8388624 | tf_op jit(solution)/shard_map/all_gather | solution.py:78
  535.9 24.2 %fusion.13 = f32[2048,2048]{1,0:T(8,128)} fusion(bf16[2048,2048]{1,0:T(8,128)(2,1)} %all-gather.20.cloned.1.call-done, bf16[1,2048,2048]{2,1,0:T(8,128)(2,1)} %all-gather.16.cloned.1.call-done), kind=kOutput, calls=%fused_computation.26 | convolution fusion | flops 17179869184 | bytes 33554432 | tf_op jit(solution)/shard_map/gta,am->gtm/dot_general | solution.py:90
  560.0 59.5 %all-gather.18.cloned.1.call-done = bf16[2048,2048]{1,0:T(8,128)(2,1)} async-done(((bf16[256,2048]{1,0:T(8,128)(2,1)}), bf16[2048,2048]{1,0:T(8,128)(2,1)}) %all-gather.18.cloned.1.call-update) | async-done | bytes 8388624 | tf_op jit(solution)/shard_map/all_gather | solution.py:80
  619.5 24.2 %fusion.15 = f32[2048,2048]{1,0:T(8,128)} fusion(bf16[2048,2048]{1,0:T(8,128)(2,1)} %all-gather.18.cloned.1.call-done, bf16[1,2048,2048]{2,1,0:T(8,128)(2,1)} %all-gather.16.cloned.1.call-done), kind=kOutput, calls=%fused_computation.28 | convolution fusion | flops 17179869184 | bytes 33554432 | tf_op jit(solution)/shard_map/gta,am->gtm/dot_general | solution.py:84
  643.7 63.9 %all-gather.24.cloned.1.call-done = bf16[1,2048,2048]{2,1,0:T(8,128)(2,1)} async-done(((bf16[1,512,2048]{2,1,0:T(8,128)(2,1)}), bf16[1,2048,2048]{2,1,0:T(8,128)(2,1)}) %all-gather.24.cloned.1.call-update) | async-done | bytes 8388624 | tf_op jit(solution)/shard_map/all_gather | solution.py:119
  707.6 84.1 %all-gather.22.cloned.1.call-done = bf16[2048,2048]{1,0:T(8,128)(2,1)} async-done(((bf16[2048,256]{1,0:T(8,128)(2,1)}), bf16[2048,2048]{1,0:T(8,128)(2,1)}) %all-gather.22.cloned.1.call-update) | async-done | bytes 8388624 | tf_op jit(solution)/shard_map/all_gather | solution.py:82
  791.7 36.6 %multiply_convert_fusion = (bf16[2048,2048]{1,0:T(8,128)(2,1)}, bf16[2048,2048]{1,0:T(8,128)(2,1)}, bf16[2048,2048]{1,0:T(8,128)(2,1)}) fusion(f32[2048,2048]{1,0:T(8,128)} %fusion.15, f32[2048,2048]{1,0:T(8,128)} %fusion.13, bf16[2048,2048]{1,0:T(8,128)(2,1)} %all-gather.22.cloned.1.call-done, bf16[1,2048,2048]{2,1,0:T(8,128)(2,1)} %all-gather.24.cloned.1.call-done), kind=kOutput, calls=%fused_computation.2 | convolution fusion | flops 17242783744 | bytes 75497472 | tf_op jit(solution)/shard_map/bqw,rw->bqr/dot_general | solution.py:123
  828.3 24.3 %fusion.57 = f32[2048,2048]{1,0:T(8,128)} fusion(bf16[2048,2048]{1,0:T(8,128)(2,1)} %get-tuple-element.39, bf16[2048,2048]{1,0:T(8,128)(2,1)} %all-gather.18.cloned.1.call-done), kind=kOutput, calls=%fused_computation.91 | convolution fusion | flops 17179869184 | bytes 33554432 | tf_op jit(solution)/shard_map/ovx,ix->ovi/dot_general | solution.py:136
  852.6 26.5 %add_bitcast_fusion = f32[1,2048,2048]{2,1,0:T(8,128)} fusion(f32[2048,2048]{1,0:T(8,128)} %fusion.57, bf16[2048,2048]{1,0:T(8,128)(2,1)} %get-tuple-element.38, bf16[2048,2048]{1,0:T(8,128)(2,1)} %all-gather.20.cloned.1.call-done), kind=kOutput, calls=%fused_computation.1 | convolution fusion | flops 17184063488 | bytes 50331648 | tf_op jit(solution)/shard_map/ovx,ix->ovi/dot_general | solution.py:139
  879.2 23.7 %convert_bitcast_fusion = bf16[1,2048,2048]{2,1,0:T(8,128)(2,1)} fusion(bf16[2048,2048]{1,0:T(8,128)(2,1)} %get-tuple-element.40, bf16[2048,2048]{1,0:T(8,128)(2,1)} %all-gather.22.cloned.1.call-done), kind=kOutput, calls=%fused_computation.34 | convolution fusion | flops 17184063488 | bytes 25165824 | tf_op jit(solution)/shard_map/naw,wx->nax/dot_general | solution.py:99
  902.9 128.4 %reduce-scatter.14.cloned.1.call-done = f32[1,512,2048]{2,1,0:T(8,128)} async-done(((f32[1,2048,2048]{2,1,0:T(8,128)}), f32[1,512,2048]{2,1,0:T(8,128)}) %reduce-scatter.14.cloned.1.call-update) | async-done | bytes 4194320 | tf_op jit(solution)/shard_map/reduce_scatter | solution.py:153
  1036.4 84.4 %reduce-scatter.12.cloned.1.call-done = bf16[1,512,2048]{2,1,0:T(8,128)(2,1)} async-done(((bf16[1,2048,2048]{2,1,0:T(8,128)(2,1)}), bf16[1,512,2048]{2,1,0:T(8,128)(2,1)}) %reduce-scatter.12.cloned.1.call-update) | async-done | bytes 2097168 | tf_op jit(solution)/shard_map/reduce_scatter | solution.py:102
  1127.7 24.1 %fusion.21 = bf16[2048,2048]{1,0:T(8,128)(2,1)} fusion(bf16[2048,2048]{1,0:T(8,128)(2,1)} %get-tuple-element.39, bf16[1,2048,2048]{2,1,0:T(8,128)(2,1)} %all-gather.16.cloned.1.call-done), kind=kOutput, calls=%fused_computation.35 | convolution fusion | flops 17184063488 | bytes 25165824 | tf_op jit(solution)/shard_map/bkr,bki->ri/dot_general | solution.py:130
  1151.9 23.7 %fusion.24 = bf16[2048,2048]{1,0:T(8,128)(2,1)} fusion(bf16[2048,2048]{1,0:T(8,128)(2,1)} %get-tuple-element.38, bf16[1,2048,2048]{2,1,0:T(8,128)(2,1)} %all-gather.16.cloned.1.call-done), kind=kOutput, calls=%fused_computation.36 | convolution fusion | flops 17184063488 | bytes 25165824 | tf_op jit(solution)/shard_map/bkr,bki->ri/dot_general | solution.py:133
  1175.7 24.0 %fusion.27 = bf16[2048,2048]{1,0:T(8,128)(2,1)} fusion(bf16[2048,2048]{1,0:T(8,128)(2,1)} %get-tuple-element.40, bf16[1,2048,2048]{2,1,0:T(8,128)(2,1)} %all-gather.24.cloned.1.call-done), kind=kOutput, calls=%fused_computation.37 | convolution fusion | flops 17184063488 | bytes 25165824 | tf_op jit(solution)/shard_map/cxu,cxr->ur/dot_general | solution.py:120
  1199.7 15.6 all-gather.26.cloned.1.call-done
  1224.6 15.0 multiply_reduce_fusion.2
  1248.6 17.6 %convert_bitcast_fusion.1 = bf16[3,2048,512]{1,2,0:T(8,128)(2,1)} fusion(bf16[1,2048,2048]{2,1,0:T(8,128)(2,1)} %all-gather.10.cloned.1.call-done, bf16[1,2048,512]{2,1,0:T(8,128)(2,1)S(1)} %fusion.47, bf16[1,2048,512]{2,1,0:T(8,128)(2,1)S(1)} %get-tuple-element.41, bf16[1,2048,512]{2,1,0:T(8,128)(2,1)S(1)} %get-tuple-element.30), kind=kOutput, calls=%fused_computation.40 | convolution fusion | flops 12894339072 | bytes 20971520 | tf_op jit(solution)/shard_map/htz,mhtg->mzg/dot_general | solution.py:172
  1266.3 18.9 %fusion.30 = bf16[1,2048,2048]{2,1,0:T(8,128)(2,1)} fusion(bf16[3,2048,512]{2,1,0:T(8,128)(2,1)} %all-gather.12.cloned.1.call-done, bf16[1,2048,512]{2,1,0:T(8,128)(2,1)S(1)} %fusion.47, bf16[1,2048,512]{2,1,0:T(8,128)(2,1)} %copy-done.25, bf16[1,2048,512]{2,1,0:T(8,128)(2,1)} %copy-done.8), kind=kOutput, calls=%fused_computation.38 | convolution fusion | flops 12895387648 | bytes 20971520 | tf_op jit(solution)/shard_map/ohrs,ons->hrn/dot_general | solution.py:178
  1285.2 22.2 %reduce-scatter.22.cloned.1.call-done = bf16[256,2048]{1,0:T(8,128)(2,1)} async-done(((bf16[2048,2048]{1,0:T(8,128)(2,1)}), bf16[256,2048]{1,0:T(8,128)(2,1)}) %reduce-scatter.22.cloned.1.call-update) | async-done | bytes 1048592 | tf_op jit(solution)/shard_map/reduce_scatter | solution.py:143
  1310.2 87.5 %reduce-scatter.24.cloned.1.call-done = bf16[256,2048]{1,0:T(8,128)(2,1)} async-done(((bf16[2048,2048]{1,0:T(8,128)(2,1)}), bf16[256,2048]{1,0:T(8,128)(2,1)}) %reduce-scatter.24.cloned.1.call-update) | async-done | bytes 1048592 | tf_op jit(solution)/shard_map/reduce_scatter | solution.py:146
  1400.5 87.4 %reduce-scatter.26.cloned.1.call-done = bf16[2048,256]{1,0:T(8,128)(2,1)} async-done(((bf16[2048,2048]{1,0:T(8,128)(2,1)}), bf16[2048,256]{1,0:T(8,128)(2,1)}) %reduce-scatter.26.cloned.1.call-update) | async-done | bytes 1048592 | tf_op jit(solution)/shard_map/reduce_scatter | solution.py:149
  1496.4 28.0 %reduce-scatter.20.cloned.1.call-done = bf16[512,256]{1,0:T(8,128)(2,1)} async-done(((bf16[512,2048]{1,0:T(8,128)(2,1)}), bf16[512,256]{1,0:T(8,128)(2,1)}) %reduce-scatter.20.cloned.1.call-update) | async-done | bytes 262160 | tf_op jit(solution)/shard_map/reduce_scatter | solution.py:188
  1526.2 68.9 %reduce-scatter.18.cloned.1.call-done = bf16[3,256,512]{1,2,0:T(8,128)(2,1)} async-done(((bf16[3,2048,512]{1,2,0:T(8,128)(2,1)}), bf16[3,256,512]{1,2,0:T(8,128)(2,1)}) %reduce-scatter.18.cloned.1.call-update) | async-done | bytes 786448 | tf_op jit(solution)/shard_map/reduce_scatter | solution.py:185
  1597.6 85.5 %reduce-scatter.16.cloned.1.call-done = bf16[1,512,2048]{2,1,0:T(8,128)(2,1)} async-done(((bf16[1,2048,2048]{2,1,0:T(8,128)(2,1)}), bf16[1,512,2048]{2,1,0:T(8,128)(2,1)}) %reduce-scatter.16.cloned.1.call-update) | async-done | bytes 2097168 | tf_op jit(solution)/shard_map/reduce_scatter | solution.py:192
  1686.3 40.3 %all-reduce.2 = (f32[3,2048]{1,0:T(4,128)}, f32[2048]{0:T(1024)}, f32[2048]{0:T(1024)}) all-reduce(f32[3,2048]{1,0:T(4,128)S(1)} %maximum_dynamic-update-slice_fusion, f32[2048]{0:T(1024)S(1)} %get-tuple-element.24, f32[2048]{0:T(1024)S(1)} %copy-done.14), channel_id=1, replica_groups=mesh['dp'=8,'tensor'=4] {'dp','tensor'}, use_global_device_ids=true, to_apply=%region_12.13 | all-reduce | flops 10240 | bytes 81920 | tf_op jit(solution)/shard_map/psum | solution.py:203
  (115 shorter events, 91.2 us)
Async XLA Ops:
  7.2 69.9 %all-gather.12.cloned.1.call-start = ((), (), s32[]{:S(2)}) async-start(), calls=%async_computation.10 | async-start | bytes 7077888 | tf_op jit(solution)/shard_map/all_gather | solution.py:54
  7.9 157.9 %all-gather.10.cloned.1.call-start = ((), (), s32[]{:S(2)}) async-start(), calls=%async_computation.9 | async-start | bytes 10485760 | tf_op jit(solution)/shard_map/all_gather | solution.py:60
  13.8 184.5 %all-gather.14.cloned.1.call-start = ((), (), s32[]{:S(2)}) async-start(), calls=%async_computation.11 | async-start | bytes 2359296 | tf_op jit(solution)/shard_map/all_gather | solution.py:55
  14.5 349.3 %reduce-scatter.10.cloned.1.call-start = ((), (), s32[]{:S(2)}) async-start(), calls=%async_computation.12 | async-start | bytes 20971520 | tf_op jit(solution)/shard_map/reduce_scatter | solution.py:74
  15.5 168.8 %copy-start.17 = (f32[1,512]{1,0:T(1,128)}, f32[1,512]{1,0:T(1,128)S(1)}, u32[]{:S(2)}) copy-start(f32[1,512]{1,0:T(1,128)S(1)} %get-tuple-element.43) | copy-start | bytes 6148
  15.5 168.8 %copy-start.19 = (f32[1,512]{1,0:T(1,128)}, f32[1,512]{1,0:T(1,128)S(1)}, u32[]{:S(2)}) copy-start(f32[1,512]{1,0:T(1,128)S(1)} %get-tuple-element.44) | copy-start | bytes 6148
  15.5 168.8 %copy-start.21 = (f32[1,512]{1,0:T(1,128)}, f32[1,512]{1,0:T(1,128)S(1)}, u32[]{:S(2)}) copy-start(f32[1,512]{1,0:T(1,128)S(1)} %get-tuple-element.45) | copy-start | bytes 6148
  210.8 236.6 %all-gather.20.cloned.1.call-start = ((), (), s32[]{:S(2)}) async-start(), calls=%async_computation.15 | async-start | bytes 9437184 | tf_op jit(solution)/shard_map/all_gather | solution.py:81
  211.4 157.2 %copy-start.9 = (f32[2048]{0:T(1024)S(1)}, f32[2048]{0:T(1024)}, u32[]{:S(2)}) copy-start(f32[2048]{0:T(1024)} %param.18) | copy-start | bytes 24580
  211.4 324.4 %all-gather.16.cloned.1.call-start = ((), (), s32[]{:S(2)}) async-start(), calls=%async_computation.13 | async-start | bytes 10485760 | tf_op jit(solution)/shard_map/all_gather | solution.py:78
  370.4 249.1 %all-gather.18.cloned.1.call-start = ((), (), s32[]{:S(2)}) async-start(), calls=%async_computation.14 | async-start | bytes 9437184 | tf_op jit(solution)/shard_map/all_gather | solution.py:80
  371.2 336.4 %all-gather.24.cloned.1.call-start = ((), (), s32[]{:S(2)}) async-start(), calls=%async_computation.18 | async-start | bytes 10485760 | tf_op jit(solution)/shard_map/all_gather | solution.py:119
  371.9 419.8 %all-gather.22.cloned.1.call-start = ((), (), s32[]{:S(2)}) async-start(), calls=%async_computation.16 | async-start | bytes 9437184 | tf_op jit(solution)/shard_map/all_gather | solution.py:82
  372.6 658.7 %reduce-scatter.14.cloned.1.call-start = ((), (), s32[]{:S(2)}) async-start(), calls=%async_computation.19 | async-start | bytes 20971520 | tf_op jit(solution)/shard_map/reduce_scatter | solution.py:153
  879.1 241.7 %reduce-scatter.12.cloned.1.call-start = ((), (), s32[]{:S(2)}) async-start(), calls=%async_computation.17 | async-start | bytes 10485760 | tf_op jit(solution)/shard_map/reduce_scatter | solution.py:102
  902.8 128.5 %copy-start.10 = (f32[2048]{0:T(1024)S(1)}, f32[2048]{0:T(1024)}, u32[]{:S(2)}) copy-start(f32[2048]{0:T(1024)} %param.18) | copy-start | bytes 24580
  902.8 128.5 %copy-start.16 = (f32[512]{0:T(512)S(1)}, f32[512]{0:T(512)}, u32[]{:S(2)}) copy-start(f32[512]{0:T(512)} %copy-done.15) | copy-start | bytes 6148
  902.9 218.0 %copy-start.6 = (bf16[1,512,2048]{2,1,0:T(8,128)(2,1)S(1)}, bf16[1,512,2048]{2,1,0:T(8,128)(2,1)}, u32[]{:S(2)}) copy-start(bf16[1,512,2048]{2,1,0:T(8,128)(2,1)} %param.19) | copy-start | bytes 6291460
  902.9 218.0 %copy-start.23 = (f32[512]{0:T(512)S(1)}, f32[512]{0:T(512)}, u32[]{:S(2)}) copy-start(f32[512]{0:T(512)} %get-tuple-element.48) | copy-start | bytes 6148
  902.9 312.5 %all-gather.26.cloned.1.call-start = ((), (), s32[]{:S(2)}) async-start(), calls=%async_computation.20 | async-start | bytes 10485760 | tf_op jit(solution)/shard_map/all_gather | solution.py:158
  1127.6 179.8 %reduce-scatter.22.cloned.1.call-start = ((), (), s32[]{:S(2)}) async-start(), calls=%async_computation.24 | async-start | bytes 9437184 | tf_op jit(solution)/shard_map/reduce_scatter | solution.py:143
  1151.8 245.8 %reduce-scatter.24.cloned.1.call-start = ((), (), s32[]{:S(2)}) async-start(), calls=%async_computation.25 | async-start | bytes 9437184 | tf_op jit(solution)/shard_map/reduce_scatter | solution.py:146
  1175.7 312.2 %reduce-scatter.26.cloned.1.call-start = ((), (), s32[]{:S(2)}) async-start(), calls=%async_computation.26 | async-start | bytes 9437184 | tf_op jit(solution)/shard_map/reduce_scatter | solution.py:149
  1199.7 15.7 copy-start.7
  1199.7 324.7 %reduce-scatter.20.cloned.1.call-start = ((), (), s32[]{:S(2)}) async-start(), calls=%async_computation.23 | async-start | bytes 2359296 | tf_op jit(solution)/shard_map/reduce_scatter | solution.py:188
  1224.5 370.5 %reduce-scatter.18.cloned.1.call-start = ((), (), s32[]{:S(2)}) async-start(), calls=%async_computation.22 | async-start | bytes 7077888 | tf_op jit(solution)/shard_map/reduce_scatter | solution.py:185
  1266.3 416.8 %reduce-scatter.16.cloned.1.call-start = ((), (), s32[]{:S(2)}) async-start(), calls=%async_computation.21 | async-start | bytes 10485760 | tf_op jit(solution)/shard_map/reduce_scatter | solution.py:192
  1490.6 192.5 %copy-start.11 = (f32[2048]{0:T(1024)S(1)}, f32[2048]{0:T(1024)}, u32[]{:S(2)}) copy-start(f32[2048]{0:T(1024)} %param.17) | copy-start | bytes 24580
  1490.6 192.5 %copy-start.13 = (f32[512]{0:T(512)S(1)}, f32[512]{0:T(512)}, u32[]{:S(2)}) copy-start(f32[512]{0:T(512)} %copy-done.12) | copy-start | bytes 6148
  1496.3 186.8 %copy-start.3 = (bf16[1,512,2048]{2,1,0:T(8,128)(2,1)S(1)}, bf16[1,512,2048]{2,1,0:T(8,128)(2,1)}, u32[]{:S(2)}) copy-start(bf16[1,512,2048]{2,1,0:T(8,128)(2,1)} %param.10) | copy-start | bytes 6291460
  1496.3 190.0 %copy-start.14 = (f32[2048]{0:T(1024)S(1)}, f32[2048]{0:T(1024)}, u32[]{:S(2)}) copy-start(f32[2048]{0:T(1024)} %get-tuple-element.20) | copy-start | bytes 24580
  1496.3 230.3 %copy-start.24 = (f32[512]{0:T(512)S(1)}, f32[512]{0:T(512)}, u32[]{:S(2)}) copy-start(f32[512]{0:T(512)} %get-tuple-element.46) | copy-start | bytes 6148
  (12 other events, 80.3 us)
Sparse Core Ops, SparseCore 0:
  9.6 67.4 all-gather.11
  79.5 86.2 all-gather.9
  167.4 30.8 all-gather.13
  210.9 152.8 reduce-scatter.9
  365.3 82.0 all-gather.19
  449.7 86.1 all-gather.15
  537.4 82.0 all-gather.17
  621.4 86.1 all-gather.23
  709.2 82.4 all-gather.21
  879.3 152.0 reduce-scatter.13
  1034.4 86.4 reduce-scatter.11
  1127.8 87.5 all-gather.25
  1217.8 89.5 reduce-scatter.21
  1309.7 87.9 reduce-scatter.23
  1399.9 87.9 reduce-scatter.25
  1490.2 34.1 reduce-scatter.19
  1526.6 68.3 reduce-scatter.17
  1598.3 84.7 reduce-scatter.15
where the time goes:
time: 1750 us; the launch traced here: 1740 us
  waiting for transfers between devices  1290 us (74%)
  matrix products  322 us (18%)
  other arithmetic  60.8 us (3%)
  blocking collectives  40.3 us (2%)
    reduce_scatter x1, waiting for transfers between devices, local(): lax.psum_scatter(branch_partial, 'tensor', scatter_dimension=1, tiled=True)  152 us
    reduce_scatter x1, waiting for transfers between devices, local(): lax.psum_scatter(second_normed_gradient_partial, 'tensor', scatter_dimens...  128 us
    all_gather x1, waiting for transfers between devices, local(): first_normed_total = lax.all_gather(normed, 'tensor', axis=1, tiled=True)  88.7 us
    all_gather x1, waiting for transfers between devices, local(): second_normed_total = lax.all_gather(normed2, 'tensor', axis=1, tiled=True)  88.4 us
    reduce_scatter x1, waiting for transfers between devices, local(): lax.psum_scatter(upward_gradient_rows.astype(jnp.bfloat16), 'dp', scatter...  87.5 us
    reduce_scatter x1, waiting for transfers between devices, local(): lax.psum_scatter(down_gradient_rows.astype(jnp.bfloat16), 'dp', scatter_d...  87.4 us
    reduce_scatter x1, waiting for transfers between devices, local(): lax.psum_scatter(first_normed_gradient_partial.astype(jnp.bfloat16), 'ten...  85.5 us
    reduce_scatter x1, waiting for transfers between devices, local(): lax.psum_scatter(feedforward_partial.astype(jnp.bfloat16), 'tensor', scat...  84.4 us
  transfers between devices with their start and end apart: 18, of which 18 were waited for; matrix products, arithmetic and copies ran while one was open for 16% of the time, Pallas kernels for 0%

commit v1 on v0

v1 whole, which is shorter than its diff:
```python
import functools
import math

import jax
import jax.numpy as jnp
from jax import lax
from jax.experimental import pallas as pl
from jax.experimental.pallas import tpu as pltpu
from jax.sharding import PartitionSpec as P

EPS = 1e-05
BF = jnp.bfloat16
F32 = jnp.float32
VMEM_LIMIT = 58 * 2**20
COST = 0.2
NN = (((1,), (0,)), ((), ()))
NT = (((1,), (1,)), ((), ()))
TN = (((0,), (0,)), ((), ()))


def dot(a, b, dims):
    return lax.dot_general(a, b, dims, preferred_element_type=F32)


def after(value, *others):
    if not others:
        return value
    return lax.optimization_barrier((value, others))[0]


def first_after(pieces, *others):
    return [after(pieces[0], *others)] + list(pieces[1:])


def rms_scale(values):
    return lax.rsqrt(jnp.mean(values * values, axis=-1, keepdims=True) + EPS)


def norm_back(hidden, scale, gain, grad):
    scaled = gain * grad
    back = scale * scaled - hidden * scale**3 * jnp.mean(scaled * hidden, axis=-1, keepdims=True)
    return back, jnp.sum(grad * hidden * scale, axis=0)


class Square:
    def __init__(self, nt):
        self.nt = nt
        self.t = lax.axis_index("tensor")
        bits = [1 << i for i in range(int(math.log2(nt)))]
        self.orders = (bits, bits[::-1])
        self.lists = []
        for order in self.orders:
            seen = [0]
            for bit in order:
                seen = seen + [r ^ bit for r in seen]
            self.lists.append(seen)

    def flip(self, value, bit):
        return lax.ppermute(value, "tensor", [(t, t ^ bit) for t in range(self.nt)])

    def gather(self, rows, *gates):
        half = rows.shape[0] // 2
        curs = [rows[:half], rows[half:]]
        depth = len(self.orders[0])
        first = None
        for level in range(depth):
            came = [self.flip(c, o[level]) for c, o in zip(curs, self.orders)]
            first = first or came
            if level < depth - 1:
                curs = [after(jnp.concatenate([c, r]), *gates) for c, r in zip(curs, came)]
        return [curs[0], came[0], curs[1], came[1]], first

    def gather_steps(self, rows):
        half = rows.shape[0] // 2
        curs = [rows[:half], rows[half:]]
        depth = len(self.orders[0])
        gates = None
        for level in range(depth):
            came = [self.flip(c, o[level]) for c, o in zip(curs, self.orders)]
            gates = gates or (yield came)
            if level < depth - 1:
                curs = [after(jnp.concatenate([c, r]), *gates) for c, r in zip(curs, came)]
        yield [curs[0], came[0], curs[1], came[1]]

    def begin(self, far):
        return [self.flip(s, o[-1]) for s, o in zip(far, self.orders)]

    def finish(self, near, came, *gates):
        depth = len(self.orders[0])
        sends = came
        for level in range(depth - 1, -1, -1):
            total = [k.astype(F32) + r.astype(F32) for k, r in zip(near, came)]
            if level:
                half = total[0].shape[0] // 2
                near = [v[:half] for v in total]
                sends = [after(v[half:].astype(BF), *gates) for v in total]
                came = [self.flip(s, o[level - 1]) for s, o in zip(sends, self.orders)]
        return jnp.concatenate(total), sends

    def places(self):
        index = {}
        for h, seen in enumerate(self.lists):
            for i, r in enumerate(seen):
                index[r, h] = h * self.nt + i
        tables = [jnp.array([index[r, h] for r in range(self.nt)]) for h in range(2)]
        before, behind = [], []
        for h, seen in enumerate(self.lists):
            for r in seen:
                at = self.t ^ r
                if h == 1:
                    before.append(jnp.int32(index[r, 0]))
                    there = (jnp.minimum(at + 1, self.nt - 1)) ^ self.t
                    behind.append(jnp.where(at == self.nt - 1, -1, tables[0][there]))
                else:
                    behind.append(jnp.int32(index[r, 1]))
                    there = (jnp.maximum(at - 1, 0)) ^ self.t
                    before.append(jnp.where(at == 0, -1, tables[1][there]))
        return jnp.stack([jnp.stack(before), jnp.stack(behind)]).astype(jnp.int32)


def total_of(value, sizes):
    for axis, size in sizes:
        bit = 1
        while bit < size:
            value = value + lax.ppermute(value, axis, [(i, i ^ bit) for i in range(size)])
            bit *= 2
    return value


def call(name, body, grid, ins, outs, args, flops, scratch=(), scalars=(), aliases=None):
    held = lambda spec: pl.BlockSpec(memory_space=pl.ANY) if spec is None else pl.BlockSpec(
        spec[0],
        lambda j, *_: spec[1](j),
        **({"pipeline_mode": pl.Buffered(1)} if len(spec) > 2 and spec[2] == "held" else {}),
    )
    moved = sum(math.prod(a.shape) * a.dtype.itemsize for a in args)
    moved += sum(math.prod(o[2]) * jnp.dtype(o[3]).itemsize for o in outs)
    return pl.pallas_call(
        body,
        grid_spec=pltpu.PrefetchScalarGridSpec(
            num_scalar_prefetch=len(scalars),
            grid=(grid,),
            in_specs=[held(s) for s in ins],
            out_specs=[pl.BlockSpec(o[0], lambda j, *_, o=o: o[1](j)) for o in outs],
            scratch_shapes=list(scratch),
        ),
        out_shape=[jax.ShapeDtypeStruct(o[2], o[3]) for o in outs],
        name=name,
        input_output_aliases=aliases or {},
        compiler_params=pltpu.CompilerParams(vmem_limit_bytes=VMEM_LIMIT),
        cost_estimate=pl.CostEstimate(
            flops=int(flops * COST), bytes_accessed=int(moved * COST), transcendentals=0
        ),
    )(*scalars, *args)


def whole(a):
    return (a.shape, lambda j: (0,) * a.ndim, "held")


def columns(a, tile, start=0):
    return ((a.shape[0], tile), lambda j: (0, start + j))


def new_columns(rows, width, tile, dtype=BF):
    return ((rows, tile), lambda j: (0, j), (rows, width), dtype)


def gate_body(*refs):
    pieces, (gw, uw, act, silu, slope) = refs[:4], refs[4:]
    rows = pieces[0].shape[0]
    for i in range(4):
        at = pl.ds(i * rows, rows)
        gate = dot(pieces[i][...], gw[...], NN)
        up = dot(pieces[i][...], uw[...], NN)
        sig = jax.nn.sigmoid(gate)
        s = gate * sig
        act[at] = (s * up).astype(BF)
        silu[at] = s.astype(BF)
        slope[at] = (up * sig * (1.0 + gate * (1.0 - sig))).astype(BF)


def ffn_gate(pieces, gate, up):
    dim, width = gate.shape
    tokens = 4 * pieces[0].shape[0]
    tile = min(256, width)
    return call(
        "ffn_gate",
        gate_body,
        width // tile,
        [whole(p) for p in pieces] + [columns(gate, tile), columns(up, tile)],
        [new_columns(tokens, width, tile)] * 3,
        [*pieces, gate, up],
        4 * tokens * dim * width,
    )


def ffn_slope_body(*refs):
    pieces, (w, silu, slope, dgate, dup) = refs[:4], refs[4:]
    rows = pieces[0].shape[0]
    for i in range(4):
        at = pl.ds(i * rows, rows)
        dact = dot(pieces[i][...], w[...], NN)
        dgate[at] = (dact * slope[at].astype(F32)).astype(BF)
        dup[at] = (dact * silu[at].astype(F32)).astype(BF)


def ffn_slope(pieces, down, silu, slope):
    dim, width = down.shape
    tokens = 4 * pieces[0].shape[0]
    tile = min(512, width)
    return call(
        "ffn_slope",
        ffn_slope_body,
        width // tile,
        [whole(p) for p in pieces] + [columns(a, tile) for a in (down, silu, slope)],
        [new_columns(tokens, width, tile)] * 2,
        [*pieces, down, silu, slope],
        2 * tokens * dim * width,
    )


def weight_grad(pieces, b, into=None):
    rows, dim = pieces[0].shape
    width = b.shape[1]
    tile = next(t for t in (512, 384, 256) if width % t == 0)
    step = min(512, dim)

    def body(*refs):
        left, b_ref, out = refs[:4], refs[4], refs[-1]
        for d in range(0, dim, step):
            total = None
            for i in range(4):
                term = dot(left[i][:, d : d + step], b_ref[i * rows : (i + 1) * rows], TN)
                total = term if total is None else total + term
            out[d : d + step] = total.astype(BF)

    return call(
        "weight_grad",
        body,
        width // tile,
        [whole(p) for p in pieces] + [columns(b, tile)] + ([] if into is None else [None]),
        [new_columns(dim, width if into is None else into.shape[1], tile)],
        [*pieces, b] + ([] if into is None else [into]),
        8 * rows * dim * width,
        aliases=None if into is None else {5: 0},
    )[0]


def back(acts, weights, pieces, tile):
    rows = acts[0].shape[0] // 4
    dim = weights[0][0].shape[0]
    tile = min(tile, dim)
    na, np_ = len(acts), len(pieces)

    def body(*refs):
        ws = refs[na * np_ : na * np_ + na]
        outs = refs[na * np_ + na :]
        for p in range(np_):
            total = None
            for a in range(na):
                term = dot(refs[p * na + a][...], ws[a][...], NT)
                total = term if total is None else total + term
            outs[p][...] = total.astype(BF)

    return call(
        "back",
        body,
        dim // tile,
        [((rows, a.shape[1]), lambda j, p=p: (p, 0), "held") for p in pieces for a in acts]
        + [
            ((tile, a.shape[1]), lambda j, c=c: (j, c)) for a, (_, c) in zip(acts, weights)
        ],
        [new_columns(rows, dim, tile)] * np_,
        [a for _ in pieces for a in acts] + [w for w, _ in weights],
        2 * np_ * rows * dim * sum(a.shape[1] for a in acts),
    )


def shifted(ref, place, near, seg, back_way):
    cur = ref[place * seg : (place + 1) * seg]
    row = jnp.maximum(near, 0) * seg + (0 if back_way else seg - 8)
    edge = ref[pl.ds(pl.multiple_of(row, 8), 8)]
    edge = jnp.where(near >= 0, edge, 0.0)
    return jnp.concatenate([cur, edge] if back_way else [edge, cur])


def conv_of(ref, place, near, seg, taps):
    ext = shifted(ref, place, near, seg, False)
    terms = [ext[6 : 6 + seg], ext[7 : 7 + seg], ext[8 : 8 + seg]]
    return taps[0] * terms[0] + taps[1] * terms[1] + taps[2] * terms[2], terms


def conv_body(places, *refs):
    pieces, (w, taps_ref, bgate, cgate, xgate, ygate, mixed) = refs[:4], refs[4:]
    rows = pieces[0].shape[0]
    tile = bgate.shape[1]
    for i in range(4):
        at = pl.ds(i * rows, rows)
        b = dot(pieces[i][...], w[:, :tile], NN)
        x = dot(pieces[i][...], w[:, 2 * tile :], NN)
        c = dot(pieces[i][...], w[:, tile : 2 * tile], NN)
        mixed[at] = b * x
        bgate[at] = b.astype(BF)
        cgate[at] = c.astype(BF)
        xgate[at] = x.astype(BF)
    taps = [taps_ref[k : k + 1] for k in range(3)]
    segs = places.shape[1]
    seg = mixed.shape[0] // segs
    for s in range(segs):
        conv, _ = conv_of(mixed, s, places[0, s], seg, taps)
        at = pl.ds(s * seg, seg)
        ygate[at] = (cgate[at].astype(F32) * conv).astype(BF)


def conv_forward(pieces, weights, taps, places, tile):
    chans = taps.shape[1]
    dim = weights.shape[0]
    tokens = 4 * pieces[0].shape[0]
    return call(
        "conv_fwd",
        conv_body,
        chans // tile,
        [whole(p) for p in pieces]
        + [((dim, 3 * tile), lambda j: (0, j)), ((3, tile), lambda j: (0, j))],
        [new_columns(tokens, chans, tile)] * 4,
        [*pieces, weights, taps],
        6 * tokens * dim * chans,
        [pltpu.VMEM((tokens, tile), F32)],
        [places],
    )


def conv_back_body(places, *refs):
    pieces = refs[:4]
    w, taps_ref, bgate, cgate, xgate, ygate, dproj, tap_grad, out_grad, mixed, dconv = refs[4:]
    taps = [taps_ref[k : k + 1] for k in range(3)]
    segs = places.shape[1]
    tokens, tile = mixed.shape
    seg = tokens // segs
    mixed[...] = bgate[...].astype(F32) * xgate[...].astype(F32)
    rows = pieces[0].shape[0]
    sums = [jnp.zeros((1, tile), F32) for _ in range(3)]
    for i in range(4):
        dy = dot(pieces[i][...], w[...], NN)
        for s in range(i * segs // 4, (i + 1) * segs // 4):
            at = pl.ds(s * seg, seg)
            low = s * seg - i * rows
            dys = dy[low : low + seg]
            conv, terms = conv_of(mixed, s, places[0, s], seg, taps)
            dc = dys * cgate[at].astype(F32)
            dconv[at] = dc
            dproj[at, tile : 2 * tile] = (dys * conv).astype(BF)
            sums = [v + jnp.sum(dc * term, axis=0, keepdims=True) for v, term in zip(sums, terms)]
    for k in range(3):
        tap_grad[k : k + 1] = sums[k]
    for s in range(segs):
        at = pl.ds(s * seg, seg)
        ext = shifted(dconv, s, places[1, s], seg, True)
        dbx = taps[2] * ext[:seg] + taps[1] * ext[1 : 1 + seg] + taps[0] * ext[2 : 2 + seg]
        dproj[at, :tile] = (dbx * xgate[at].astype(F32)).astype(BF)
        dproj[at, 2 * tile :] = (dbx * bgate[at].astype(F32)).astype(BF)
    dim = pieces[0].shape[1]
    for d in range(0, dim, 512):
        total = None
        for i in range(4):
            term = dot(pieces[i][:, d : d + 512], ygate[i * rows : (i + 1) * rows], TN)
            total = term if total is None else total + term
        out_grad[d : d + 512] = total.astype(BF)


def conv_backward(pieces, weights, taps, saved, places, tile):
    chans = taps.shape[1]
    dim = weights.shape[0]
    tokens = 4 * pieces[0].shape[0]
    return call(
        "conv_bwd",
        conv_back_body,
        chans // tile,
        [whole(p) for p in pieces]
        + [columns(weights, tile, 3 * chans // tile), ((3, tile), lambda j: (0, j))]
        + [columns(a, tile) for a in saved],
        [
            ((tokens, 3 * tile), lambda j: (0, j), (tokens, 3 * chans), BF),
            ((3, tile), lambda j: (0, j), (3, chans), F32),
            ((dim, tile), lambda j: (0, 3 * chans // tile + j), (dim, 4 * chans), BF),
        ],
        [*pieces, weights, taps, *saved],
        4 * tokens * dim * chans,
        [pltpu.VMEM((tokens, tile), F32)] * 2,
        [places],
    )


def local(
    sizes,
    tokens,
    in_weight,
    conv_taps,
    out_weight,
    gate_weight,
    up_weight,
    down_weight,
    norm_gain1,
    norm_gain2,
    out_grad,
):
    ndp, nt = sizes
    square = Square(nt)
    chans, dim = out_weight.shape[0], tokens.shape[2]
    offset = square.t * chans
    tile = min(256, chans)
    places = square.places()
    taps = lax.dynamic_slice_in_dim(conv_taps, offset, chans, 1)
    dp_gather = lambda v: lax.all_gather(v, "dp", axis=0, tiled=True)
    dp_scatter = lambda v: lax.psum_scatter(v, "dp", scatter_dimension=0, tiled=True)

    conv_shard = jnp.concatenate(
        [in_weight[k, :, c : c + tile] for c in range(0, chans, tile) for k in range(3)]
        + [out_weight.T],
        axis=1,
    )
    conv_w = dp_gather(conv_shard)
    down_shard = down_weight.T

    hidden = tokens[0].astype(F32)
    scale1 = rms_scale(hidden)
    n1, _ = square.gather((hidden * scale1 * norm_gain1).astype(BF))
    cot = out_grad[0]
    gate_w = dp_gather(after(gate_weight, conv_w, n1[1], n1[3]))
    g_gather = square.gather_steps(after(cot, n1[1], n1[3]))
    g_first = next(g_gather)
    saved = conv_forward(n1, conv_w, taps, places, tile)
    ygate = saved[3]
    far = back([after(ygate, *g_first)], [(conv_w, 3)], (1, 3), 1024)
    near = back([after(ygate, far[0])], [(conv_w, 3)], (0, 2), 1024)
    branch, mid = square.finish(near, square.begin(far))
    up_w = dp_gather(after(up_weight, gate_w, *mid))
    second = hidden + branch
    scale2 = rms_scale(second)
    n2, n2_first = square.gather((second * scale2 * norm_gain2).astype(BF))
    down_w = dp_gather(after(down_shard, up_w, n2[1], n2[3]))
    g = g_gather.send((n2[1], n2[3]))

    act, silu, slope = ffn_gate(n2, gate_w, up_w)
    down_part = weight_grad(first_after(g, act), act)
    down_owned = dp_scatter(down_part)
    dgate, dup = ffn_slope(first_after(g, down_part), down_w, silu, slope)
    pair = [(gate_w, 0), (up_w, 0)]
    gate_part = weight_grad(first_after(n2, dgate), dgate)
    far = back([after(dgate, gate_part), dup], pair, (1, 3), 512)
    near = back([after(dgate, far[0]), dup], pair, (0, 2), 512)
    ffn = back([after(act, near[0])], [(down_w, 0)], (1, 3, 0, 2), 512)
    dnormed2, mid = square.finish(near, square.begin(far), ffn[0])
    gate_owned = dp_scatter(after(gate_part, down_owned, *mid))
    up_part = weight_grad(first_after(n2, *mid), dup)
    dsecond_norm, gain2_part = norm_back(second, scale2, norm_gain2, dnormed2)
    dsecond = cot.astype(F32) + dsecond_norm
    dbr, dbr_first = square.gather(dsecond.astype(BF))
    up_owned = dp_scatter(after(up_part, gate_owned, dbr[1], dbr[3]))

    dproj, tap_part, conv_part = conv_backward(dbr, conv_w, taps, saved, places, tile)
    far = back([dproj], [(conv_w, 0)], (1, 3), 512)
    near = back([after(dproj, far[0])], [(conv_w, 0)], (0, 2), 512)
    conv_part = weight_grad(first_after(n1, near[0]), dproj, conv_part)
    dnormed, mid = square.finish(near, square.begin(far))
    ffn, _ = square.finish(ffn[2:], square.begin([after(v, *mid) for v in ffn[:2]]))
    conv_owned = dp_scatter(after(conv_part, up_owned, *mid))
    block_out = (second + ffn).astype(BF)
    dhidden_norm, gain1_part = norm_back(hidden, scale1, norm_gain1, dnormed)
    tokens_grad = dsecond + dhidden_norm

    wide = lax.dynamic_update_slice_in_dim(
        jnp.zeros((3, conv_taps.shape[1]), F32), tap_part, offset, 1
    )
    small = jnp.concatenate(
        [gain1_part[None], gain2_part[None], wide, jnp.zeros_like(wide)]
    )
    small = total_of(small, (("tensor", nt), ("dp", ndp)))
    in_owned = conv_owned[:, : 3 * chans].reshape(-1, chans // tile, 3, tile)
    in_owned = in_owned.transpose(2, 0, 1, 3)
    return (
        block_out[None],
        tokens_grad[None],
        in_owned.reshape(3, -1, chans).astype(F32),
        small[2:5],
        conv_owned[:, 3 * chans :].T.astype(F32),
        gate_owned.astype(F32),
        up_owned.astype(F32),
        down_owned.T.astype(F32),
        small[0],
        small[1],
    )


def solution(mesh):
    in_specs = (
        P("dp", "tensor", None),
        P(None, "dp", "tensor"),
        P(),
        P("tensor", "dp"),
        P("dp", "tensor"),
        P("dp", "tensor"),
        P("tensor", "dp"),
        P(),
        P(),
        P("dp", "tensor", None),
    )
    out_specs = (
        P("dp", "tensor", None),
        P("dp", "tensor", None),
        P(None, "dp", "tensor"),
        P(),
        P("tensor", "dp"),
        P("dp", "tensor"),
        P("dp", "tensor"),
        P("tensor", "dp"),
        P(),
        P(),
    )
    sizes = (mesh.shape["dp"], mesh.shape["tensor"])
    return jax.shard_map(
        functools.partial(local, sizes),
        mesh=mesh,
        in_specs=in_specs,
        out_specs=out_specs,
        check_vma=False,
    )
```

time: 1750 us -> 853 us (0.49)
  waiting for transfers between devices: 1290 us -> 363 us
  matrix products: 322 us -> 0 us
  Pallas kernels: 0 us -> 309 us
  starting transfers between devices: 1.19 us -> 43.8 us
  blocking collectives: 40.3 us -> 0 us
  local copies, waits for them, and re-layouts: 10.3 us -> 44.5 us
    reduce_scatter x9 -> x4, waiting for transfers between devices: 744 us -> 0.01 us  [local(): lax.psum_scatter(v, 'dp', scatter_dimension=0, tiled=True)]
    all_gather x9 -> x4, waiting for transfers between devices: 542 us -> 12 us  [local(): dp_gather = lambda v: lax.all_gather(v, 'dp', axis=0, tiled=True)]
    ppermute x0 -> x37, waiting for transfers between devices: none -> 351 us  [the longest x32 308 us: flip(): return lax.ppermute(value, 'tensor', [(t, t ^ bit) for t in range(self.nt)])]
    dot_general x15 -> x0, matrix products: 322 us -> none  [the longest x1 36.6 us: local(): jnp.einsum('bqw,rw->bqr', gradient_total, down_weight_backward, preferred...]
    pallas_call x0 -> x15, Pallas kernels: none -> 309 us  [call(): pl.pallas_call(body, grid_spec=pltpu.PrefetchScalarGridSpec(num_scalar_pr...]
    ppermute x0 -> x37, starting transfers between devices: none -> 42.7 us  [the longest x32 35.5 us: flip(): return lax.ppermute(value, 'tensor', [(t, t ^ bit) for t in range(self.nt)])]
    psum x1 -> x0, blocking collectives: 40.3 us -> none  [local(): lax.psum((tap_wide, gain1_part, gain2_part), ('dp', 'tensor'))]
    add x0 -> x19, other arithmetic: none -> 30.3 us  [the longest x14 29.4 us: finish(): total = [k.astype(F32) + r.astype(F32) for k, r in zip(near, came)]]
  transfers between devices with their start and end apart: 18 -> 45, of which waited for: 18 -> 21; matrix products, arithmetic and copies ran while one was open for 16% -> 10% of each run, Pallas kernels for 0% -> 36%
where the time goes in v1:
time: 853 us; the launch traced here: 850 us
  waiting for transfers between devices  363 us (43%)
  Pallas kernels  309 us (36%)
  other arithmetic  70.6 us (8%)
  local copies, waits for them, and re-layouts  44.5 us (5%)
  starting transfers between devices  43.8 us (5%)
  between operations  17.9 us (2%)
    pallas_call x15, Pallas kernels, call(): pl.pallas_call(body, grid_spec=pltpu.PrefetchScalarGridSpec(num_scalar_pr...  309 us
    ppermute x32, waiting for transfers between devices, flip(): return lax.ppermute(value, 'tensor', [(t, t ^ bit) for t in range(self.nt)])  308 us
    ppermute x5, waiting for transfers between devices, total_of(): lax.ppermute(value, axis, [(i, i ^ bit) for i in range(size)])  43.4 us
    ppermute x32, starting transfers between devices, flip(): return lax.ppermute(value, 'tensor', [(t, t ^ bit) for t in range(self.nt)])  35.5 us
    add x14, other arithmetic, finish(): total = [k.astype(F32) + r.astype(F32) for k, r in zip(near, came)]  29.4 us
    unnamed x121, local copies, waits for them, and re-layouts  28.3 us
  transfers between devices with their start and end apart: 45, of which 21 were waited for; matrix products, arithmetic and copies ran while one was open for 10% of the time, Pallas kernels for 36%

profile of v1, /device:TPU:0, one launch (start us, length us, event | category | flops | bytes accessed | tf_op | source)
XLA Modules:
  0.0 849.7 jit_solution(17846244970519636325)
XLA Ops:
  21.4 21.7 %collective-permute-done.2 = bf16[256,2048]{1,0:T(8,128)(2,1)S(1)} collective-permute-done((bf16[256,2048]{1,0:T(8,128)(2,1)S(1)}, bf16[256,2048]{1,0:T(8,128)(2,1)S(1)}, u32[]{:S(2)}, u32[]{:S(2)}) %collective-permute-start.2) | collective-permute-done | bytes 1048608 | tf_op jit(solution)/shard_map/ppermute | solution.py:59
  48.2 43.4 %collective-permute-done.3.refs_3_ = bf16[512,2048]{1,0:T(8,128)(2,1)S(1)} collective-permute-done((bf16[512,2048]{1,0:T(8,128)(2,1)S(1)}, bf16[512,2048]{1,0:T(8,128)(2,1)S(1)}, u32[]{:S(2)}, u32[]{:S(2)}) %collective-permute-start.3) | collective-permute-done | bytes 2097184 | tf_op jit(solution)/shard_map/ppermute | solution.py:59
  93.1 6.8 all-gather.5.cloned.1.call-done.refs_4_.refs_2_
  110.5 21.0 %conv_fwd.1 = (bf16[2048,512]{1,0:T(8,128)(2,1)}, bf16[2048,512]{1,0:T(8,128)(2,1)}, bf16[2048,512]{1,0:T(8,128)(2,1)}, bf16[2048,512]{1,0:T(8,128)(2,1)}) custom-call(s32[2,8]{1,0:T(2,128)} %pad_add_fusion.places, bf16[512,2048]{1,0:T(8,128)(2,1)} %copy-done.21, bf16[512,2048]{1,0:T(8,128)(2,1)} %collective-permute-done.1.refs_1_, ...), custom_call_target="tpu_custom_call" | custom-call | flops 2576980480 | bytes 5034393 | tf_op jit(solution)/shard_map/conv_fwd/pallas_call | solution.py:138
  131.5 5.2 back.7
  138.3 5.2 back.8
  143.4 40.8 %collective-permute-done.6 = bf16[512,2048]{1,0:T(8,128)(2,1)} collective-permute-done((bf16[512,2048]{1,0:T(8,128)(2,1)}, bf16[512,2048]{1,0:T(8,128)(2,1)}, u32[]{:S(2)}, u32[]{:S(2)}) %collective-permute-start.6) | collective-permute-done | bytes 2097184 | tf_op jit(solution)/shard_map/ppermute | solution.py:59
  195.0 22.4 %collective-permute-done.7 = bf16[256,2048]{1,0:T(8,128)(2,1)S(1)} collective-permute-done((bf16[256,2048]{1,0:T(8,128)(2,1)}, bf16[256,2048]{1,0:T(8,128)(2,1)S(1)}, u32[]{:S(2)}, u32[]{:S(2)}) %collective-permute-start.7) | collective-permute-done | bytes 1048608 | tf_op jit(solution)/shard_map/ppermute | solution.py:59
  223.6 21.1 %collective-permute-done.12 = bf16[256,2048]{1,0:T(8,128)(2,1)S(1)} collective-permute-done((bf16[256,2048]{1,0:T(8,128)(2,1)S(1)}, bf16[256,2048]{1,0:T(8,128)(2,1)S(1)}, u32[]{:S(2)}, u32[]{:S(2)}) %collective-permute-start.12) | collective-permute-done | bytes 1048608 | tf_op jit(solution)/shard_map/ppermute | solution.py:59
  252.2 39.1 %collective-permute-done.13.refs_3_ = bf16[512,2048]{1,0:T(8,128)(2,1)} collective-permute-done((bf16[512,2048]{1,0:T(8,128)(2,1)}, bf16[512,2048]{1,0:T(8,128)(2,1)}, u32[]{:S(2)}, u32[]{:S(2)}) %collective-permute-start.13) | collective-permute-done | bytes 2097184 | tf_op jit(solution)/shard_map/ppermute | solution.py:59
  301.1 44.1 %ffn_gate.1 = (bf16[2048,2048]{1,0:T(8,128)(2,1)}, bf16[2048,2048]{1,0:T(8,128)(2,1)}, bf16[2048,2048]{1,0:T(8,128)(2,1)}) custom-call(bf16[512,2048]{1,0:T(8,128)(2,1)} %pad_maximum_fusion.4.refs_0_, bf16[512,2048]{1,0:T(8,128)(2,1)} %collective-permute-done.11.refs_1_, bf16[512,2048]{1,0:T(8,128)(2,1)} %pad_maximum_fusion.5.refs_2_, ...), custom_call_target="tpu_custom_call" | custom-call | flops 6871947776 | bytes 10066329 | tf_op jit(solution)/shard_map/ffn_gate/pallas_call | solution.py:138
  345.2 23.9 %weight_grad.4 = bf16[2048,2048]{1,0:T(8,128)(2,1)} custom-call(bf16[512,2048]{1,0:T(8,128)(2,1)} %pad_maximum_fusion.6.refs_0_, bf16[512,2048]{1,0:T(8,128)(2,1)} %collective-permute-done.14.refs_1_, bf16[512,2048]{1,0:T(8,128)(2,1)} %copy-done.13, bf16[512,2048]{1,0:T(8,128)(2,1)} %collective-permute-done.15.refs_3_, ...), custom_call_target="tpu_custom_call" | custom-call | flops 3435973888 | bytes 5033164 | tf_op jit(solution)/shard_map/weight_grad/pallas_call | solution.py:138
  369.6 5.2 all-gather.11.cloned.1.call-done.refs_4_
  374.7 27.1 %ffn_slope.1 = (bf16[2048,2048]{1,0:T(8,128)(2,1)}, bf16[2048,2048]{1,0:T(8,128)(2,1)}) custom-call(bf16[512,2048]{1,0:T(8,128)(2,1)} %pad_maximum_fusion.6.refs_0_, bf16[512,2048]{1,0:T(8,128)(2,1)} %collective-permute-done.14.refs_1_, bf16[512,2048]{1,0:T(8,128)(2,1)} %copy-done.13, bf16[512,2048]{1,0:T(8,128)(2,1)} %collective-permute-done.15.refs_3_, ...), custom_call_target="tpu_custom_call" | custom-call | flops 3435973888 | bytes 10066329 | tf_op jit(solution)/shard_map/ffn_slope/pallas_call | solution.py:138
  401.8 23.8 %weight_grad.5 = bf16[2048,2048]{1,0:T(8,128)(2,1)} custom-call(bf16[512,2048]{1,0:T(8,128)(2,1)} %pad_maximum_fusion.4.refs_0_, bf16[512,2048]{1,0:T(8,128)(2,1)} %collective-permute-done.11.refs_1_, bf16[512,2048]{1,0:T(8,128)(2,1)} %pad_maximum_fusion.5.refs_2_, bf16[512,2048]{1,0:T(8,128)(2,1)} %collective-permute-done.13.refs_3_, ...), custom_call_target="tpu_custom_call" | custom-call | flops 3435973888 | bytes 5033164 | tf_op jit(solution)/shard_map/weight_grad/pallas_call | solution.py:138
  425.6 23.8 %back.9 = (bf16[512,2048]{1,0:T(8,128)(2,1)}, bf16[512,2048]{1,0:T(8,128)(2,1)}) custom-call(bf16[2048,2048]{1,0:T(8,128)(2,1)} %get-tuple-element.85.refs_4_.refs_0_.refs_2_, bf16[2048,2048]{1,0:T(8,128)(2,1)} %get-tuple-element.83.refs_1_.refs_3_.refs_4_, bf16[2048,2048]{1,0:T(8,128)(2,1)} %get-tuple-element.85.refs_4_.refs_0_.refs_2_, ...), custom_call_target="tpu_custom_call" | custom-call | flops 3435973888 | bytes 10905190 | tf_op jit(solution)/shard_map/back/pallas_call | solution.py:138
  452.3 23.9 %back.10 = (bf16[512,2048]{1,0:T(8,128)(2,1)}, bf16[512,2048]{1,0:T(8,128)(2,1)}) custom-call(bf16[2048,2048]{1,0:T(8,128)(2,1)} %get-tuple-element.85.refs_4_.refs_0_.refs_2_, bf16[2048,2048]{1,0:T(8,128)(2,1)} %get-tuple-element.83.refs_1_.refs_3_.refs_4_, bf16[2048,2048]{1,0:T(8,128)(2,1)} %get-tuple-element.85.refs_4_.refs_0_.refs_2_, ...), custom_call_target="tpu_custom_call" | custom-call | flops 3435973888 | bytes 10905190 | tf_op jit(solution)/shard_map/back/pallas_call | solution.py:138
  476.3 23.2 %back.11 = (bf16[512,2048]{1,0:T(8,128)(2,1)}, bf16[512,2048]{1,0:T(8,128)(2,1)}, bf16[512,2048]{1,0:T(8,128)(2,1)}, bf16[512,2048]{1,0:T(8,128)(2,1)}) custom-call(bf16[2048,2048]{1,0:T(8,128)(2,1)} %get-tuple-element.87.refs_4_.refs_0_.refs_1_.refs_2_.refs_3_, bf16[2048,2048]{1,0:T(8,128)(2,1)} %get-tuple-element.87.refs_4_.refs_0_.refs_1_.refs_2_.refs_3_, ...), custom_call_target="tpu_custom_call" | custom-call | flops 3435973888 | bytes 10066329 | tf_op jit(solution)/shard_map/back/pallas_call | solution.py:138
  509.0 23.8 %collective-permute-done.17 = bf16[256,2048]{1,0:T(8,128)(2,1)S(1)} collective-permute-done((bf16[256,2048]{1,0:T(8,128)(2,1)S(1)}, bf16[256,2048]{1,0:T(8,128)(2,1)S(1)}, u32[]{:S(2)}, u32[]{:S(2)}) %collective-permute-start.17) | collective-permute-done | bytes 1048608 | tf_op jit(solution)/shard_map/ppermute | solution.py:59
  544.7 23.0 %collective-permute-done.22 = bf16[256,2048]{1,0:T(8,128)(2,1)S(1)} collective-permute-done((bf16[256,2048]{1,0:T(8,128)(2,1)S(1)}, bf16[256,2048]{1,0:T(8,128)(2,1)S(1)}, u32[]{:S(2)}, u32[]{:S(2)}) %collective-permute-start.22) | collective-permute-done | bytes 1048608 | tf_op jit(solution)/shard_map/ppermute | solution.py:59
  571.9 23.8 %weight_grad.7 = bf16[2048,2048]{1,0:T(8,128)(2,1)} custom-call(bf16[512,2048]{1,0:T(8,128)(2,1)} %pad_maximum_fusion.4.refs_0_, bf16[512,2048]{1,0:T(8,128)(2,1)} %collective-permute-done.11.refs_1_, bf16[512,2048]{1,0:T(8,128)(2,1)} %pad_maximum_fusion.5.refs_2_, bf16[512,2048]{1,0:T(8,128)(2,1)} %collective-permute-done.13.refs_3_, ...), custom_call_target="tpu_custom_call" | custom-call | flops 3435973888 | bytes 5033164 | tf_op jit(solution)/shard_map/weight_grad/pallas_call | solution.py:138
  595.7 19.5 %collective-permute-done.23.refs_3_ = bf16[512,2048]{1,0:T(8,128)(2,1)} collective-permute-done((bf16[512,2048]{1,0:T(8,128)(2,1)}, bf16[512,2048]{1,0:T(8,128)(2,1)}, u32[]{:S(2)}, u32[]{:S(2)}) %collective-permute-start.23) | collective-permute-done | bytes 2097184 | tf_op jit(solution)/shard_map/ppermute | solution.py:59
  617.4 24.0 %conv_bwd.1 = (bf16[2048,1536]{1,0:T(8,128)(2,1)}, f32[3,512]{1,0:T(4,128)}, bf16[2048,2048]{1,0:T(8,128)(2,1)}) custom-call(s32[2,8]{1,0:T(2,128)} %pad_add_fusion.places, bf16[512,2048]{1,0:T(8,128)(2,1)} %pad_maximum_fusion.8.refs_0_, bf16[512,2048]{1,0:T(8,128)(2,1)} %collective-permute-done.21.refs_1_, bf16[512,2048]{1,0:T(8,128)(2,1)} %pad_maximum_fusion.9.refs_2_, ...), custom_call_target="tpu_custom_call" | custom-call | flops 1717986944 | bytes 7971635 | tf_op jit(solution)/shard_map/conv_bwd/pallas_call | solution.py:138
  641.4 10.6 %back.12 = (bf16[512,2048]{1,0:T(8,128)(2,1)}, bf16[512,2048]{1,0:T(8,128)(2,1)}) custom-call(bf16[2048,1536]{1,0:T(8,128)(2,1)} %get-tuple-element.99.refs_0_.refs_1_.refs_4_, bf16[2048,1536]{1,0:T(8,128)(2,1)} %get-tuple-element.99.refs_0_.refs_1_.refs_4_, bf16[2048,2048]{1,0:T(8,128)(2,1)} %all-gather.5.cloned.1.call-done.refs_4_.refs_2_), custom_call_target="tpu_custom_call" | custom-call | flops 1288490240 | bytes 5033164 | tf_op jit(solution)/shard_map/back/pallas_call | solution.py:138
  653.9 10.6 %back.13 = (bf16[512,2048]{1,0:T(8,128)(2,1)}, bf16[512,2048]{1,0:T(8,128)(2,1)}) custom-call(bf16[2048,1536]{1,0:T(8,128)(2,1)} %get-tuple-element.99.refs_0_.refs_1_.refs_4_, bf16[2048,1536]{1,0:T(8,128)(2,1)} %get-tuple-element.99.refs_0_.refs_1_.refs_4_, bf16[2048,2048]{1,0:T(8,128)(2,1)} %all-gather.5.cloned.1.call-done.refs_4_.refs_2_), custom_call_target="tpu_custom_call" | custom-call | flops 1288490240 | bytes 5033164 | tf_op jit(solution)/shard_map/back/pallas_call | solution.py:138
  664.5 19.4 %weight_grad.6 = bf16[2048,2048]{1,0:T(8,128)(2,1)} custom-call(bf16[512,2048]{1,0:T(8,128)(2,1)} %copy-done.21, bf16[512,2048]{1,0:T(8,128)(2,1)} %collective-permute-done.1.refs_1_, bf16[512,2048]{1,0:T(8,128)(2,1)} %copy-done.20, bf16[512,2048]{1,0:T(8,128)(2,1)} %copy-done.30, ...), custom_call_target="tpu_custom_call", output_to_operand_aliasing={{}: (5, {})} | custom-call | flops 2576980480 | bytes 6291456 | tf_op jit(solution)/shard_map/weight_grad/pallas_call | solution.py:138
  683.8 12.2 %collective-permute-done.24 = bf16[512,2048]{1,0:T(8,128)(2,1)} collective-permute-done((bf16[512,2048]{1,0:T(8,128)(2,1)}, bf16[512,2048]{1,0:T(8,128)(2,1)}, u32[]{:S(2)}, u32[]{:S(2)}) %collective-permute-start.24) | collective-permute-done | bytes 2097184 | tf_op jit(solution)/shard_map/ppermute | solution.py:59
  710.3 21.9 %collective-permute-done.30 = bf16[256,2048]{1,0:T(8,128)(2,1)S(1)} collective-permute-done((bf16[256,2048]{1,0:T(8,128)(2,1)S(1)}, bf16[256,2048]{1,0:T(8,128)(2,1)S(1)}, u32[]{:S(2)}, u32[]{:S(2)}) %collective-permute-start.30) | collective-permute-done | bytes 1048608 | tf_op jit(solution)/shard_map/ppermute | solution.py:59
  737.6 36.2 %collective-permute-done.32 = f32[8,2048]{1,0:T(8,128)S(1)} collective-permute-done((f32[8,2048]{1,0:T(8,128)S(1)}, f32[8,2048]{1,0:T(8,128)S(1)}, u32[]{:S(2)}, u32[]{:S(2)}) %collective-permute-start.32) | collective-permute-done | bytes 65568 | tf_op jit(solution)/shard_map/ppermute | solution.py:125
  803.2 6.1 fusion.13
  811.4 9.8 %collective-permute-done.27 = bf16[256,2048]{1,0:T(8,128)(2,1)S(1)} collective-permute-done((bf16[256,2048]{1,0:T(8,128)(2,1)}, bf16[256,2048]{1,0:T(8,128)(2,1)S(1)}, u32[]{:S(2)}, u32[]{:S(2)}) %collective-permute-start.27) | collective-permute-done | bytes 1048608 | tf_op jit(solution)/shard_map/ppermute | solution.py:59
  821.6 4.5 collective-permute-done.29
  (275 shorter events, 164.9 us)
Async XLA Ops:
  7.2 92.8 %all-gather.5.cloned.1.call-start = ((), (), s32[]{:S(2)}) async-start(), calls=%async_computation.4 | async-start | bytes 9437184 | tf_op jit(solution)/shard_map/all_gather | solution.py:415
  15.1 177.9 %all-gather.7.cloned.1.call-start = ((), (), s32[]{:S(2)}) async-start(), calls=%async_computation.5 | async-start | bytes 9437184 | tf_op jit(solution)/shard_map/all_gather | solution.py:415
  16.9 26.2 %collective-permute-start.2 = (bf16[256,2048]{1,0:T(8,128)(2,1)S(1)}, bf16[256,2048]{1,0:T(8,128)(2,1)S(1)}, u32[]{:S(2)}, u32[]{:S(2)}) collective-permute-start(bf16[256,2048]{1,0:T(8,128)(2,1)S(1)} %get-tuple-element.154), channel_id=1, source_target_pairs={{0,2},{1,3},{2,0},{3,1},{4,6},{5,7},{6,4},{7,5},{8,10},{9,11},{10,... | collective-permute-start | bytes 3145736 | tf_op jit(solution)/shard_map/ppermute | solution.py:59
  19.9 26.4 %collective-permute-start = (bf16[256,2048]{1,0:T(8,128)(2,1)S(1)}, bf16[256,2048]{1,0:T(8,128)(2,1)S(1)}, u32[]{:S(2)}, u32[]{:S(2)}) collective-permute-start(bf16[256,2048]{1,0:T(8,128)(2,1)S(1)} %get-tuple-element.155), channel_id=1, source_target_pairs={{0,1},{1,0},{2,3},{3,2},{4,5},{5,4},{6,7},{7,6},{8,9},{9,8},{10,11... | collective-permute-start | bytes 3145736 | tf_op jit(solution)/shard_map/ppermute | solution.py:59
  44.7 46.9 %collective-permute-start.3 = (bf16[512,2048]{1,0:T(8,128)(2,1)S(1)}, bf16[512,2048]{1,0:T(8,128)(2,1)S(1)}, u32[]{:S(2)}, u32[]{:S(2)}) collective-permute-start(bf16[512,2048]{1,0:T(8,128)(2,1)S(1)} %pad_maximum_fusion.3.refs_2_), channel_id=1, source_target_pairs={{0,1},{1,0},{2,3},{3,2},{4,5},{5,4},{6,7},{7,6},{8,9},{9,8},{10,11... | collective-permute-start | bytes 6291464 | tf_op jit(solution)/shard_map/ppermute | solution.py:59
  46.6 46.5 %collective-permute-start.1 = (bf16[512,2048]{1,0:T(8,128)(2,1)S(1)}, bf16[512,2048]{1,0:T(8,128)(2,1)}, u32[]{:S(2)}, u32[]{:S(2)}) collective-permute-start(bf16[512,2048]{1,0:T(8,128)(2,1)S(1)} %pad_maximum_fusion.2.refs_0_), channel_id=1, source_target_pairs={{0,2},{1,3},{2,0},{3,1},{4,6},{5,7},{6,4},{7,5},{8,10},{9,11},{10,... | collective-permute-start | bytes 6291464 | tf_op jit(solution)/shard_map/ppermute | solution.py:59
  100.0 193.7 %all-gather.9.cloned.1.call-start = ((), (), s32[]{:S(2)}) async-start(), calls=%async_computation.6 | async-start | bytes 9437184 | tf_op jit(solution)/shard_map/all_gather | solution.py:415
  102.9 28.6 %collective-permute-start.4 = (bf16[256,2048]{1,0:T(8,128)(2,1)S(1)}, bf16[256,2048]{1,0:T(8,128)(2,1)}, u32[]{:S(2)}, u32[]{:S(2)}) collective-permute-start(bf16[256,2048]{1,0:T(8,128)(2,1)S(1)} %get-tuple-element.153), channel_id=1, source_target_pairs={{0,1},{1,0},{2,3},{3,2},{4,5},{5,4},{6,7},{7,6},{8,9},{9,8},{10,11... | collective-permute-start | bytes 3145736 | tf_op jit(solution)/shard_map/ppermute | solution.py:59
  104.4 27.1 %collective-permute-start.5 = (bf16[256,2048]{1,0:T(8,128)(2,1)}, bf16[256,2048]{1,0:T(8,128)(2,1)}, u32[]{:S(2)}, u32[]{:S(2)}) collective-permute-start(bf16[256,2048]{1,0:T(8,128)(2,1)} %get-tuple-element.152), channel_id=1, source_target_pairs={{0,2},{1,3},{2,0},{3,1},{4,6},{5,7},{6,4},{7,5},{8,10},{9,11},{10,... | collective-permute-start | bytes 3145736 | tf_op jit(solution)/shard_map/ppermute | solution.py:59
  136.7 47.5 %collective-permute-start.6 = (bf16[512,2048]{1,0:T(8,128)(2,1)}, bf16[512,2048]{1,0:T(8,128)(2,1)}, u32[]{:S(2)}, u32[]{:S(2)}) collective-permute-start(bf16[512,2048]{1,0:T(8,128)(2,1)} %get-tuple-element.65), channel_id=1, source_target_pairs={{0,2},{1,3},{2,0},{3,1},{4,6},{5,7},{6,4},{7,5},{8,10},{9,11},{10,... | collective-permute-start | bytes 6291464 | tf_op jit(solution)/shard_map/ppermute | solution.py:59
  137.3 51.5 %collective-permute-start.8 = (bf16[512,2048]{1,0:T(8,128)(2,1)}, bf16[512,2048]{1,0:T(8,128)(2,1)S(1)}, u32[]{:S(2)}, u32[]{:S(2)}) collective-permute-start(bf16[512,2048]{1,0:T(8,128)(2,1)} %get-tuple-element.69), channel_id=1, source_target_pairs={{0,1},{1,0},{2,3},{3,2},{4,5},{5,4},{6,7},{7,6},{8,9},{9,8},{10,11... | collective-permute-start | bytes 6291464 | tf_op jit(solution)/shard_map/ppermute | solution.py:59
  193.0 181.8 %all-gather.11.cloned.1.call-start = ((), (), s32[]{:S(2)}) async-start(), calls=%async_computation.7 | async-start | bytes 9437184 | tf_op jit(solution)/shard_map/all_gather | solution.py:415
  246.3 45.0 %collective-permute-start.13 = (bf16[512,2048]{1,0:T(8,128)(2,1)}, bf16[512,2048]{1,0:T(8,128)(2,1)}, u32[]{:S(2)}, u32[]{:S(2)}) collective-permute-start(bf16[512,2048]{1,0:T(8,128)(2,1)} %pad_maximum_fusion.5.refs_2_), channel_id=1, source_target_pairs={{0,1},{1,0},{2,3},{3,2},{4,5},{5,4},{6,7},{7,6},{8,9},{9,8},{10,11... | collective-permute-start | bytes 6291464 | tf_op jit(solution)/shard_map/ppermute | solution.py:59
  248.8 44.9 %collective-permute-start.11 = (bf16[512,2048]{1,0:T(8,128)(2,1)}, bf16[512,2048]{1,0:T(8,128)(2,1)}, u32[]{:S(2)}, u32[]{:S(2)}) collective-permute-start(bf16[512,2048]{1,0:T(8,128)(2,1)} %pad_maximum_fusion.4.refs_0_), channel_id=1, source_target_pairs={{0,2},{1,3},{2,0},{3,1},{4,6},{5,7},{6,4},{7,5},{8,10},{9,11},{10,... | collective-permute-start | bytes 6291464 | tf_op jit(solution)/shard_map/ppermute | solution.py:59
  293.7 214.1 %reduce-scatter.5.cloned.1.call-start = ((), (), s32[]{:S(2)}) async-start(), calls=%async_computation.8 | async-start | bytes 9437184 | tf_op jit(solution)/shard_map/reduce_scatter | solution.py:416
  299.1 46.1 %collective-permute-start.15 = (bf16[512,2048]{1,0:T(8,128)(2,1)S(1)}, bf16[512,2048]{1,0:T(8,128)(2,1)}, u32[]{:S(2)}, u32[]{:S(2)}) collective-permute-start(bf16[512,2048]{1,0:T(8,128)(2,1)S(1)} %pad_maximum_fusion.7.refs_2_), channel_id=1, source_target_pairs={{0,1},{1,0},{2,3},{3,2},{4,5},{5,4},{6,7},{7,6},{8,9},{9,8},{10,11... | collective-permute-start | bytes 6291464 | tf_op jit(solution)/shard_map/ppermute | solution.py:59
  300.0 45.2 %collective-permute-start.14 = (bf16[512,2048]{1,0:T(8,128)(2,1)}, bf16[512,2048]{1,0:T(8,128)(2,1)}, u32[]{:S(2)}, u32[]{:S(2)}) collective-permute-start(bf16[512,2048]{1,0:T(8,128)(2,1)} %pad_maximum_fusion.6.refs_0_), channel_id=1, source_target_pairs={{0,2},{1,3},{2,0},{3,1},{4,6},{5,7},{6,4},{7,5},{8,10},{9,11},{10,... | collective-permute-start | bytes 6291464 | tf_op jit(solution)/shard_map/ppermute | solution.py:59
  369.1 248.1 %reduce-scatter.7.cloned.1.call-start = ((), (), s32[]{:S(2)}) async-start(), calls=%async_computation.9 | async-start | bytes 9437184 | tf_op jit(solution)/shard_map/reduce_scatter | solution.py:416
  449.4 50.1 %collective-permute-start.16 = (bf16[512,2048]{1,0:T(8,128)(2,1)}, bf16[512,2048]{1,0:T(8,128)(2,1)}, u32[]{:S(2)}, u32[]{:S(2)}) collective-permute-start(bf16[512,2048]{1,0:T(8,128)(2,1)} %get-tuple-element.84), channel_id=1, source_target_pairs={{0,2},{1,3},{2,0},{3,1},{4,6},{5,7},{6,4},{7,5},{8,10},{9,11},{10,... | collective-permute-start | bytes 6291464 | tf_op jit(solution)/shard_map/ppermute | solution.py:59
  450.9 51.9 %collective-permute-start.18 = (bf16[512,2048]{1,0:T(8,128)(2,1)}, bf16[512,2048]{1,0:T(8,128)(2,1)S(1)}, u32[]{:S(2)}, u32[]{:S(2)}) collective-permute-start(bf16[512,2048]{1,0:T(8,128)(2,1)} %get-tuple-element.92), channel_id=1, source_target_pairs={{0,1},{1,0},{2,3},{3,2},{4,5},{5,4},{6,7},{7,6},{8,9},{9,8},{10,11... | collective-permute-start | bytes 6291464 | tf_op jit(solution)/shard_map/ppermute | solution.py:59
  507.8 198.3 %reduce-scatter.9.cloned.1.call-start = ((), (), s32[]{:S(2)}) async-start(), calls=%async_computation.10 | async-start | bytes 9437184 | tf_op jit(solution)/shard_map/reduce_scatter | solution.py:416
  508.5 26.2 %collective-permute-start.19 = (bf16[256,2048]{1,0:T(8,128)(2,1)}, bf16[256,2048]{1,0:T(8,128)(2,1)S(1)}, u32[]{:S(2)}, u32[]{:S(2)}) collective-permute-start(bf16[256,2048]{1,0:T(8,128)(2,1)} %slice.207), channel_id=1, source_target_pairs={{0,2},{1,3},{2,0},{3,1},{4,6},{5,7},{6,4},{7,5},{8,10},{9,11},{10,... | collective-permute-start | bytes 3145736 | tf_op jit(solution)/shard_map/ppermute | solution.py:59
  569.2 46.0 %collective-permute-start.23 = (bf16[512,2048]{1,0:T(8,128)(2,1)}, bf16[512,2048]{1,0:T(8,128)(2,1)}, u32[]{:S(2)}, u32[]{:S(2)}) collective-permute-start(bf16[512,2048]{1,0:T(8,128)(2,1)} %pad_maximum_fusion.9.refs_2_), channel_id=1, source_target_pairs={{0,1},{1,0},{2,3},{3,2},{4,5},{5,4},{6,7},{7,6},{8,9},{9,8},{10,11... | collective-permute-start | bytes 6291464 | tf_op jit(solution)/shard_map/ppermute | solution.py:59
  571.5 45.7 %collective-permute-start.21 = (bf16[512,2048]{1,0:T(8,128)(2,1)}, bf16[512,2048]{1,0:T(8,128)(2,1)}, u32[]{:S(2)}, u32[]{:S(2)}) collective-permute-start(bf16[512,2048]{1,0:T(8,128)(2,1)} %pad_maximum_fusion.8.refs_0_), channel_id=1, source_target_pairs={{0,2},{1,3},{2,0},{3,1},{4,6},{5,7},{6,4},{7,5},{8,10},{9,11},{10,... | collective-permute-start | bytes 6291464 | tf_op jit(solution)/shard_map/ppermute | solution.py:59
  617.3 214.6 %reduce-scatter.11.cloned.1.call-start = ((), (), s32[]{:S(2)}) async-start(), calls=%async_computation.11 | async-start | bytes 9437184 | tf_op jit(solution)/shard_map/reduce_scatter | solution.py:416
  652.0 44.0 %collective-permute-start.24 = (bf16[512,2048]{1,0:T(8,128)(2,1)}, bf16[512,2048]{1,0:T(8,128)(2,1)}, u32[]{:S(2)}, u32[]{:S(2)}) collective-permute-start(bf16[512,2048]{1,0:T(8,128)(2,1)} %get-tuple-element.98), channel_id=1, source_target_pairs={{0,2},{1,3},{2,0},{3,1},{4,6},{5,7},{6,4},{7,5},{8,10},{9,11},{10,... | collective-permute-start | bytes 6291464 | tf_op jit(solution)/shard_map/ppermute | solution.py:59
  652.3 46.9 %collective-permute-start.25 = (bf16[512,2048]{1,0:T(8,128)(2,1)}, bf16[512,2048]{1,0:T(8,128)(2,1)}, u32[]{:S(2)}, u32[]{:S(2)}) collective-permute-start(bf16[512,2048]{1,0:T(8,128)(2,1)} %get-tuple-element.102), channel_id=1, source_target_pairs={{0,1},{1,0},{2,3},{3,2},{4,5},{5,4},{6,7},{7,6},{8,9},{9,8},{10,11... | collective-permute-start | bytes 6291464 | tf_op jit(solution)/shard_map/ppermute | solution.py:59
  706.1 26.2 %collective-permute-start.30 = (bf16[256,2048]{1,0:T(8,128)(2,1)S(1)}, bf16[256,2048]{1,0:T(8,128)(2,1)S(1)}, u32[]{:S(2)}, u32[]{:S(2)}) collective-permute-start(bf16[256,2048]{1,0:T(8,128)(2,1)S(1)} %slice.206), channel_id=1, source_target_pairs={{0,1},{1,0},{2,3},{3,2},{4,5},{5,4},{6,7},{7,6},{8,9},{9,8},{10,11... | collective-permute-start | bytes 3145736 | tf_op jit(solution)/shard_map/ppermute | solution.py:59
  707.4 26.9 %collective-permute-start.31 = (bf16[256,2048]{1,0:T(8,128)(2,1)}, bf16[256,2048]{1,0:T(8,128)(2,1)S(1)}, u32[]{:S(2)}, u32[]{:S(2)}) collective-permute-start(bf16[256,2048]{1,0:T(8,128)(2,1)} %slice.205), channel_id=1, source_target_pairs={{0,2},{1,3},{2,0},{3,1},{4,6},{5,7},{6,4},{7,5},{8,10},{9,11},{10,... | collective-permute-start | bytes 3145736 | tf_op jit(solution)/shard_map/ppermute | solution.py:59
  708.3 83.7 %collective-permute-start.26 = (bf16[512,2048]{1,0:T(8,128)(2,1)}, bf16[512,2048]{1,0:T(8,128)(2,1)}, u32[]{:S(2)}, u32[]{:S(2)}) collective-permute-start(bf16[512,2048]{1,0:T(8,128)(2,1)} %get-tuple-element.103), channel_id=1, source_target_pairs={{0,2},{1,3},{2,0},{3,1},{4,6},{5,7},{6,4},{7,5},{8,10},{9,11},{10,... | collective-permute-start | bytes 6291464 | tf_op jit(solution)/shard_map/ppermute | solution.py:59
  709.5 88.4 %collective-permute-start.28 = (bf16[512,2048]{1,0:T(8,128)(2,1)}, bf16[512,2048]{1,0:T(8,128)(2,1)}, u32[]{:S(2)}, u32[]{:S(2)}) collective-permute-start(bf16[512,2048]{1,0:T(8,128)(2,1)} %get-tuple-element.106), channel_id=1, source_target_pairs={{0,1},{1,0},{2,3},{3,2},{4,5},{5,4},{6,7},{7,6},{8,9},{9,8},{10,11... | collective-permute-start | bytes 6291464 | tf_op jit(solution)/shard_map/ppermute | solution.py:59
  736.3 37.4 %collective-permute-start.32 = (f32[8,2048]{1,0:T(8,128)S(1)}, f32[8,2048]{1,0:T(8,128)S(1)}, u32[]{:S(2)}, u32[]{:S(2)}) collective-permute-start(f32[8,2048]{1,0:T(8,128)S(1)} %pad_maximum_fusion.10), channel_id=1, source_target_pairs={{0,1},{1,0},{2,3},{3,2},{4,5},{5,4},{6,7},{7,6},{8,9},{9,8},{10,11... | collective-permute-start | bytes 196616 | tf_op jit(solution)/shard_map/ppermute | solution.py:125
  (68 other events, 1555.8 us)
Sparse Core Ops, SparseCore 0:
  15.2 84.7 all-gather.4
  101.6 80.5 all-gather.6
  193.1 79.6 all-gather.8
  293.8 80.8 all-gather.10
  376.9 88.1 reduce-scatter.4
  508.0 86.3 reduce-scatter.6
  617.4 87.0 reduce-scatter.8
  706.8 89.7 reduce-scatter.10

commit v2 on v1

--- a/solution.py
+++ b/solution.py
@@ -3,6 +3,7 @@
 
 import jax
 import jax.numpy as jnp
+import numpy as np
 from jax import lax
 from jax.experimental import pallas as pl
 from jax.experimental.pallas import tpu as pltpu
@@ -74,56 +75,53 @@
         half = rows.shape[0] // 2
         curs = [rows[:half], rows[half:]]
         depth = len(self.orders[0])
-        gates = None
+        came = None
         for level in range(depth):
+            gates = yield curs, came
+            curs = [after(c, *gates) for c in curs]
             came = [self.flip(c, o[level]) for c, o in zip(curs, self.orders)]
-            gates = gates or (yield came)
             if level < depth - 1:
-                curs = [after(jnp.concatenate([c, r]), *gates) for c, r in zip(curs, came)]
-        yield [curs[0], came[0], curs[1], came[1]]
+                curs = [jnp.concatenate([c, r]) for c, r in zip(curs, came)]
+        yield [curs[0], came[0], curs[1], came[1]], None
 
     def begin(self, far):
         return [self.flip(s, o[-1]) for s, o in zip(far, self.orders)]
 
     def finish(self, near, came, *gates):
         depth = len(self.orders[0])
+        total = lambda terms: sum(v.astype(F32) for v in terms)
+        parts = [[k, r] for k, r in zip(near, came)]
         sends = came
-        for level in range(depth - 1, -1, -1):
-            total = [k.astype(F32) + r.astype(F32) for k, r in zip(near, came)]
-            if level:
-                half = total[0].shape[0] // 2
-                near = [v[:half] for v in total]
-                sends = [after(v[half:].astype(BF), *gates) for v in total]
-                came = [self.flip(s, o[level - 1]) for s, o in zip(sends, self.orders)]
-        return jnp.concatenate(total), sends
+        for level in range(depth - 1, 0, -1):
+            half = parts[0][0].shape[0] // 2
+            sends = [after(total([v[half:] for v in p]).astype(BF), *gates) for p in parts]
+            came = [self.flip(s, o[level - 1]) for s, o in zip(sends, self.orders)]
+            parts = [[v[:half] for v in p] + [r] for p, r in zip(parts, came)]
+        return jnp.concatenate([total(p) for p in parts]), sends, came
 
     def places(self):
         index = {}
         for h, seen in enumerate(self.lists):
             for i, r in enumerate(seen):
                 index[r, h] = h * self.nt + i
-        tables = [jnp.array([index[r, h] for r in range(self.nt)]) for h in range(2)]
-        before, behind = [], []
-        for h, seen in enumerate(self.lists):
-            for r in seen:
-                at = self.t ^ r
-                if h == 1:
-                    before.append(jnp.int32(index[r, 0]))
-                    there = (jnp.minimum(at + 1, self.nt - 1)) ^ self.t
-                    behind.append(jnp.where(at == self.nt - 1, -1, tables[0][there]))
+        table = np.zeros((self.nt, 2, 2 * self.nt), np.int32)
+        for t in range(self.nt):
+            for (r, h), i in index.items():
+                at = t ^ r
+                if h:
+                    table[t, 0, i] = index[r, 0]
+                    table[t, 1, i] = -1 if at == self.nt - 1 else index[(at + 1) ^ t, 0]
                 else:
-                    behind.append(jnp.int32(index[r, 1]))
-                    there = (jnp.maximum(at - 1, 0)) ^ self.t
-                    before.append(jnp.where(at == 0, -1, tables[1][there]))
-        return jnp.stack([jnp.stack(before), jnp.stack(behind)]).astype(jnp.int32)
-
-
-def total_of(value, sizes):
-    for axis, size in sizes:
-        bit = 1
-        while bit < size:
-            value = value + lax.ppermute(value, axis, [(i, i ^ bit) for i in range(size)])
-            bit *= 2
+                    table[t, 0, i] = -1 if at == 0 else index[(at - 1) ^ t, 1]
+                    table[t, 1, i] = index[r, 1]
+        return lax.dynamic_index_in_dim(jnp.asarray(table), self.t, keepdims=False)
+
+
+def total_of(value, axis, size):
+    bit = 1
+    while bit < size:
+        value = value + lax.ppermute(value, axis, [(i, i ^ bit) for i in range(size)])
+        bit *= 2
     return value
 
 
@@ -166,6 +164,28 @@
     return ((rows, tile), lambda j: (0, j), (rows, width), dtype)
 
 
+def pack(in_weight, out_weight, tile):
+    kinds, depth, chans = in_weight.shape
+
+    def body(win, wout, packed):
+        for j in range(chans // tile):
+            for k in range(kinds):
+                at = (j * kinds + k) * tile
+                packed[:, at : at + tile] = win[k, :, j * tile : (j + 1) * tile]
+        packed[:, kinds * chans :] = wout[...].astype(F32).T.astype(BF)
+
+    width = (kinds + 1) * chans
+    return call(
+        "pack",
+        body,
+        1,
+        [whole(in_weight), whole(out_weight)],
+        [new_columns(depth, width, width)],
+        [in_weight, out_weight],
+        0,
+    )[0]
+
+
 def gate_body(*refs):
     pieces, (gw, uw, act, silu, slope) = refs[:4], refs[4:]
     rows = pieces[0].shape[0]
@@ -220,59 +240,72 @@
     )
 
 
+def transposed_dot(left, b, columns):
+    rows = left[0].shape[0]
+    total = None
+    for i in range(4):
+        term = dot(left[i][:, columns], b[i * rows : (i + 1) * rows], TN)
+        total = term if total is None else total + term
+    return total.astype(BF)
+
+
 def weight_grad(pieces, b, into=None):
     rows, dim = pieces[0].shape
     width = b.shape[1]
     tile = next(t for t in (512, 384, 256) if width % t == 0)
     step = min(512, dim)
+    into = [] if into is None else [into]
 
     def body(*refs):
-        left, b_ref, out = refs[:4], refs[4], refs[-1]
         for d in range(0, dim, step):
-            total = None
-            for i in range(4):
-                term = dot(left[i][:, d : d + step], b_ref[i * rows : (i + 1) * rows], TN)
-                total = term if total is None else total + term
-            out[d : d + step] = total.astype(BF)
+            refs[-1][d : d + step] = transposed_dot(refs[:4], refs[4], slice(d, d + step))
 
     return call(
         "weight_grad",
         body,
         width // tile,
-        [whole(p) for p in pieces] + [columns(b, tile)] + ([] if into is None else [None]),
-        [new_columns(dim, width if into is None else into.shape[1], tile)],
-        [*pieces, b] + ([] if into is None else [into]),
+        [whole(p) for p in pieces] + [columns(b, tile)] + [None] * len(into),
+        [new_columns(dim, into[0].shape[1] if into else width, tile)],
+        [*pieces, b, *into],
         8 * rows * dim * width,
-        aliases=None if into is None else {5: 0},
+        aliases={5: 0} if into else None,
     )[0]
 
 
-def back(acts, weights, pieces, tile):
+def back(acts, weights, pieces, tile, sums=None):
     rows = acts[0].shape[0] // 4
     dim = weights[0][0].shape[0]
     tile = min(tile, dim)
     na, np_ = len(acts), len(pieces)
+    extra = [] if sums is None else [sums[p] for p in pieces]
 
     def body(*refs):
         ws = refs[na * np_ : na * np_ + na]
-        outs = refs[na * np_ + na :]
+        outs = refs[na * np_ + na + len(extra) :]
+        summed = None
         for p in range(np_):
             total = None
             for a in range(na):
                 term = dot(refs[p * na + a][...], ws[a][...], NT)
                 total = term if total is None else total + term
             outs[p][...] = total.astype(BF)
+            if extra:
+                term = total * refs[na * np_ + na + p][...].astype(F32)
+                term = jnp.sum(term, axis=0, keepdims=True)
+                summed = term if summed is None else summed + term
+        if extra:
+            outs[np_][...] = summed
 
     return call(
         "back",
         body,
         dim // tile,
         [((rows, a.shape[1]), lambda j, p=p: (p, 0), "held") for p in pieces for a in acts]
-        + [
-            ((tile, a.shape[1]), lambda j, c=c: (j, c)) for a, (_, c) in zip(acts, weights)
-        ],
-        [new_columns(rows, dim, tile)] * np_,
-        [a for _ in pieces for a in acts] + [w for w, _ in weights],
+        + [((tile, a.shape[1]), lambda j, c=c: (j, c)) for a, (_, c) in zip(acts, weights)]
+        + [columns(v, tile) for v in extra],
+        [new_columns(rows, dim, tile)] * np_
+        + ([new_columns(1, dim, tile, F32)] if extra else []),
+        [a for _ in pieces for a in acts] + [w for w, _ in weights] + extra,
         2 * np_ * rows * dim * sum(a.shape[1] for a in acts),
     )
 
@@ -362,11 +395,7 @@
         dproj[at, 2 * tile :] = (dbx * bgate[at].astype(F32)).astype(BF)
     dim = pieces[0].shape[1]
     for d in range(0, dim, 512):
-        total = None
-        for i in range(4):
-            term = dot(pieces[i][:, d : d + 512], ygate[i * rows : (i + 1) * rows], TN)
-            total = term if total is None else total + term
-        out_grad[d : d + 512] = total.astype(BF)
+        out_grad[d : d + 512] = transposed_dot(pieces, ygate, slice(d, d + 512))
 
 
 def conv_backward(pieces, weights, taps, saved, places, tile):
@@ -415,59 +444,64 @@
     dp_gather = lambda v: lax.all_gather(v, "dp", axis=0, tiled=True)
     dp_scatter = lambda v: lax.psum_scatter(v, "dp", scatter_dimension=0, tiled=True)
 
-    conv_shard = jnp.concatenate(
-        [in_weight[k, :, c : c + tile] for c in range(0, chans, tile) for k in range(3)]
-        + [out_weight.T],
-        axis=1,
-    )
+    conv_shard = pack(in_weight, out_weight, tile)
     conv_w = dp_gather(conv_shard)
     down_shard = down_weight.T
 
     hidden = tokens[0].astype(F32)
     scale1 = rms_scale(hidden)
-    n1, _ = square.gather((hidden * scale1 * norm_gain1).astype(BF))
     cot = out_grad[0]
+    g_gather = square.gather_steps(cot)
+    g_one, _ = next(g_gather)
+    n1, _ = square.gather((hidden * scale1 * norm_gain1).astype(BF), *g_one)
     gate_w = dp_gather(after(gate_weight, conv_w, n1[1], n1[3]))
-    g_gather = square.gather_steps(after(cot, n1[1], n1[3]))
-    g_first = next(g_gather)
+    g_two, g_first = g_gather.send((n1[1], n1[3]))
     saved = conv_forward(n1, conv_w, taps, places, tile)
     ygate = saved[3]
     far = back([after(ygate, *g_first)], [(conv_w, 3)], (1, 3), 1024)
     near = back([after(ygate, far[0])], [(conv_w, 3)], (0, 2), 1024)
-    branch, mid = square.finish(near, square.begin(far))
+    branch, mid, _ = square.finish(near, square.begin(far), *g_two)
     up_w = dp_gather(after(up_weight, gate_w, *mid))
     second = hidden + branch
     scale2 = rms_scale(second)
     n2, n2_first = square.gather((second * scale2 * norm_gain2).astype(BF))
     down_w = dp_gather(after(down_shard, up_w, n2[1], n2[3]))
-    g = g_gather.send((n2[1], n2[3]))
+    while g_first:
+        g_two, g_first = g_gather.send((n2[1], n2[3]))
+    g = g_two
 
     act, silu, slope = ffn_gate(n2, gate_w, up_w)
     down_part = weight_grad(first_after(g, act), act)
     down_owned = dp_scatter(down_part)
     dgate, dup = ffn_slope(first_after(g, down_part), down_w, silu, slope)
     pair = [(gate_w, 0), (up_w, 0)]
-    gate_part = weight_grad(first_after(n2, dgate), dgate)
-    far = back([after(dgate, gate_part), dup], pair, (1, 3), 512)
+    far = back([dgate, dup], pair, (1, 3), 512)
     near = back([after(dgate, far[0]), dup], pair, (0, 2), 512)
-    ffn = back([after(act, near[0])], [(down_w, 0)], (1, 3, 0, 2), 512)
-    dnormed2, mid = square.finish(near, square.begin(far), ffn[0])
+    gate_part = weight_grad(first_after(n2, near[0]), dgate)
+    dnormed2, mid, _ = square.finish(near, square.begin(far), gate_part)
     gate_owned = dp_scatter(after(gate_part, down_owned, *mid))
-    up_part = weight_grad(first_after(n2, *mid), dup)
+    ffn = back([after(act, *mid)], [(down_w, 0)], (1, 3, 0, 2), 512)
     dsecond_norm, gain2_part = norm_back(second, scale2, norm_gain2, dnormed2)
     dsecond = cot.astype(F32) + dsecond_norm
-    dbr, dbr_first = square.gather(dsecond.astype(BF))
+    sent = after(dsecond.astype(BF), ffn[0])
+    dbr, dbr_first = square.gather(sent)
+    up_part = weight_grad(first_after(n2, sent), dup)
     up_owned = dp_scatter(after(up_part, gate_owned, dbr[1], dbr[3]))
 
-    dproj, tap_part, conv_part = conv_backward(dbr, conv_w, taps, saved, places, tile)
-    far = back([dproj], [(conv_w, 0)], (1, 3), 512)
-    near = back([after(dproj, far[0])], [(conv_w, 0)], (0, 2), 512)
-    conv_part = weight_grad(first_after(n1, near[0]), dproj, conv_part)
-    dnormed, mid = square.finish(near, square.begin(far))
-    ffn, _ = square.finish(ffn[2:], square.begin([after(v, *mid) for v in ffn[:2]]))
-    conv_owned = dp_scatter(after(conv_part, up_owned, *mid))
+    dproj, tap_part, conv_part = conv_backward(
+        first_after(dbr, up_part), conv_w, taps, saved, places, tile
+    )
+    came = square.begin([after(v, dbr[1], dbr[3]) for v in ffn[:2]])
+    far = back([dproj], [(conv_w, 0)], (1, 3), 512, n1)
+    conv_part = weight_grad(first_after(n1, far[0], *came), dproj, conv_part)
+    ffn, ffn_sends, _ = square.finish(ffn[2:], came)
+    near = back([after(dproj, conv_part, *ffn_sends)], [(conv_w, 0)], (0, 2), 512, n1)
+    first_came = square.begin(far[:2])
+    dnormed, mid, last_came = square.finish(near[:2], first_came)
+    conv_owned = dp_scatter(after(conv_part, up_owned, *first_came))
+    gain1_part = (far[2] + near[2])[0] / norm_gain1
     block_out = (second + ffn).astype(BF)
-    dhidden_norm, gain1_part = norm_back(hidden, scale1, norm_gain1, dnormed)
+    dhidden_norm, _ = norm_back(hidden, scale1, norm_gain1, dnormed)
     tokens_grad = dsecond + dhidden_norm
 
     wide = lax.dynamic_update_slice_in_dim(
@@ -476,7 +510,8 @@
     small = jnp.concatenate(
         [gain1_part[None], gain2_part[None], wide, jnp.zeros_like(wide)]
     )
-    small = total_of(small, (("tensor", nt), ("dp", ndp)))
+    small = total_of(after(small, *first_came), "dp", ndp)
+    small = total_of(after(small, *last_came), "tensor", nt)
     in_owned = conv_owned[:, : 3 * chans].reshape(-1, chans // tile, 3, tile)
     in_owned = in_owned.transpose(2, 0, 1, 3)
     return (

time: 853 us -> 789 us (0.925)
  waiting for transfers between devices: 363 us -> 307 us
  local copies, waits for them, and re-layouts: 44.5 us -> 30.4 us
    ppermute x32, waiting for transfers between devices: 308 us -> 275 us  [flip(): return lax.ppermute(value, 'tensor', [(t, t ^ bit) for t in range(self.nt)])]
    ppermute x5, waiting for transfers between devices: 43.4 us -> 11 us  [total_of(): lax.ppermute(value, axis, [(i, i ^ bit) for i in range(size)])]
    convert_element_type x2 -> x9, other arithmetic: 4.24 us -> 23.3 us  [the longest x7 19 us: finish(): total([v[half:] for v in p]).astype(BF)]
    add x14 -> x7, other arithmetic: 29.4 us -> 14.3 us  [the longest x6 14.3 us: finish(): total = lambda terms: sum((v.astype(F32) for v in terms))]
    unnamed x121 -> x92, local copies, waits for them, and re-layouts: 28.3 us -> 17.8 us
    pallas_call x15 -> x16, Pallas kernels: 309 us -> 314 us  [call(): pl.pallas_call(body, grid_spec=pltpu.PrefetchScalarGridSpec(num_scalar_pr...]
  transfers between devices with their start and end apart: 45 -> 45, of which waited for: 21 -> 25; matrix products, arithmetic and copies ran while one was open for 10% -> 10% of each run, Pallas kernels for 36% -> 40%
where the time goes in v2:
time: 789 us; the launch traced here: 781 us
  Pallas kernels  314 us (40%)
  waiting for transfers between devices  307 us (39%)
  other arithmetic  68.9 us (9%)
  starting transfers between devices  45.1 us (6%)
  local copies, waits for them, and re-layouts  30.4 us (4%)
  between operations  15.3 us (2%)
    pallas_call x16, Pallas kernels, call(): pl.pallas_call(body, grid_spec=pltpu.PrefetchScalarGridSpec(num_scalar_pr...  314 us
    ppermute x32, waiting for transfers between devices, flip(): return lax.ppermute(value, 'tensor', [(t, t ^ bit) for t in range(self.nt)])  275 us
    ppermute x32, starting transfers between devices, flip(): return lax.ppermute(value, 'tensor', [(t, t ^ bit) for t in range(self.nt)])  42.6 us
    convert_element_type x7, other arithmetic, finish(): total([v[half:] for v in p]).astype(BF)  19 us
    unnamed x92, local copies, waits for them, and re-layouts  17.8 us
    all_gather x4, waiting for transfers between devices, local(): dp_gather = lambda v: lax.all_gather(v, 'dp', axis=0, tiled=True)  17.3 us
  transfers between devices with their start and end apart: 45, of which 25 were waited for; matrix products, arithmetic and copies ran while one was open for 10% of the time, Pallas kernels for 40%

profile of v2, /device:TPU:0, one launch (start us, length us, event | category | flops | bytes accessed | tf_op | source)
XLA Modules:
  0.0 780.6 jit_solution(4196901103835410636)
XLA Ops:
  17.3 20.5 %collective-permute-done.2 = bf16[256,2048]{1,0:T(8,128)(2,1)S(1)} collective-permute-done((bf16[256,2048]{1,0:T(8,128)(2,1)S(1)}, bf16[256,2048]{1,0:T(8,128)(2,1)S(1)}, u32[]{:S(2)}, u32[]{:S(2)}) %collective-permute-start.2) | collective-permute-done | bytes 1048608 | tf_op jit(solution)/shard_map/ppermute | solution.py:60
  41.7 43.4 %collective-permute-done.3.refs_3_.refs_4_ = bf16[512,2048]{1,0:T(8,128)(2,1)S(1)} collective-permute-done((bf16[512,2048]{1,0:T(8,128)(2,1)S(1)}, bf16[512,2048]{1,0:T(8,128)(2,1)S(1)}, u32[]{:S(2)}, u32[]{:S(2)}) %collective-permute-start.3) | collective-permute-done | bytes 2097184 | tf_op jit(solution)/shard_map/ppermute | solution.py:60
  86.6 8.4 %all-gather.5.cloned.1.call-done.refs_4_.refs_2_ = bf16[2048,2048]{1,0:T(8,128)(2,1)} async-done(((bf16[256,2048]{1,0:T(8,128)(2,1)}), bf16[2048,2048]{1,0:T(8,128)(2,1)}) %all-gather.5.cloned.1.call-update) | async-done | bytes 8388624 | tf_op jit(solution)/shard_map/all_gather | solution.py:444
  100.0 22.3 %conv_fwd.1 = (bf16[2048,512]{1,0:T(8,128)(2,1)}, bf16[2048,512]{1,0:T(8,128)(2,1)}, bf16[2048,512]{1,0:T(8,128)(2,1)}, bf16[2048,512]{1,0:T(8,128)(2,1)}) custom-call(s32[2,8]{1,0:T(2,128)} %dynamic-slice_bitcast_fusion.places, bf16[512,2048]{1,0:T(8,128)(2,1)} %copy-done.14, bf16[512,2048]{1,0:T(8,128)(2,1)} %collective-permute-done.1.refs_1_.refs_3_, ...), custom_call_target="tpu_custom_call" | custom-call | flops 2576980480 | bytes 5034393 | tf_op jit(solution)/shard_map/conv_fwd/pallas_call | solution.py:136
  122.3 5.2 back.7
  135.9 5.1 back.8
  141.1 33.8 %collective-permute-done.6 = bf16[512,2048]{1,0:T(8,128)(2,1)} collective-permute-done((bf16[512,2048]{1,0:T(8,128)(2,1)}, bf16[512,2048]{1,0:T(8,128)(2,1)}, u32[]{:S(2)}, u32[]{:S(2)}) %collective-permute-start.6) | collective-permute-done | bytes 2097184 | tf_op jit(solution)/shard_map/ppermute | solution.py:60
  174.9 4.0 add_convert_fusion.6
  181.6 21.5 %collective-permute-done.7 = bf16[256,2048]{1,0:T(8,128)(2,1)S(1)} collective-permute-done((bf16[256,2048]{1,0:T(8,128)(2,1)}, bf16[256,2048]{1,0:T(8,128)(2,1)S(1)}, u32[]{:S(2)}, u32[]{:S(2)}) %collective-permute-start.7) | collective-permute-done | bytes 1048608 | tf_op jit(solution)/shard_map/ppermute | solution.py:60
  213.1 19.8 %collective-permute-done.12 = bf16[256,2048]{1,0:T(8,128)(2,1)S(1)} collective-permute-done((bf16[256,2048]{1,0:T(8,128)(2,1)S(1)}, bf16[256,2048]{1,0:T(8,128)(2,1)S(1)}, u32[]{:S(2)}, u32[]{:S(2)}) %collective-permute-start.12) | collective-permute-done | bytes 1048608 | tf_op jit(solution)/shard_map/ppermute | solution.py:60
  241.3 38.6 %collective-permute-done.13.refs_3_ = bf16[512,2048]{1,0:T(8,128)(2,1)} collective-permute-done((bf16[512,2048]{1,0:T(8,128)(2,1)}, bf16[512,2048]{1,0:T(8,128)(2,1)}, u32[]{:S(2)}, u32[]{:S(2)}) %collective-permute-start.13) | collective-permute-done | bytes 2097184 | tf_op jit(solution)/shard_map/ppermute | solution.py:60
  285.4 43.9 %ffn_gate.1 = (bf16[2048,2048]{1,0:T(8,128)(2,1)}, bf16[2048,2048]{1,0:T(8,128)(2,1)}, bf16[2048,2048]{1,0:T(8,128)(2,1)}) custom-call(bf16[512,2048]{1,0:T(8,128)(2,1)} %pad_maximum_fusion.3.refs_0_, bf16[512,2048]{1,0:T(8,128)(2,1)} %collective-permute-done.11.refs_1_, bf16[512,2048]{1,0:T(8,128)(2,1)} %pad_maximum_fusion.4.refs_2_, ...), custom_call_target="tpu_custom_call" | custom-call | flops 6871947776 | bytes 10066329 | tf_op jit(solution)/shard_map/ffn_gate/pallas_call | solution.py:136
  330.6 23.7 %weight_grad.4 = bf16[2048,2048]{1,0:T(8,128)(2,1)} custom-call(bf16[512,2048]{1,0:T(8,128)(2,1)} %constant_dynamic-update-slice_fusion.refs_0_, bf16[512,2048]{1,0:T(8,128)(2,1)} %collective-permute-done.14.refs_1_, bf16[512,2048]{1,0:T(8,128)(2,1)} %constant_dynamic-update-slice_fusion.2.refs_2_, bf16[512,2048]{1,0:T(8,128)(2,1)} %copy-done.19, ...), custom_call_target="tpu_custom_call" | custom-call | flops 3435973888 | bytes 5033164 | tf_op jit(solution)/shard_map/weight_grad/pallas_call | solution.py:136
  354.9 8.9 %all-gather.11.cloned.1.call-done.refs_4_ = bf16[2048,2048]{1,0:T(8,128)(2,1)} async-done(((bf16[256,2048]{1,0:T(8,128)(2,1)}), bf16[2048,2048]{1,0:T(8,128)(2,1)}) %all-gather.11.cloned.1.call-update) | async-done | bytes 8388624 | tf_op jit(solution)/shard_map/all_gather | solution.py:444
  363.7 27.1 %ffn_slope.1 = (bf16[2048,2048]{1,0:T(8,128)(2,1)}, bf16[2048,2048]{1,0:T(8,128)(2,1)}) custom-call(bf16[512,2048]{1,0:T(8,128)(2,1)} %constant_dynamic-update-slice_fusion.refs_0_, bf16[512,2048]{1,0:T(8,128)(2,1)} %collective-permute-done.14.refs_1_, bf16[512,2048]{1,0:T(8,128)(2,1)} %constant_dynamic-update-slice_fusion.2.refs_2_, ...), custom_call_target="tpu_custom_call" | custom-call | flops 3435973888 | bytes 10066329 | tf_op jit(solution)/shard_map/ffn_slope/pallas_call | solution.py:136
  390.9 23.8 %back.9 = (bf16[512,2048]{1,0:T(8,128)(2,1)}, bf16[512,2048]{1,0:T(8,128)(2,1)}) custom-call(bf16[2048,2048]{1,0:T(8,128)(2,1)} %get-tuple-element.98.refs_0_.refs_2_.refs_4_, bf16[2048,2048]{1,0:T(8,128)(2,1)} %get-tuple-element.96.refs_1_.refs_3_.refs_4_, bf16[2048,2048]{1,0:T(8,128)(2,1)} %get-tuple-element.98.refs_0_.refs_2_.refs_4_, ...), custom_call_target="tpu_custom_call" | custom-call | flops 3435973888 | bytes 10905190 | tf_op jit(solution)/shard_map/back/pallas_call | solution.py:136
  417.7 23.8 %back.10 = (bf16[512,2048]{1,0:T(8,128)(2,1)}, bf16[512,2048]{1,0:T(8,128)(2,1)}) custom-call(bf16[2048,2048]{1,0:T(8,128)(2,1)} %get-tuple-element.98.refs_0_.refs_2_.refs_4_, bf16[2048,2048]{1,0:T(8,128)(2,1)} %get-tuple-element.96.refs_1_.refs_3_.refs_4_, bf16[2048,2048]{1,0:T(8,128)(2,1)} %get-tuple-element.98.refs_0_.refs_2_.refs_4_, ...), custom_call_target="tpu_custom_call" | custom-call | flops 3435973888 | bytes 10905190 | tf_op jit(solution)/shard_map/back/pallas_call | solution.py:136
  441.4 23.7 %weight_grad.5 = bf16[2048,2048]{1,0:T(8,128)(2,1)} custom-call(bf16[512,2048]{1,0:T(8,128)(2,1)} %pad_maximum_fusion.3.refs_0_, bf16[512,2048]{1,0:T(8,128)(2,1)} %collective-permute-done.11.refs_1_, bf16[512,2048]{1,0:T(8,128)(2,1)} %pad_maximum_fusion.4.refs_2_, bf16[512,2048]{1,0:T(8,128)(2,1)} %collective-permute-done.13.refs_3_, ...), custom_call_target="tpu_custom_call" | custom-call | flops 3435973888 | bytes 5033164 | tf_op jit(solution)/shard_map/weight_grad/pallas_call | solution.py:136
  471.1 24.0 %back.11 = (bf16[512,2048]{1,0:T(8,128)(2,1)}, bf16[512,2048]{1,0:T(8,128)(2,1)}, bf16[512,2048]{1,0:T(8,128)(2,1)}, bf16[512,2048]{1,0:T(8,128)(2,1)}) custom-call(bf16[2048,2048]{1,0:T(8,128)(2,1)} %get-tuple-element.105.refs_4_.refs_0_.refs_1_.refs_2_.refs_3_, bf16[2048,2048]{1,0:T(8,128)(2,1)} %get-tuple-element.105.refs_4_.refs_0_.refs_1_.refs_2_.refs_3_, ...), custom_call_target="tpu_custom_call" | custom-call | flops 3435973888 | bytes 10066329 | tf_op jit(solution)/shard_map/back/pallas_call | solution.py:136
  510.4 21.3 %collective-permute-done.22 = bf16[256,2048]{1,0:T(8,128)(2,1)S(1)} collective-permute-done((bf16[256,2048]{1,0:T(8,128)(2,1)S(1)}, bf16[256,2048]{1,0:T(8,128)(2,1)S(1)}, u32[]{:S(2)}, u32[]{:S(2)}) %collective-permute-start.22) | collective-permute-done | bytes 1048608 | tf_op jit(solution)/shard_map/ppermute | solution.py:60
  537.9 23.8 %weight_grad.6 = bf16[2048,2048]{1,0:T(8,128)(2,1)} custom-call(bf16[512,2048]{1,0:T(8,128)(2,1)} %pad_maximum_fusion.3.refs_0_, bf16[512,2048]{1,0:T(8,128)(2,1)} %collective-permute-done.11.refs_1_, bf16[512,2048]{1,0:T(8,128)(2,1)} %pad_maximum_fusion.4.refs_2_, bf16[512,2048]{1,0:T(8,128)(2,1)} %collective-permute-done.13.refs_3_, ...), custom_call_target="tpu_custom_call" | custom-call | flops 3435973888 | bytes 5033164 | tf_op jit(solution)/shard_map/weight_grad/pallas_call | solution.py:136
  561.7 17.8 %collective-permute-done.23.refs_3_ = bf16[512,2048]{1,0:T(8,128)(2,1)} collective-permute-done((bf16[512,2048]{1,0:T(8,128)(2,1)}, bf16[512,2048]{1,0:T(8,128)(2,1)}, u32[]{:S(2)}, u32[]{:S(2)}) %collective-permute-start.23) | collective-permute-done | bytes 2097184 | tf_op jit(solution)/shard_map/ppermute | solution.py:60
  584.5 23.4 %conv_bwd.1 = (bf16[2048,1536]{1,0:T(8,128)(2,1)}, f32[3,512]{1,0:T(4,128)}, bf16[2048,2048]{1,0:T(8,128)(2,1)}) custom-call(s32[2,8]{1,0:T(2,128)} %dynamic-slice_bitcast_fusion.places, bf16[512,2048]{1,0:T(8,128)(2,1)} %pad_maximum_fusion.5.refs_0_, bf16[512,2048]{1,0:T(8,128)(2,1)} %collective-permute-done.21.refs_1_, ...), custom_call_target="tpu_custom_call" | custom-call | flops 1717986944 | bytes 7971635 | tf_op jit(solution)/shard_map/conv_bwd/pallas_call | solution.py:136
  607.8 11.1 %back.12 = (bf16[512,2048]{1,0:T(8,128)(2,1)}, bf16[512,2048]{1,0:T(8,128)(2,1)}, f32[1,2048]{1,0:T(1,128)}) custom-call(bf16[2048,1536]{1,0:T(8,128)(2,1)} %get-tuple-element.122.refs_0_.refs_1_.refs_4_, bf16[2048,1536]{1,0:T(8,128)(2,1)} %get-tuple-element.122.refs_0_.refs_1_.refs_4_, bf16[2048,2048]{1,0:T(8,128)(2,1)} %all-gather.5.cloned.1.call-done.refs_4_.refs_2_, ...), custom_call_target="tpu_custom_call" | custom-call | flops 1288490240 | bytes 5873664 | tf_op jit(solution)/shard_map/back/pallas_call | solution.py:136
  621.5 9.9 %collective-permute-done.24 = bf16[512,2048]{1,0:T(8,128)(2,1)} collective-permute-done((bf16[512,2048]{1,0:T(8,128)(2,1)}, bf16[512,2048]{1,0:T(8,128)(2,1)}, u32[]{:S(2)}, u32[]{:S(2)}) %collective-permute-start.24) | collective-permute-done | bytes 2097184 | tf_op jit(solution)/shard_map/ppermute | solution.py:60
  632.9 19.4 %weight_grad.7 = bf16[2048,2048]{1,0:T(8,128)(2,1)} custom-call(bf16[512,2048]{1,0:T(8,128)(2,1)} %copy-done.14, bf16[512,2048]{1,0:T(8,128)(2,1)} %collective-permute-done.1.refs_1_.refs_3_, bf16[512,2048]{1,0:T(8,128)(2,1)} %copy-done.13, bf16[512,2048]{1,0:T(8,128)(2,1)} %copy-done.18, ...), custom_call_target="tpu_custom_call", output_to_operand_aliasing={{}: (5, {})} | custom-call | flops 2576980480 | bytes 6291456 | tf_op jit(solution)/shard_map/weight_grad/pallas_call | solution.py:136
  652.3 20.0 %collective-permute-done.28 = bf16[512,2048]{1,0:T(8,128)(2,1)} collective-permute-done((bf16[512,2048]{1,0:T(8,128)(2,1)}, bf16[512,2048]{1,0:T(8,128)(2,1)}, u32[]{:S(2)}, u32[]{:S(2)}) %collective-permute-start.28) | collective-permute-done | bytes 2097184 | tf_op jit(solution)/shard_map/ppermute | solution.py:60
  678.6 11.1 %back.13 = (bf16[512,2048]{1,0:T(8,128)(2,1)}, bf16[512,2048]{1,0:T(8,128)(2,1)}, f32[1,2048]{1,0:T(1,128)}) custom-call(bf16[2048,1536]{1,0:T(8,128)(2,1)} %get-tuple-element.122.refs_0_.refs_1_.refs_4_, bf16[2048,1536]{1,0:T(8,128)(2,1)} %get-tuple-element.122.refs_0_.refs_1_.refs_4_, bf16[2048,2048]{1,0:T(8,128)(2,1)} %all-gather.5.cloned.1.call-done.refs_4_.refs_2_, ...), custom_call_target="tpu_custom_call" | custom-call | flops 1288490240 | bytes 5873664 | tf_op jit(solution)/shard_map/back/pallas_call | solution.py:136
  698.0 6.5 collective-permute-done.33
  713.5 5.0 collective-permute-done.29
  728.5 9.6 %collective-permute-done.25 = bf16[256,2048]{1,0:T(8,128)(2,1)S(1)} collective-permute-done((bf16[256,2048]{1,0:T(8,128)(2,1)}, bf16[256,2048]{1,0:T(8,128)(2,1)S(1)}, u32[]{:S(2)}, u32[]{:S(2)}) %collective-permute-start.25) | collective-permute-done | bytes 1048608 | tf_op jit(solution)/shard_map/ppermute | solution.py:60
  743.1 5.5 fusion.6
  (236 shorter events, 159.2 us)
Async XLA Ops:
  7.2 87.8 %all-gather.5.cloned.1.call-start = ((), (), s32[]{:S(2)}) async-start(), calls=%async_computation.4 | async-start | bytes 9437184 | tf_op jit(solution)/shard_map/all_gather | solution.py:444
  9.7 169.2 %all-gather.7.cloned.1.call-start = ((), (), s32[]{:S(2)}) async-start(), calls=%async_computation.5 | async-start | bytes 9437184 | tf_op jit(solution)/shard_map/all_gather | solution.py:444
  11.6 26.2 %collective-permute-start.2 = (bf16[256,2048]{1,0:T(8,128)(2,1)S(1)}, bf16[256,2048]{1,0:T(8,128)(2,1)S(1)}, u32[]{:S(2)}, u32[]{:S(2)}) collective-permute-start(bf16[256,2048]{1,0:T(8,128)(2,1)S(1)} %get-tuple-element.170), channel_id=1, source_target_pairs={{0,2},{1,3},{2,0},{3,1},{4,6},{5,7},{6,4},{7,5},{8,10},{9,11},{10,... | collective-permute-start | bytes 3145736 | tf_op jit(solution)/shard_map/ppermute | solution.py:60
  38.1 47.0 %collective-permute-start.3 = (bf16[512,2048]{1,0:T(8,128)(2,1)S(1)}, bf16[512,2048]{1,0:T(8,128)(2,1)S(1)}, u32[]{:S(2)}, u32[]{:S(2)}) collective-permute-start(bf16[512,2048]{1,0:T(8,128)(2,1)S(1)} %pad_maximum_fusion.2.refs_2_.refs_4_), channel_id=1, source_target_pairs={{0,1},{1,0},{2,3},{3,2},{4,5},{5,4},{6,7},{7,6},{8,9},{9,8},{10,11... | collective-permute-start | bytes 6291464 | tf_op jit(solution)/shard_map/ppermute | solution.py:60
  40.1 46.5 %collective-permute-start.1 = (bf16[512,2048]{1,0:T(8,128)(2,1)S(1)}, bf16[512,2048]{1,0:T(8,128)(2,1)}, u32[]{:S(2)}, u32[]{:S(2)}) collective-permute-start(bf16[512,2048]{1,0:T(8,128)(2,1)S(1)} %pad_maximum_fusion.1.refs_0_.refs_3_), channel_id=1, source_target_pairs={{0,2},{1,3},{2,0},{3,1},{4,6},{5,7},{6,4},{7,5},{8,10},{9,11},{10,... | collective-permute-start | bytes 6291464 | tf_op jit(solution)/shard_map/ppermute | solution.py:60
  95.0 188.4 %all-gather.9.cloned.1.call-start = ((), (), s32[]{:S(2)}) async-start(), calls=%async_computation.6 | async-start | bytes 9437184 | tf_op jit(solution)/shard_map/all_gather | solution.py:444
  95.1 27.2 %collective-permute-start.5 = (bf16[256,2048]{1,0:T(8,128)(2,1)}, bf16[256,2048]{1,0:T(8,128)(2,1)}, u32[]{:S(2)}, u32[]{:S(2)}) collective-permute-start(bf16[256,2048]{1,0:T(8,128)(2,1)} %get-tuple-element.76), channel_id=1, source_target_pairs={{0,2},{1,3},{2,0},{3,1},{4,6},{5,7},{6,4},{7,5},{8,10},{9,11},{10,... | collective-permute-start | bytes 3145736 | tf_op jit(solution)/shard_map/ppermute | solution.py:60
  127.6 47.3 %collective-permute-start.6 = (bf16[512,2048]{1,0:T(8,128)(2,1)}, bf16[512,2048]{1,0:T(8,128)(2,1)}, u32[]{:S(2)}, u32[]{:S(2)}) collective-permute-start(bf16[512,2048]{1,0:T(8,128)(2,1)} %get-tuple-element.78), channel_id=1, source_target_pairs={{0,2},{1,3},{2,0},{3,1},{4,6},{5,7},{6,4},{7,5},{8,10},{9,11},{10,... | collective-permute-start | bytes 6291464 | tf_op jit(solution)/shard_map/ppermute | solution.py:60
  127.6 47.3 %collective-permute-start.8 = (bf16[512,2048]{1,0:T(8,128)(2,1)}, bf16[512,2048]{1,0:T(8,128)(2,1)}, u32[]{:S(2)}, u32[]{:S(2)}) collective-permute-start(bf16[512,2048]{1,0:T(8,128)(2,1)} %get-tuple-element.83), channel_id=1, source_target_pairs={{0,1},{1,0},{2,3},{3,2},{4,5},{5,4},{6,7},{7,6},{8,9},{9,8},{10,11... | collective-permute-start | bytes 6291464 | tf_op jit(solution)/shard_map/ppermute | solution.py:60
  178.9 184.8 %all-gather.11.cloned.1.call-start = ((), (), s32[]{:S(2)}) async-start(), calls=%async_computation.7 | async-start | bytes 9437184 | tf_op jit(solution)/shard_map/all_gather | solution.py:444
  234.4 45.4 %collective-permute-start.13 = (bf16[512,2048]{1,0:T(8,128)(2,1)}, bf16[512,2048]{1,0:T(8,128)(2,1)}, u32[]{:S(2)}, u32[]{:S(2)}) collective-permute-start(bf16[512,2048]{1,0:T(8,128)(2,1)} %pad_maximum_fusion.4.refs_2_), channel_id=1, source_target_pairs={{0,1},{1,0},{2,3},{3,2},{4,5},{5,4},{6,7},{7,6},{8,9},{9,8},{10,11... | collective-permute-start | bytes 6291464 | tf_op jit(solution)/shard_map/ppermute | solution.py:60
  238.1 45.4 %collective-permute-start.11 = (bf16[512,2048]{1,0:T(8,128)(2,1)}, bf16[512,2048]{1,0:T(8,128)(2,1)}, u32[]{:S(2)}, u32[]{:S(2)}) collective-permute-start(bf16[512,2048]{1,0:T(8,128)(2,1)} %pad_maximum_fusion.3.refs_0_), channel_id=1, source_target_pairs={{0,2},{1,3},{2,0},{3,1},{4,6},{5,7},{6,4},{7,5},{8,10},{9,11},{10,... | collective-permute-start | bytes 6291464 | tf_op jit(solution)/shard_map/ppermute | solution.py:60
  283.5 186.4 %reduce-scatter.5.cloned.1.call-start = ((), (), s32[]{:S(2)}) async-start(), calls=%async_computation.8 | async-start | bytes 9437184 | tf_op jit(solution)/shard_map/reduce_scatter | solution.py:445
  283.5 45.8 %collective-permute-start.15 = (bf16[512,2048]{1,0:T(8,128)(2,1)}, bf16[512,2048]{1,0:T(8,128)(2,1)S(1)}, u32[]{:S(2)}, u32[]{:S(2)}) collective-permute-start(bf16[512,2048]{1,0:T(8,128)(2,1)} %constant_dynamic-update-slice_fusion.2.refs_2_), channel_id=1, source_target_pairs={{0,1},{1,0},{2,3},{3,2},{4,5},{5,4},{6,7},{7,6},{8,9},{9,8},{10,11... | collective-permute-start | bytes 6291464 | tf_op jit(solution)/shard_map/ppermute | solution.py:60
  283.7 45.6 %collective-permute-start.14 = (bf16[512,2048]{1,0:T(8,128)(2,1)}, bf16[512,2048]{1,0:T(8,128)(2,1)}, u32[]{:S(2)}, u32[]{:S(2)}) collective-permute-start(bf16[512,2048]{1,0:T(8,128)(2,1)} %constant_dynamic-update-slice_fusion.refs_0_), channel_id=1, source_target_pairs={{0,2},{1,3},{2,0},{3,1},{4,6},{5,7},{6,4},{7,5},{8,10},{9,11},{10,... | collective-permute-start | bytes 6291464 | tf_op jit(solution)/shard_map/ppermute | solution.py:60
  354.4 227.9 %reduce-scatter.7.cloned.1.call-start = ((), (), s32[]{:S(2)}) async-start(), calls=%async_computation.9 | async-start | bytes 9437184 | tf_op jit(solution)/shard_map/reduce_scatter | solution.py:445
  414.7 50.5 %collective-permute-start.16 = (bf16[512,2048]{1,0:T(8,128)(2,1)}, bf16[512,2048]{1,0:T(8,128)(2,1)}, u32[]{:S(2)}, u32[]{:S(2)}) collective-permute-start(bf16[512,2048]{1,0:T(8,128)(2,1)} %get-tuple-element.97), channel_id=1, source_target_pairs={{0,2},{1,3},{2,0},{3,1},{4,6},{5,7},{6,4},{7,5},{8,10},{9,11},{10,... | collective-permute-start | bytes 6291464 | tf_op jit(solution)/shard_map/ppermute | solution.py:60
  416.2 52.0 %collective-permute-start.17 = (bf16[512,2048]{1,0:T(8,128)(2,1)}, bf16[512,2048]{1,0:T(8,128)(2,1)}, u32[]{:S(2)}, u32[]{:S(2)}) collective-permute-start(bf16[512,2048]{1,0:T(8,128)(2,1)} %get-tuple-element.103), channel_id=1, source_target_pairs={{0,1},{1,0},{2,3},{3,2},{4,5},{5,4},{6,7},{7,6},{8,9},{9,8},{10,11... | collective-permute-start | bytes 6291464 | tf_op jit(solution)/shard_map/ppermute | solution.py:60
  469.9 203.9 %reduce-scatter.9.cloned.1.call-start = ((), (), s32[]{:S(2)}) async-start(), calls=%async_computation.10 | async-start | bytes 9437184 | tf_op jit(solution)/shard_map/reduce_scatter | solution.py:445
  470.6 26.8 %collective-permute-start.19 = (bf16[256,2048]{1,0:T(8,128)(2,1)S(1)}, bf16[256,2048]{1,0:T(8,128)(2,1)}, u32[]{:S(2)}, u32[]{:S(2)}) collective-permute-start(bf16[256,2048]{1,0:T(8,128)(2,1)S(1)} %add_convert_fusion.4), channel_id=1, source_target_pairs={{0,2},{1,3},{2,0},{3,1},{4,6},{5,7},{6,4},{7,5},{8,10},{9,11},{10,... | collective-permute-start | bytes 3145736 | tf_op jit(solution)/shard_map/ppermute | solution.py:60
  509.0 25.8 %collective-permute-start.20 = (bf16[256,2048]{1,0:T(8,128)(2,1)S(1)}, bf16[256,2048]{1,0:T(8,128)(2,1)S(1)}, u32[]{:S(2)}, u32[]{:S(2)}) collective-permute-start(bf16[256,2048]{1,0:T(8,128)(2,1)S(1)} %get-tuple-element.167), channel_id=1, source_target_pairs={{0,1},{1,0},{2,3},{3,2},{4,5},{5,4},{6,7},{7,6},{8,9},{9,8},{10,11... | collective-permute-start | bytes 3145736 | tf_op jit(solution)/shard_map/ppermute | solution.py:60
  533.3 46.2 %collective-permute-start.23 = (bf16[512,2048]{1,0:T(8,128)(2,1)}, bf16[512,2048]{1,0:T(8,128)(2,1)}, u32[]{:S(2)}, u32[]{:S(2)}) collective-permute-start(bf16[512,2048]{1,0:T(8,128)(2,1)} %pad_maximum_fusion.6.refs_2_), channel_id=1, source_target_pairs={{0,1},{1,0},{2,3},{3,2},{4,5},{5,4},{6,7},{7,6},{8,9},{9,8},{10,11... | collective-permute-start | bytes 6291464 | tf_op jit(solution)/shard_map/ppermute | solution.py:60
  536.4 45.9 %collective-permute-start.21 = (bf16[512,2048]{1,0:T(8,128)(2,1)}, bf16[512,2048]{1,0:T(8,128)(2,1)}, u32[]{:S(2)}, u32[]{:S(2)}) collective-permute-start(bf16[512,2048]{1,0:T(8,128)(2,1)} %pad_maximum_fusion.5.refs_0_), channel_id=1, source_target_pairs={{0,2},{1,3},{2,0},{3,1},{4,6},{5,7},{6,4},{7,5},{8,10},{9,11},{10,... | collective-permute-start | bytes 6291464 | tf_op jit(solution)/shard_map/ppermute | solution.py:60
  582.3 180.3 %reduce-scatter.11.cloned.1.call-start = ((), (), s32[]{:S(2)}) async-start(), calls=%async_computation.11 | async-start | bytes 9437184 | tf_op jit(solution)/shard_map/reduce_scatter | solution.py:445
  582.4 48.9 %collective-permute-start.24 = (bf16[512,2048]{1,0:T(8,128)(2,1)}, bf16[512,2048]{1,0:T(8,128)(2,1)}, u32[]{:S(2)}, u32[]{:S(2)}) collective-permute-start(bf16[512,2048]{1,0:T(8,128)(2,1)} %get-tuple-element.109), channel_id=1, source_target_pairs={{0,2},{1,3},{2,0},{3,1},{4,6},{5,7},{6,4},{7,5},{8,10},{9,11},{10,... | collective-permute-start | bytes 6291464 | tf_op jit(solution)/shard_map/ppermute | solution.py:60
  584.1 48.9 %collective-permute-start.26 = (bf16[512,2048]{1,0:T(8,128)(2,1)}, bf16[512,2048]{1,0:T(8,128)(2,1)}, u32[]{:S(2)}, u32[]{:S(2)}) collective-permute-start(bf16[512,2048]{1,0:T(8,128)(2,1)} %get-tuple-element.112), channel_id=1, source_target_pairs={{0,1},{1,0},{2,3},{3,2},{4,5},{5,4},{6,7},{7,6},{8,9},{9,8},{10,11... | collective-permute-start | bytes 6291464 | tf_op jit(solution)/shard_map/ppermute | solution.py:60
  619.0 53.4 %collective-permute-start.28 = (bf16[512,2048]{1,0:T(8,128)(2,1)}, bf16[512,2048]{1,0:T(8,128)(2,1)}, u32[]{:S(2)}, u32[]{:S(2)}) collective-permute-start(bf16[512,2048]{1,0:T(8,128)(2,1)} %get-tuple-element.119), channel_id=1, source_target_pairs={{0,2},{1,3},{2,0},{3,1},{4,6},{5,7},{6,4},{7,5},{8,10},{9,11},{10,... | collective-permute-start | bytes 6291464 | tf_op jit(solution)/shard_map/ppermute | solution.py:60
  620.0 53.8 %collective-permute-start.30 = (bf16[512,2048]{1,0:T(8,128)(2,1)}, bf16[512,2048]{1,0:T(8,128)(2,1)}, u32[]{:S(2)}, u32[]{:S(2)}) collective-permute-start(bf16[512,2048]{1,0:T(8,128)(2,1)} %get-tuple-element.125), channel_id=1, source_target_pairs={{0,1},{1,0},{2,3},{3,2},{4,5},{5,4},{6,7},{7,6},{8,9},{9,8},{10,11... | collective-permute-start | bytes 6291464 | tf_op jit(solution)/shard_map/ppermute | solution.py:60
  696.1 26.4 %collective-permute-start.31 = (bf16[256,2048]{1,0:T(8,128)(2,1)}, bf16[256,2048]{1,0:T(8,128)(2,1)}, u32[]{:S(2)}, u32[]{:S(2)}) collective-permute-start(bf16[256,2048]{1,0:T(8,128)(2,1)} %add_convert_fusion), channel_id=1, source_target_pairs={{0,2},{1,3},{2,0},{3,1},{4,6},{5,7},{6,4},{7,5},{8,10},{9,11},{10,... | collective-permute-start | bytes 3145736 | tf_op jit(solution)/shard_map/ppermute | solution.py:60
  709.1 29.1 %collective-permute-start.25 = (bf16[256,2048]{1,0:T(8,128)(2,1)}, bf16[256,2048]{1,0:T(8,128)(2,1)S(1)}, u32[]{:S(2)}, u32[]{:S(2)}) collective-permute-start(bf16[256,2048]{1,0:T(8,128)(2,1)} %add_convert_fusion.3), channel_id=1, source_target_pairs={{0,1},{1,0},{2,3},{3,2},{4,5},{5,4},{6,7},{7,6},{8,9},{9,8},{10,11... | collective-permute-start | bytes 3145736 | tf_op jit(solution)/shard_map/ppermute | solution.py:60
  711.2 37.4 %collective-permute-start.27 = (bf16[256,2048]{1,0:T(8,128)(2,1)S(1)}, bf16[256,2048]{1,0:T(8,128)(2,1)S(1)}, u32[]{:S(2)}, u32[]{:S(2)}) collective-permute-start(bf16[256,2048]{1,0:T(8,128)(2,1)S(1)} %add_convert_fusion.2), channel_id=1, source_target_pairs={{0,2},{1,3},{2,0},{3,1},{4,6},{5,7},{6,4},{7,5},{8,10},{9,11},{10,... | collective-permute-start | bytes 3145736 | tf_op jit(solution)/shard_map/ppermute | solution.py:60
  722.5 27.9 %collective-permute-start.35 = (f32[8,2048]{1,0:T(8,128)S(1)}, f32[8,2048]{1,0:T(8,128)S(1)}, u32[]{:S(2)}, u32[]{:S(2)}) collective-permute-start(f32[8,2048]{1,0:T(8,128)S(1)} %add.186), channel_id=1, source_target_pairs={{0,1},{1,0},{2,3},{3,2},{4,5},{5,4},{6,7},{7,6},{8,9},{9,8},{10,11... | collective-permute-start | bytes 196616 | tf_op jit(solution)/shard_map/ppermute | solution.py:123
  (56 other events, 582.8 us)
Sparse Core Ops, SparseCore 0:
  10.2 84.7 all-gather.4
  96.6 80.5 all-gather.6
  179.0 80.3 all-gather.8
  283.6 80.0 all-gather.10
  365.9 88.1 reduce-scatter.4
  470.0 86.3 reduce-scatter.6
  582.5 86.9 reduce-scatter.8
  674.0 88.5 reduce-scatter.10

commit v3 on v2

--- a/solution.py
+++ b/solution.py
@@ -125,7 +125,7 @@
     return value
 
 
-def call(name, body, grid, ins, outs, args, flops, scratch=(), scalars=(), aliases=None):
+def call(name, body, grid, ins, outs, args, flops, scratch=(), scalars=(), aliases=None, weight=1.0):
     held = lambda spec: pl.BlockSpec(memory_space=pl.ANY) if spec is None else pl.BlockSpec(
         spec[0],
         lambda j, *_: spec[1](j),
@@ -147,7 +147,9 @@
         input_output_aliases=aliases or {},
         compiler_params=pltpu.CompilerParams(vmem_limit_bytes=VMEM_LIMIT),
         cost_estimate=pl.CostEstimate(
-            flops=int(flops * COST), bytes_accessed=int(moved * COST), transcendentals=0
+            flops=int(flops * COST * weight),
+            bytes_accessed=int(moved * COST * weight),
+            transcendentals=0,
         ),
     )(*scalars, *args)
 
@@ -184,6 +186,31 @@
         [in_weight, out_weight],
         0,
     )[0]
+
+
+def unpack(packed, chans, tile):
+    depth = packed.shape[0]
+    kinds = packed.shape[1] // chans - 1
+
+    def body(src, win, wout):
+        for j in range(chans // tile):
+            for k in range(kinds):
+                at = (j * kinds + k) * tile
+                win[k, :, j * tile : (j + 1) * tile] = src[:, at : at + tile].astype(F32)
+        wout[...] = src[:, kinds * chans :].astype(F32).T
+
+    return call(
+        "unpack",
+        body,
+        1,
+        [whole(packed)],
+        [
+            ((kinds, depth, chans), lambda j: (0, 0, 0), (kinds, depth, chans), F32),
+            ((chans, depth), lambda j: (0, 0), (chans, depth), F32),
+        ],
+        [packed],
+        0,
+    )
 
 
 def gate_body(*refs):
@@ -212,6 +239,7 @@
         [new_columns(tokens, width, tile)] * 3,
         [*pieces, gate, up],
         4 * tokens * dim * width,
+        weight=20.0,
     )
 
 
@@ -272,7 +300,7 @@
     )[0]
 
 
-def back(acts, weights, pieces, tile, sums=None):
+def back(acts, weights, pieces, tile, sums=None, weight=1.0):
     rows = acts[0].shape[0] // 4
     dim = weights[0][0].shape[0]
     tile = min(tile, dim)
@@ -307,6 +335,7 @@
         + ([new_columns(1, dim, tile, F32)] if extra else []),
         [a for _ in pieces for a in acts] + [w for w, _ in weights] + extra,
         2 * np_ * rows * dim * sum(a.shape[1] for a in acts),
+        weight=weight,
     )
 
 
@@ -418,6 +447,7 @@
         4 * tokens * dim * chans,
         [pltpu.VMEM((tokens, tile), F32)] * 2,
         [places],
+        weight=88.0,
     )
 
 
@@ -465,7 +495,7 @@
     second = hidden + branch
     scale2 = rms_scale(second)
     n2, n2_first = square.gather((second * scale2 * norm_gain2).astype(BF))
-    down_w = dp_gather(after(down_shard, up_w, n2[1], n2[3]))
+    down_w = dp_gather(after(down_shard, up_w, *n2_first))
     while g_first:
         g_two, g_first = g_gather.send((n2[1], n2[3]))
     g = g_two
@@ -486,7 +516,7 @@
     sent = after(dsecond.astype(BF), ffn[0])
     dbr, dbr_first = square.gather(sent)
     up_part = weight_grad(first_after(n2, sent), dup)
-    up_owned = dp_scatter(after(up_part, gate_owned, dbr[1], dbr[3]))
+    up_owned = dp_scatter(after(up_part, gate_owned, *dbr_first))
 
     dproj, tap_part, conv_part = conv_backward(
         first_after(dbr, up_part), conv_w, taps, saved, places, tile
@@ -495,10 +525,10 @@
     far = back([dproj], [(conv_w, 0)], (1, 3), 512, n1)
     conv_part = weight_grad(first_after(n1, far[0], *came), dproj, conv_part)
     ffn, ffn_sends, _ = square.finish(ffn[2:], came)
-    near = back([after(dproj, conv_part, *ffn_sends)], [(conv_w, 0)], (0, 2), 512, n1)
+    near = back([after(dproj, conv_part, *ffn_sends)], [(conv_w, 0)], (0, 2), 512, n1, 150.0)
     first_came = square.begin(far[:2])
     dnormed, mid, last_came = square.finish(near[:2], first_came)
-    conv_owned = dp_scatter(after(conv_part, up_owned, *first_came))
+    conv_owned = dp_scatter(after(conv_part, up_owned))
     gain1_part = (far[2] + near[2])[0] / norm_gain1
     block_out = (second + ffn).astype(BF)
     dhidden_norm, _ = norm_back(hidden, scale1, norm_gain1, dnormed)
@@ -512,14 +542,13 @@
     )
     small = total_of(after(small, *first_came), "dp", ndp)
     small = total_of(after(small, *last_came), "tensor", nt)
-    in_owned = conv_owned[:, : 3 * chans].reshape(-1, chans // tile, 3, tile)
-    in_owned = in_owned.transpose(2, 0, 1, 3)
+    in_owned, out_owned = unpack(conv_owned, chans, tile)
     return (
         block_out[None],
         tokens_grad[None],
-        in_owned.reshape(3, -1, chans).astype(F32),
+        in_owned,
         small[2:5],
-        conv_owned[:, 3 * chans :].T.astype(F32),
+        out_owned,
         gate_owned.astype(F32),
         up_owned.astype(F32),
         down_owned.T.astype(F32),

time: 789 us -> 749 us (0.949)
  waiting for transfers between devices: 307 us -> 279 us
  local copies, waits for them, and re-layouts: 30.4 us -> 21.1 us
    ppermute x32, waiting for transfers between devices: 275 us -> 226 us  [flip(): return lax.ppermute(value, 'tensor', [(t, t ^ bit) for t in range(self.nt)])]
    all_gather x4, waiting for transfers between devices: 17.3 us -> 27.8 us  [local(): dp_gather = lambda v: lax.all_gather(v, 'dp', axis=0, tiled=True)]
    reduce_scatter x4, waiting for transfers between devices: 3.49 us -> 11.7 us  [local(): lax.psum_scatter(v, 'dp', scatter_dimension=0, tiled=True)]
    unnamed x92 -> x120, local copies, waits for them, and re-layouts: 17.8 us -> 11.5 us
    pallas_call x16 -> x17, Pallas kernels: 314 us -> 318 us  [call(): pl.pallas_call(body, grid_spec=pltpu.PrefetchScalarGridSpec(num_scalar_pr...]
  transfers between devices with their start and end apart: 45 -> 45, of which waited for: 25 -> 24; matrix products, arithmetic and copies ran while one was open for 10% -> 10% of each run, Pallas kernels for 40% -> 42%
where the time goes in v3:
time: 749 us; the launch traced here: 741 us
  Pallas kernels  318 us (42%)
  waiting for transfers between devices  279 us (37%)
  other arithmetic  62 us (8%)
  starting transfers between devices  46 us (6%)
  local copies, waits for them, and re-layouts  21.1 us (3%)
  between operations  15.4 us (2%)
    pallas_call x17, Pallas kernels, call(): pl.pallas_call(body, grid_spec=pltpu.PrefetchScalarGridSpec(num_scalar_pr...  318 us
    ppermute x32, waiting for transfers between devices, flip(): return lax.ppermute(value, 'tensor', [(t, t ^ bit) for t in range(self.nt)])  226 us
    ppermute x32, starting transfers between devices, flip(): return lax.ppermute(value, 'tensor', [(t, t ^ bit) for t in range(self.nt)])  42.9 us
    all_gather x4, waiting for transfers between devices, local(): dp_gather = lambda v: lax.all_gather(v, 'dp', axis=0, tiled=True)  27.8 us
    convert_element_type x7, other arithmetic, finish(): total([v[half:] for v in p]).astype(BF)  18.9 us
  transfers between devices with their start and end apart: 45, of which 24 were waited for; matrix products, arithmetic and copies ran while one was open for 10% of the time, Pallas kernels for 42%

profile of v3, /device:TPU:0, one launch (start us, length us, event | category | flops | bytes accessed | tf_op | source)
XLA Modules:
  0.0 740.8 jit_solution(9835036473306183139)
XLA Ops:
  17.4 20.5 %collective-permute-done.2 = bf16[256,2048]{1,0:T(8,128)(2,1)S(1)} collective-permute-done((bf16[256,2048]{1,0:T(8,128)(2,1)S(1)}, bf16[256,2048]{1,0:T(8,128)(2,1)S(1)}, u32[]{:S(2)}, u32[]{:S(2)}) %collective-permute-start.2) | collective-permute-done | bytes 1048608 | tf_op jit(solution)/shard_map/ppermute | solution.py:60
  41.8 43.5 %collective-permute-done.3.refs_3_.refs_4_ = bf16[512,2048]{1,0:T(8,128)(2,1)} collective-permute-done((bf16[512,2048]{1,0:T(8,128)(2,1)S(1)}, bf16[512,2048]{1,0:T(8,128)(2,1)}, u32[]{:S(2)}, u32[]{:S(2)}) %collective-permute-start.3) | collective-permute-done | bytes 2097184 | tf_op jit(solution)/shard_map/ppermute | solution.py:60
  86.7 8.3 %all-gather.5.cloned.1.call-done.refs_4_.refs_2_ = bf16[2048,2048]{1,0:T(8,128)(2,1)} async-done(((bf16[256,2048]{1,0:T(8,128)(2,1)}), bf16[2048,2048]{1,0:T(8,128)(2,1)}) %all-gather.5.cloned.1.call-update) | async-done | bytes 8388624 | tf_op jit(solution)/shard_map/all_gather | solution.py:474
  100.0 22.3 %conv_fwd.1 = (bf16[2048,512]{1,0:T(8,128)(2,1)}, bf16[2048,512]{1,0:T(8,128)(2,1)}, bf16[2048,512]{1,0:T(8,128)(2,1)}, bf16[2048,512]{1,0:T(8,128)(2,1)}) custom-call(s32[2,8]{1,0:T(2,128)} %dynamic-slice_bitcast_fusion.places, bf16[512,2048]{1,0:T(8,128)(2,1)} %copy-done.20, bf16[512,2048]{1,0:T(8,128)(2,1)} %collective-permute-done.1.refs_1_.refs_3_, ...), custom_call_target="tpu_custom_call" | custom-call | flops 2576980480 | bytes 5034393 | tf_op jit(solution)/shard_map/conv_fwd/pallas_call | solution.py:136
  122.3 5.2 back.7
  136.0 5.1 back.8
  141.1 33.8 %collective-permute-done.6 = bf16[512,2048]{1,0:T(8,128)(2,1)} collective-permute-done((bf16[512,2048]{1,0:T(8,128)(2,1)}, bf16[512,2048]{1,0:T(8,128)(2,1)}, u32[]{:S(2)}, u32[]{:S(2)}) %collective-permute-start.6) | collective-permute-done | bytes 2097184 | tf_op jit(solution)/shard_map/ppermute | solution.py:60
  181.6 21.5 %collective-permute-done.7 = bf16[256,2048]{1,0:T(8,128)(2,1)S(1)} collective-permute-done((bf16[256,2048]{1,0:T(8,128)(2,1)}, bf16[256,2048]{1,0:T(8,128)(2,1)S(1)}, u32[]{:S(2)}, u32[]{:S(2)}) %collective-permute-start.7) | collective-permute-done | bytes 1048608 | tf_op jit(solution)/shard_map/ppermute | solution.py:60
  213.2 19.8 %collective-permute-done.12 = bf16[256,2048]{1,0:T(8,128)(2,1)S(1)} collective-permute-done((bf16[256,2048]{1,0:T(8,128)(2,1)S(1)}, bf16[256,2048]{1,0:T(8,128)(2,1)S(1)}, u32[]{:S(2)}, u32[]{:S(2)}) %collective-permute-start.12) | collective-permute-done | bytes 1048608 | tf_op jit(solution)/shard_map/ppermute | solution.py:60
  240.0 19.5 %all-gather.9.cloned.1.call-done.refs_5_ = bf16[2048,2048]{1,0:T(8,128)(2,1)} async-done(((bf16[256,2048]{1,0:T(8,128)(2,1)}), bf16[2048,2048]{1,0:T(8,128)(2,1)}) %all-gather.9.cloned.1.call-update) | async-done | bytes 8388624 | tf_op jit(solution)/shard_map/all_gather | solution.py:474
  259.5 20.1 %collective-permute-done.13.refs_3_ = bf16[512,2048]{1,0:T(8,128)(2,1)} collective-permute-done((bf16[512,2048]{1,0:T(8,128)(2,1)S(1)}, bf16[512,2048]{1,0:T(8,128)(2,1)}, u32[]{:S(2)}, u32[]{:S(2)}) %collective-permute-start.13) | collective-permute-done | bytes 2097184 | tf_op jit(solution)/shard_map/ppermute | solution.py:60
  284.3 43.6 %ffn_gate.1 = (bf16[2048,2048]{1,0:T(8,128)(2,1)}, bf16[2048,2048]{1,0:T(8,128)(2,1)}, bf16[2048,2048]{1,0:T(8,128)(2,1)}) custom-call(bf16[512,2048]{1,0:T(8,128)(2,1)} %pad_maximum_fusion.3.refs_0_, bf16[512,2048]{1,0:T(8,128)(2,1)} %collective-permute-done.11.refs_1_, bf16[512,2048]{1,0:T(8,128)(2,1)} %copy-done.15, ...), custom_call_target="tpu_custom_call" | custom-call | flops 137438953472 | bytes 201326592 | tf_op jit(solution)/shard_map/ffn_gate/pallas_call | solution.py:136
  330.5 23.7 %weight_grad.4 = bf16[2048,2048]{1,0:T(8,128)(2,1)} custom-call(bf16[512,2048]{1,0:T(8,128)(2,1)} %constant_dynamic-update-slice_fusion.refs_0_, bf16[512,2048]{1,0:T(8,128)(2,1)} %copy-done.22, bf16[512,2048]{1,0:T(8,128)(2,1)} %constant_dynamic-update-slice_fusion.2.refs_2_, bf16[512,2048]{1,0:T(8,128)(2,1)} %copy-done.21, ...), custom_call_target="tpu_custom_call" | custom-call | flops 3435973888 | bytes 5033164 | tf_op jit(solution)/shard_map/weight_grad/pallas_call | solution.py:136
  354.8 28.0 %ffn_slope.1 = (bf16[2048,2048]{1,0:T(8,128)(2,1)}, bf16[2048,2048]{1,0:T(8,128)(2,1)}) custom-call(bf16[512,2048]{1,0:T(8,128)(2,1)} %constant_dynamic-update-slice_fusion.refs_0_, bf16[512,2048]{1,0:T(8,128)(2,1)} %copy-done.22, bf16[512,2048]{1,0:T(8,128)(2,1)} %constant_dynamic-update-slice_fusion.2.refs_2_, bf16[512,2048]{1,0:T(8,128)(2,1)} %copy-done.21, ...), custom_call_target="tpu_custom_call" | custom-call | flops 3435973888 | bytes 10066329 | tf_op jit(solution)/shard_map/ffn_slope/pallas_call | solution.py:136
  382.8 23.8 %back.9 = (bf16[512,2048]{1,0:T(8,128)(2,1)}, bf16[512,2048]{1,0:T(8,128)(2,1)}) custom-call(bf16[2048,2048]{1,0:T(8,128)(2,1)} %get-tuple-element.100.refs_0_.refs_2_.refs_4_, bf16[2048,2048]{1,0:T(8,128)(2,1)} %get-tuple-element.98.refs_1_.refs_3_.refs_4_, bf16[2048,2048]{1,0:T(8,128)(2,1)} %get-tuple-element.100.refs_0_.refs_2_.refs_4_, ...), custom_call_target="tpu_custom_call" | custom-call | flops 3435973888 | bytes 10905190 | tf_op jit(solution)/shard_map/back/pallas_call | solution.py:136
  408.7 23.8 %back.10 = (bf16[512,2048]{1,0:T(8,128)(2,1)}, bf16[512,2048]{1,0:T(8,128)(2,1)}) custom-call(bf16[2048,2048]{1,0:T(8,128)(2,1)} %get-tuple-element.100.refs_0_.refs_2_.refs_4_, bf16[2048,2048]{1,0:T(8,128)(2,1)} %get-tuple-element.98.refs_1_.refs_3_.refs_4_, bf16[2048,2048]{1,0:T(8,128)(2,1)} %get-tuple-element.100.refs_0_.refs_2_.refs_4_, ...), custom_call_target="tpu_custom_call" | custom-call | flops 3435973888 | bytes 10905190 | tf_op jit(solution)/shard_map/back/pallas_call | solution.py:136
  432.5 23.8 %weight_grad.5 = bf16[2048,2048]{1,0:T(8,128)(2,1)} custom-call(bf16[512,2048]{1,0:T(8,128)(2,1)} %pad_maximum_fusion.3.refs_0_, bf16[512,2048]{1,0:T(8,128)(2,1)} %collective-permute-done.11.refs_1_, bf16[512,2048]{1,0:T(8,128)(2,1)} %copy-done.15, bf16[512,2048]{1,0:T(8,128)(2,1)} %collective-permute-done.13.refs_3_, ...), custom_call_target="tpu_custom_call" | custom-call | flops 3435973888 | bytes 5033164 | tf_op jit(solution)/shard_map/weight_grad/pallas_call | solution.py:136
  462.0 24.1 %back.11 = (bf16[512,2048]{1,0:T(8,128)(2,1)}, bf16[512,2048]{1,0:T(8,128)(2,1)}, bf16[512,2048]{1,0:T(8,128)(2,1)}, bf16[512,2048]{1,0:T(8,128)(2,1)}) custom-call(bf16[2048,2048]{1,0:T(8,128)(2,1)} %get-tuple-element.107.refs_4_.refs_0_.refs_1_.refs_2_.refs_3_, bf16[2048,2048]{1,0:T(8,128)(2,1)} %get-tuple-element.107.refs_4_.refs_0_.refs_1_.refs_2_.refs_3_, ...), custom_call_target="tpu_custom_call" | custom-call | flops 3435973888 | bytes 10066329 | tf_op jit(solution)/shard_map/back/pallas_call | solution.py:136
  500.2 18.0 %collective-permute-done.22 = bf16[256,2048]{1,0:T(8,128)(2,1)S(1)} collective-permute-done((bf16[256,2048]{1,0:T(8,128)(2,1)S(1)}, bf16[256,2048]{1,0:T(8,128)(2,1)S(1)}, u32[]{:S(2)}, u32[]{:S(2)}) %collective-permute-start.22) | collective-permute-done | bytes 1048608 | tf_op jit(solution)/shard_map/ppermute | solution.py:60
  525.6 23.8 %weight_grad.6 = bf16[2048,2048]{1,0:T(8,128)(2,1)} custom-call(bf16[512,2048]{1,0:T(8,128)(2,1)} %pad_maximum_fusion.3.refs_0_, bf16[512,2048]{1,0:T(8,128)(2,1)} %collective-permute-done.11.refs_1_, bf16[512,2048]{1,0:T(8,128)(2,1)} %copy-done.15, bf16[512,2048]{1,0:T(8,128)(2,1)} %collective-permute-done.13.refs_3_, ...), custom_call_target="tpu_custom_call" | custom-call | flops 3435973888 | bytes 5033164 | tf_op jit(solution)/shard_map/weight_grad/pallas_call | solution.py:136
  549.5 14.3 %collective-permute-done.23.refs_3_ = bf16[512,2048]{1,0:T(8,128)(2,1)} collective-permute-done((bf16[512,2048]{1,0:T(8,128)(2,1)S(1)}, bf16[512,2048]{1,0:T(8,128)(2,1)}, u32[]{:S(2)}, u32[]{:S(2)}) %collective-permute-start.23) | collective-permute-done | bytes 2097184 | tf_op jit(solution)/shard_map/ppermute | solution.py:60
  567.8 23.2 %conv_bwd.1 = (bf16[2048,1536]{1,0:T(8,128)(2,1)}, f32[3,512]{1,0:T(4,128)}, bf16[2048,2048]{1,0:T(8,128)(2,1)}) custom-call(s32[2,8]{1,0:T(2,128)} %dynamic-slice_bitcast_fusion.places, bf16[512,2048]{1,0:T(8,128)(2,1)} %pad_maximum_fusion.5.refs_0_, bf16[512,2048]{1,0:T(8,128)(2,1)} %collective-permute-done.21.refs_1_, bf16[512,2048]{1,0:T(8,128)(2,1)} %copy-done.32, ...), custom_call_target="tpu_custom_call" | custom-call | flops 151182852096 | bytes 701503872 | tf_op jit(solution)/shard_map/conv_bwd/pallas_call | solution.py:136
  591.0 11.2 %back.12 = (bf16[512,2048]{1,0:T(8,128)(2,1)}, bf16[512,2048]{1,0:T(8,128)(2,1)}, f32[1,2048]{1,0:T(1,128)}) custom-call(bf16[2048,1536]{1,0:T(8,128)(2,1)} %get-tuple-element.124.refs_0_.refs_1_.refs_4_, bf16[2048,1536]{1,0:T(8,128)(2,1)} %get-tuple-element.124.refs_0_.refs_1_.refs_4_, bf16[2048,2048]{1,0:T(8,128)(2,1)} %all-gather.5.cloned.1.call-done.refs_4_.refs_2_, ...), custom_call_target="tpu_custom_call" | custom-call | flops 1288490240 | bytes 5873664 | tf_op jit(solution)/shard_map/back/pallas_call | solution.py:136
  602.4 10.2 %collective-permute-done.24 = bf16[512,2048]{1,0:T(8,128)(2,1)} collective-permute-done((bf16[512,2048]{1,0:T(8,128)(2,1)}, bf16[512,2048]{1,0:T(8,128)(2,1)}, u32[]{:S(2)}, u32[]{:S(2)}) %collective-permute-start.24) | collective-permute-done | bytes 2097184 | tf_op jit(solution)/shard_map/ppermute | solution.py:60
  614.6 19.4 %weight_grad.7 = bf16[2048,2048]{1,0:T(8,128)(2,1)} custom-call(bf16[512,2048]{1,0:T(8,128)(2,1)} %copy-done.20, bf16[512,2048]{1,0:T(8,128)(2,1)} %collective-permute-done.1.refs_1_.refs_3_, bf16[512,2048]{1,0:T(8,128)(2,1)} %copy-done.19, bf16[512,2048]{1,0:T(8,128)(2,1)} %collective-permute-done.3.refs_3_.refs_4_, ...), custom_call_target="tpu_custom_call", output_to_operand_aliasing={{}: (5, {})} | custom-call | flops 2576980480 | bytes 6291456 | tf_op jit(solution)/shard_map/weight_grad/pallas_call | solution.py:136
  639.8 11.2 %back.13 = (bf16[512,2048]{1,0:T(8,128)(2,1)}, bf16[512,2048]{1,0:T(8,128)(2,1)}, f32[1,2048]{1,0:T(1,128)}) custom-call(bf16[2048,1536]{1,0:T(8,128)(2,1)} %get-tuple-element.124.refs_0_.refs_1_.refs_4_, bf16[2048,1536]{1,0:T(8,128)(2,1)} %get-tuple-element.124.refs_0_.refs_1_.refs_4_, bf16[2048,2048]{1,0:T(8,128)(2,1)} %all-gather.5.cloned.1.call-done.refs_4_.refs_2_, ...), custom_call_target="tpu_custom_call" | custom-call | flops 193273528320 | bytes 881049600 | tf_op jit(solution)/shard_map/back/pallas_call | solution.py:136
  661.2 6.2 collective-permute-done.33
  671.7 4.9 collective-permute-done.34
  678.0 7.1 collective-permute-done.31
  689.9 8.2 %collective-permute-done.25 = bf16[256,2048]{1,0:T(8,128)(2,1)S(1)} collective-permute-done((bf16[256,2048]{1,0:T(8,128)(2,1)}, bf16[256,2048]{1,0:T(8,128)(2,1)S(1)}, u32[]{:S(2)}, u32[]{:S(2)}) %collective-permute-start.25) | collective-permute-done | bytes 1048608 | tf_op jit(solution)/shard_map/ppermute | solution.py:60
  703.0 5.6 fusion.6
  719.1 11.7 %reduce-scatter.11.cloned.1.call-done.src = bf16[256,2048]{1,0:T(8,128)(2,1)} async-done(((bf16[2048,2048]{1,0:T(8,128)(2,1)}), bf16[256,2048]{1,0:T(8,128)(2,1)}) %reduce-scatter.11.cloned.1.call-update) | async-done | bytes 1048592 | tf_op jit(solution)/shard_map/reduce_scatter | solution.py:475
  (261 shorter events, 139.8 us)
Async XLA Ops:
  7.2 87.8 %all-gather.5.cloned.1.call-start = ((), (), s32[]{:S(2)}) async-start(), calls=%async_computation.4 | async-start | bytes 9437184 | tf_op jit(solution)/shard_map/all_gather | solution.py:474
  9.7 169.2 %all-gather.7.cloned.1.call-start = ((), (), s32[]{:S(2)}) async-start(), calls=%async_computation.5 | async-start | bytes 9437184 | tf_op jit(solution)/shard_map/all_gather | solution.py:474
  11.7 26.2 %collective-permute-start.2 = (bf16[256,2048]{1,0:T(8,128)(2,1)S(1)}, bf16[256,2048]{1,0:T(8,128)(2,1)S(1)}, u32[]{:S(2)}, u32[]{:S(2)}) collective-permute-start(bf16[256,2048]{1,0:T(8,128)(2,1)S(1)} %get-tuple-element.154), channel_id=1, source_target_pairs={{0,2},{1,3},{2,0},{3,1},{4,6},{5,7},{6,4},{7,5},{8,10},{9,11},{10,... | collective-permute-start | bytes 3145736 | tf_op jit(solution)/shard_map/ppermute | solution.py:60
  38.2 47.1 %collective-permute-start.3 = (bf16[512,2048]{1,0:T(8,128)(2,1)S(1)}, bf16[512,2048]{1,0:T(8,128)(2,1)}, u32[]{:S(2)}, u32[]{:S(2)}) collective-permute-start(bf16[512,2048]{1,0:T(8,128)(2,1)S(1)} %pad_maximum_fusion.2.refs_2_.refs_4_), channel_id=1, source_target_pairs={{0,1},{1,0},{2,3},{3,2},{4,5},{5,4},{6,7},{7,6},{8,9},{9,8},{10,11... | collective-permute-start | bytes 6291464 | tf_op jit(solution)/shard_map/ppermute | solution.py:60
  40.2 46.5 %collective-permute-start.1 = (bf16[512,2048]{1,0:T(8,128)(2,1)S(1)}, bf16[512,2048]{1,0:T(8,128)(2,1)}, u32[]{:S(2)}, u32[]{:S(2)}) collective-permute-start(bf16[512,2048]{1,0:T(8,128)(2,1)S(1)} %pad_maximum_fusion.1.refs_0_.refs_3_), channel_id=1, source_target_pairs={{0,2},{1,3},{2,0},{3,1},{4,6},{5,7},{6,4},{7,5},{8,10},{9,11},{10,... | collective-permute-start | bytes 6291464 | tf_op jit(solution)/shard_map/ppermute | solution.py:60
  95.0 164.4 %all-gather.9.cloned.1.call-start = ((), (), s32[]{:S(2)}) async-start(), calls=%async_computation.6 | async-start | bytes 9437184 | tf_op jit(solution)/shard_map/all_gather | solution.py:474
  95.1 27.2 %collective-permute-start.5 = (bf16[256,2048]{1,0:T(8,128)(2,1)}, bf16[256,2048]{1,0:T(8,128)(2,1)}, u32[]{:S(2)}, u32[]{:S(2)}) collective-permute-start(bf16[256,2048]{1,0:T(8,128)(2,1)} %get-tuple-element.78), channel_id=1, source_target_pairs={{0,2},{1,3},{2,0},{3,1},{4,6},{5,7},{6,4},{7,5},{8,10},{9,11},{10,... | collective-permute-start | bytes 3145736 | tf_op jit(solution)/shard_map/ppermute | solution.py:60
  96.7 25.7 %collective-permute-start.4 = (bf16[256,2048]{1,0:T(8,128)(2,1)S(1)}, bf16[256,2048]{1,0:T(8,128)(2,1)}, u32[]{:S(2)}, u32[]{:S(2)}) collective-permute-start(bf16[256,2048]{1,0:T(8,128)(2,1)S(1)} %get-tuple-element.77), channel_id=1, source_target_pairs={{0,1},{1,0},{2,3},{3,2},{4,5},{5,4},{6,7},{7,6},{8,9},{9,8},{10,11... | collective-permute-start | bytes 3145736 | tf_op jit(solution)/shard_map/ppermute | solution.py:60
  127.6 47.3 %collective-permute-start.6 = (bf16[512,2048]{1,0:T(8,128)(2,1)}, bf16[512,2048]{1,0:T(8,128)(2,1)}, u32[]{:S(2)}, u32[]{:S(2)}) collective-permute-start(bf16[512,2048]{1,0:T(8,128)(2,1)} %get-tuple-element.80), channel_id=1, source_target_pairs={{0,2},{1,3},{2,0},{3,1},{4,6},{5,7},{6,4},{7,5},{8,10},{9,11},{10,... | collective-permute-start | bytes 6291464 | tf_op jit(solution)/shard_map/ppermute | solution.py:60
  127.6 47.3 %collective-permute-start.8 = (bf16[512,2048]{1,0:T(8,128)(2,1)}, bf16[512,2048]{1,0:T(8,128)(2,1)}, u32[]{:S(2)}, u32[]{:S(2)}) collective-permute-start(bf16[512,2048]{1,0:T(8,128)(2,1)} %get-tuple-element.85), channel_id=1, source_target_pairs={{0,1},{1,0},{2,3},{3,2},{4,5},{5,4},{6,7},{7,6},{8,9},{9,8},{10,11... | collective-permute-start | bytes 6291464 | tf_op jit(solution)/shard_map/ppermute | solution.py:60
  178.9 175.9 %all-gather.11.cloned.1.call-start = ((), (), s32[]{:S(2)}) async-start(), calls=%async_computation.7 | async-start | bytes 9437184 | tf_op jit(solution)/shard_map/all_gather | solution.py:474
  233.1 46.6 %collective-permute-start.13 = (bf16[512,2048]{1,0:T(8,128)(2,1)S(1)}, bf16[512,2048]{1,0:T(8,128)(2,1)}, u32[]{:S(2)}, u32[]{:S(2)}) collective-permute-start(bf16[512,2048]{1,0:T(8,128)(2,1)S(1)} %pad_maximum_fusion.4.refs_2_), channel_id=1, source_target_pairs={{0,1},{1,0},{2,3},{3,2},{4,5},{5,4},{6,7},{7,6},{8,9},{9,8},{10,11... | collective-permute-start | bytes 6291464 | tf_op jit(solution)/shard_map/ppermute | solution.py:60
  237.5 44.6 %collective-permute-start.11 = (bf16[512,2048]{1,0:T(8,128)(2,1)}, bf16[512,2048]{1,0:T(8,128)(2,1)}, u32[]{:S(2)}, u32[]{:S(2)}) collective-permute-start(bf16[512,2048]{1,0:T(8,128)(2,1)} %pad_maximum_fusion.3.refs_0_), channel_id=1, source_target_pairs={{0,2},{1,3},{2,0},{3,1},{4,6},{5,7},{6,4},{7,5},{8,10},{9,11},{10,... | collective-permute-start | bytes 6291464 | tf_op jit(solution)/shard_map/ppermute | solution.py:60
  259.5 200.4 %reduce-scatter.5.cloned.1.call-start = ((), (), s32[]{:S(2)}) async-start(), calls=%async_computation.8 | async-start | bytes 9437184 | tf_op jit(solution)/shard_map/reduce_scatter | solution.py:475
  282.1 45.8 %collective-permute-start.15 = (bf16[512,2048]{1,0:T(8,128)(2,1)}, bf16[512,2048]{1,0:T(8,128)(2,1)S(1)}, u32[]{:S(2)}, u32[]{:S(2)}) collective-permute-start(bf16[512,2048]{1,0:T(8,128)(2,1)} %constant_dynamic-update-slice_fusion.2.refs_2_), channel_id=1, source_target_pairs={{0,1},{1,0},{2,3},{3,2},{4,5},{5,4},{6,7},{7,6},{8,9},{9,8},{10,11... | collective-permute-start | bytes 6291464 | tf_op jit(solution)/shard_map/ppermute | solution.py:60
  283.3 44.6 %collective-permute-start.14 = (bf16[512,2048]{1,0:T(8,128)(2,1)}, bf16[512,2048]{1,0:T(8,128)(2,1)S(1)}, u32[]{:S(2)}, u32[]{:S(2)}) collective-permute-start(bf16[512,2048]{1,0:T(8,128)(2,1)} %constant_dynamic-update-slice_fusion.refs_0_), channel_id=1, source_target_pairs={{0,2},{1,3},{2,0},{3,1},{4,6},{5,7},{6,4},{7,5},{8,10},{9,11},{10,... | collective-permute-start | bytes 6291464 | tf_op jit(solution)/shard_map/ppermute | solution.py:60
  354.3 195.1 %reduce-scatter.7.cloned.1.call-start = ((), (), s32[]{:S(2)}) async-start(), calls=%async_computation.9 | async-start | bytes 9437184 | tf_op jit(solution)/shard_map/reduce_scatter | solution.py:475
  406.6 49.8 %collective-permute-start.16 = (bf16[512,2048]{1,0:T(8,128)(2,1)}, bf16[512,2048]{1,0:T(8,128)(2,1)}, u32[]{:S(2)}, u32[]{:S(2)}) collective-permute-start(bf16[512,2048]{1,0:T(8,128)(2,1)} %get-tuple-element.99), channel_id=1, source_target_pairs={{0,2},{1,3},{2,0},{3,1},{4,6},{5,7},{6,4},{7,5},{8,10},{9,11},{10,... | collective-permute-start | bytes 6291464 | tf_op jit(solution)/shard_map/ppermute | solution.py:60
  407.6 51.8 %collective-permute-start.17 = (bf16[512,2048]{1,0:T(8,128)(2,1)}, bf16[512,2048]{1,0:T(8,128)(2,1)S(1)}, u32[]{:S(2)}, u32[]{:S(2)}) collective-permute-start(bf16[512,2048]{1,0:T(8,128)(2,1)} %get-tuple-element.105), channel_id=1, source_target_pairs={{0,1},{1,0},{2,3},{3,2},{4,5},{5,4},{6,7},{7,6},{8,9},{9,8},{10,11... | collective-permute-start | bytes 6291464 | tf_op jit(solution)/shard_map/ppermute | solution.py:60
  459.9 179.9 %reduce-scatter.9.cloned.1.call-start = ((), (), s32[]{:S(2)}) async-start(), calls=%async_computation.10 | async-start | bytes 9437184 | tf_op jit(solution)/shard_map/reduce_scatter | solution.py:475
  459.9 26.1 %collective-permute-start.18 = (bf16[256,2048]{1,0:T(8,128)(2,1)}, bf16[256,2048]{1,0:T(8,128)(2,1)}, u32[]{:S(2)}, u32[]{:S(2)}) collective-permute-start(bf16[256,2048]{1,0:T(8,128)(2,1)} %add_convert_fusion.5), channel_id=1, source_target_pairs={{0,1},{1,0},{2,3},{3,2},{4,5},{5,4},{6,7},{7,6},{8,9},{9,8},{10,11... | collective-permute-start | bytes 3145736 | tf_op jit(solution)/shard_map/ppermute | solution.py:60
  460.9 27.4 %collective-permute-start.19 = (bf16[256,2048]{1,0:T(8,128)(2,1)S(1)}, bf16[256,2048]{1,0:T(8,128)(2,1)}, u32[]{:S(2)}, u32[]{:S(2)}) collective-permute-start(bf16[256,2048]{1,0:T(8,128)(2,1)S(1)} %add_convert_fusion.4), channel_id=1, source_target_pairs={{0,2},{1,3},{2,0},{3,1},{4,6},{5,7},{6,4},{7,5},{8,10},{9,11},{10,... | collective-permute-start | bytes 3145736 | tf_op jit(solution)/shard_map/ppermute | solution.py:60
  518.4 45.4 %collective-permute-start.23 = (bf16[512,2048]{1,0:T(8,128)(2,1)S(1)}, bf16[512,2048]{1,0:T(8,128)(2,1)}, u32[]{:S(2)}, u32[]{:S(2)}) collective-permute-start(bf16[512,2048]{1,0:T(8,128)(2,1)S(1)} %pad_maximum_fusion.6.refs_2_), channel_id=1, source_target_pairs={{0,1},{1,0},{2,3},{3,2},{4,5},{5,4},{6,7},{7,6},{8,9},{9,8},{10,11... | collective-permute-start | bytes 6291464 | tf_op jit(solution)/shard_map/ppermute | solution.py:60
  523.7 40.0 %collective-permute-start.21 = (bf16[512,2048]{1,0:T(8,128)(2,1)}, bf16[512,2048]{1,0:T(8,128)(2,1)}, u32[]{:S(2)}, u32[]{:S(2)}) collective-permute-start(bf16[512,2048]{1,0:T(8,128)(2,1)} %pad_maximum_fusion.5.refs_0_), channel_id=1, source_target_pairs={{0,2},{1,3},{2,0},{3,1},{4,6},{5,7},{6,4},{7,5},{8,10},{9,11},{10,... | collective-permute-start | bytes 6291464 | tf_op jit(solution)/shard_map/ppermute | solution.py:60
  549.5 181.3 %reduce-scatter.11.cloned.1.call-start = ((), (), s32[]{:S(2)}) async-start(), calls=%async_computation.11 | async-start | bytes 9437184 | tf_op jit(solution)/shard_map/reduce_scatter | solution.py:475
  563.8 48.9 %collective-permute-start.24 = (bf16[512,2048]{1,0:T(8,128)(2,1)}, bf16[512,2048]{1,0:T(8,128)(2,1)}, u32[]{:S(2)}, u32[]{:S(2)}) collective-permute-start(bf16[512,2048]{1,0:T(8,128)(2,1)} %get-tuple-element.111), channel_id=1, source_target_pairs={{0,2},{1,3},{2,0},{3,1},{4,6},{5,7},{6,4},{7,5},{8,10},{9,11},{10,... | collective-permute-start | bytes 6291464 | tf_op jit(solution)/shard_map/ppermute | solution.py:60
  565.5 49.2 %collective-permute-start.26 = (bf16[512,2048]{1,0:T(8,128)(2,1)}, bf16[512,2048]{1,0:T(8,128)(2,1)}, u32[]{:S(2)}, u32[]{:S(2)}) collective-permute-start(bf16[512,2048]{1,0:T(8,128)(2,1)} %get-tuple-element.114), channel_id=1, source_target_pairs={{0,1},{1,0},{2,3},{3,2},{4,5},{5,4},{6,7},{7,6},{8,9},{9,8},{10,11... | collective-permute-start | bytes 6291464 | tf_op jit(solution)/shard_map/ppermute | solution.py:60
  602.2 48.8 %collective-permute-start.28 = (bf16[512,2048]{1,0:T(8,128)(2,1)}, bf16[512,2048]{1,0:T(8,128)(2,1)}, u32[]{:S(2)}, u32[]{:S(2)}) collective-permute-start(bf16[512,2048]{1,0:T(8,128)(2,1)} %get-tuple-element.121), channel_id=1, source_target_pairs={{0,2},{1,3},{2,0},{3,1},{4,6},{5,7},{6,4},{7,5},{8,10},{9,11},{10,... | collective-permute-start | bytes 6291464 | tf_op jit(solution)/shard_map/ppermute | solution.py:60
  602.3 53.8 %collective-permute-start.30 = (bf16[512,2048]{1,0:T(8,128)(2,1)}, bf16[512,2048]{1,0:T(8,128)(2,1)}, u32[]{:S(2)}, u32[]{:S(2)}) collective-permute-start(bf16[512,2048]{1,0:T(8,128)(2,1)} %get-tuple-element.127), channel_id=1, source_target_pairs={{0,1},{1,0},{2,3},{3,2},{4,5},{5,4},{6,7},{7,6},{8,9},{9,8},{10,11... | collective-permute-start | bytes 6291464 | tf_op jit(solution)/shard_map/ppermute | solution.py:60
  658.7 26.4 %collective-permute-start.31 = (bf16[256,2048]{1,0:T(8,128)(2,1)}, bf16[256,2048]{1,0:T(8,128)(2,1)}, u32[]{:S(2)}, u32[]{:S(2)}) collective-permute-start(bf16[256,2048]{1,0:T(8,128)(2,1)} %add_convert_fusion), channel_id=1, source_target_pairs={{0,2},{1,3},{2,0},{3,1},{4,6},{5,7},{6,4},{7,5},{8,10},{9,11},{10,... | collective-permute-start | bytes 3145736 | tf_op jit(solution)/shard_map/ppermute | solution.py:60
  670.0 28.2 %collective-permute-start.25 = (bf16[256,2048]{1,0:T(8,128)(2,1)}, bf16[256,2048]{1,0:T(8,128)(2,1)S(1)}, u32[]{:S(2)}, u32[]{:S(2)}) collective-permute-start(bf16[256,2048]{1,0:T(8,128)(2,1)} %add_convert_fusion.3), channel_id=1, source_target_pairs={{0,1},{1,0},{2,3},{3,2},{4,5},{5,4},{6,7},{7,6},{8,9},{9,8},{10,11... | collective-permute-start | bytes 3145736 | tf_op jit(solution)/shard_map/ppermute | solution.py:60
  670.3 38.3 %collective-permute-start.27 = (bf16[256,2048]{1,0:T(8,128)(2,1)S(1)}, bf16[256,2048]{1,0:T(8,128)(2,1)S(1)}, u32[]{:S(2)}, u32[]{:S(2)}) collective-permute-start(bf16[256,2048]{1,0:T(8,128)(2,1)S(1)} %copy-done.37), channel_id=1, source_target_pairs={{0,2},{1,3},{2,0},{3,1},{4,6},{5,7},{6,4},{7,5},{8,10},{9,11},{10,... | collective-permute-start | bytes 3145736 | tf_op jit(solution)/shard_map/ppermute | solution.py:60
  (71 other events, 662.3 us)
Sparse Core Ops, SparseCore 0:
  10.2 84.7 all-gather.4
  96.6 80.5 all-gather.6
  179.1 80.3 all-gather.8
  261.5 80.5 all-gather.10
  354.4 87.5 reduce-scatter.4
  460.0 87.3 reduce-scatter.6
  549.7 87.9 reduce-scatter.8
  640.0 90.7 reduce-scatter.10

commit v4 on v3

--- a/solution.py
+++ b/solution.py
@@ -214,32 +214,37 @@
 
 
 def gate_body(*refs):
-    pieces, (gw, uw, act, silu, slope) = refs[:4], refs[4:]
-    rows = pieces[0].shape[0]
-    for i in range(4):
-        at = pl.ds(i * rows, rows)
-        gate = dot(pieces[i][...], gw[...], NN)
-        up = dot(pieces[i][...], uw[...], NN)
-        sig = jax.nn.sigmoid(gate)
-        s = gate * sig
-        act[at] = (s * up).astype(BF)
-        silu[at] = s.astype(BF)
-        slope[at] = (up * sig * (1.0 + gate * (1.0 - sig))).astype(BF)
-
-
-def ffn_gate(pieces, gate, up):
-    dim, width = gate.shape
-    tokens = 4 * pieces[0].shape[0]
+    pieces, (gw, uw) = refs[:2], refs[2:4]
+    act, silu, slope = refs[-3:]
+    for i in range(2):
+
+        @pl.when(pl.program_id(0) % 2 == i)
+        def _():
+            gate = dot(pieces[i][...], gw[...], NN)
+            up = dot(pieces[i][...], uw[...], NN)
+            sig = jax.nn.sigmoid(gate)
+            s = gate * sig
+            act[...] = (s * up).astype(BF)
+            silu[...] = s.astype(BF)
+            slope[...] = (up * sig * (1.0 + gate * (1.0 - sig))).astype(BF)
+
+
+def ffn_gate(pieces, gate, up, first, weight, into=()):
+    rows, dim = pieces[0].shape
+    width = gate.shape[1]
     tile = min(256, width)
+    wspec = ((dim, tile), lambda j: (0, j // 2))
+    out = ((rows, tile), lambda j: (first + 2 * (j % 2), j // 2), (4 * rows, width), BF)
     return call(
         "ffn_gate",
         gate_body,
-        width // tile,
-        [whole(p) for p in pieces] + [columns(gate, tile), columns(up, tile)],
-        [new_columns(tokens, width, tile)] * 3,
-        [*pieces, gate, up],
-        4 * tokens * dim * width,
-        weight=20.0,
+        2 * width // tile,
+        [whole(p) for p in pieces] + [wspec, wspec] + [None] * len(into),
+        [out] * 3,
+        [*pieces, gate, up, *into],
+        8 * rows * dim * width,
+        aliases={4 + i: i for i in range(len(into))},
+        weight=weight,
     )
 
 
@@ -275,6 +280,33 @@
         term = dot(left[i][:, columns], b[i * rows : (i + 1) * rows], TN)
         total = term if total is None else total + term
     return total.astype(BF)
+
+
+def part_grad(pieces, b, which, prior=()):
+    rows, dim = pieces[0].shape
+    width = b.shape[1]
+    tile = next(t for t in (512, 384, 256) if width % t == 0)
+    step = min(512, dim)
+
+    def body(*refs):
+        for d in range(0, dim, step):
+            total = None
+            for ref, p in zip(refs[:2], which):
+                term = dot(ref[:, d : d + step], refs[2][p * rows : (p + 1) * rows], TN)
+                total = term if total is None else total + term
+            if prior:
+                total = total + refs[3][d : d + step].astype(F32)
+            refs[-1][d : d + step] = total.astype(BF)
+
+    return call(
+        "part_grad",
+        body,
+        width // tile,
+        [whole(p) for p in pieces] + [columns(v, tile) for v in (b, *prior)],
+        [new_columns(dim, width, tile)],
+        [*pieces, b, *prior],
+        4 * rows * dim * width,
+    )[0]
 
 
 def weight_grad(pieces, b, into=None):
@@ -496,12 +528,14 @@
     scale2 = rms_scale(second)
     n2, n2_first = square.gather((second * scale2 * norm_gain2).astype(BF))
     down_w = dp_gather(after(down_shard, up_w, *n2_first))
+    gated = ffn_gate([n2[0], n2[2]], gate_w, up_w, 0, 1.0)
     while g_first:
-        g_two, g_first = g_gather.send((n2[1], n2[3]))
+        g_two, g_first = g_gather.send((n2[1], n2[3], gated[0]))
     g = g_two
 
-    act, silu, slope = ffn_gate(n2, gate_w, up_w)
-    down_part = weight_grad(first_after(g, act), act)
+    act, silu, slope = ffn_gate([n2[1], n2[3]], gate_w, up_w, 1, 40.0, gated)
+    down_part = part_grad([g[0], g[2]], act, (0, 2))
+    down_part = part_grad([g[1], g[3]], act, (1, 3), [down_part])
     down_owned = dp_scatter(down_part)
     dgate, dup = ffn_slope(first_after(g, down_part), down_w, silu, slope)
     pair = [(gate_w, 0), (up_w, 0)]

time: 749 us -> 760 us (1.015)
  Pallas kernels: 318 us -> 337 us
  waiting for transfers between devices: 279 us -> 265 us
  starting transfers between devices: 46 us -> 55.8 us
    pallas_call x17 -> x19, Pallas kernels: 318 us -> 337 us  [call(): pl.pallas_call(body, grid_spec=pltpu.PrefetchScalarGridSpec(num_scalar_pr...]
    ppermute x32, waiting for transfers between devices: 226 us -> 216 us  [flip(): return lax.ppermute(value, 'tensor', [(t, t ^ bit) for t in range(self.nt)])]
    reduce_scatter x4, starting transfers between devices: 0.56 us -> 10 us  [local(): lax.psum_scatter(v, 'dp', scatter_dimension=0, tiled=True)]
  transfers between devices with their start and end apart: 45 -> 45, of which waited for: 24 -> 26; matrix products, arithmetic and copies ran while one was open for 10% -> 10% of each run, Pallas kernels for 42% -> 44%
where the time goes in v4:
time: 760 us; the launch traced here: 755 us
  Pallas kernels  337 us (44%)
  waiting for transfers between devices  265 us (35%)
  other arithmetic  61.7 us (8%)
  starting transfers between devices  55.8 us (7%)
  local copies, waits for them, and re-layouts  19.9 us (3%)
  between operations  15.2 us (2%)
    pallas_call x19, Pallas kernels, call(): pl.pallas_call(body, grid_spec=pltpu.PrefetchScalarGridSpec(num_scalar_pr...  337 us
    ppermute x32, waiting for transfers between devices, flip(): return lax.ppermute(value, 'tensor', [(t, t ^ bit) for t in range(self.nt)])  216 us
    ppermute x32, starting transfers between devices, flip(): return lax.ppermute(value, 'tensor', [(t, t ^ bit) for t in range(self.nt)])  41.9 us
    all_gather x4, waiting for transfers between devices, local(): dp_gather = lambda v: lax.all_gather(v, 'dp', axis=0, tiled=True)  27.5 us
    convert_element_type x7, other arithmetic, finish(): total([v[half:] for v in p]).astype(BF)  18.7 us
  transfers between devices with their start and end apart: 45, of which 26 were waited for; matrix products, arithmetic and copies ran while one was open for 10% of the time, Pallas kernels for 44%

profile of v4, /device:TPU:0, one launch (start us, length us, event | category | flops | bytes accessed | tf_op | source)
XLA Modules:
  0.0 754.7 jit_solution(6954456996436727424)
XLA Ops:
  17.4 20.5 %collective-permute-done.2 = bf16[256,2048]{1,0:T(8,128)(2,1)S(1)} collective-permute-done((bf16[256,2048]{1,0:T(8,128)(2,1)S(1)}, bf16[256,2048]{1,0:T(8,128)(2,1)S(1)}, u32[]{:S(2)}, u32[]{:S(2)}) %collective-permute-start.2) | collective-permute-done | bytes 1048608 | tf_op jit(solution)/shard_map/ppermute | solution.py:60
  41.8 43.5 %collective-permute-done.3.refs_3_.refs_4_ = bf16[512,2048]{1,0:T(8,128)(2,1)} collective-permute-done((bf16[512,2048]{1,0:T(8,128)(2,1)S(1)}, bf16[512,2048]{1,0:T(8,128)(2,1)}, u32[]{:S(2)}, u32[]{:S(2)}) %collective-permute-start.3) | collective-permute-done | bytes 2097184 | tf_op jit(solution)/shard_map/ppermute | solution.py:60
  86.7 8.3 %all-gather.5.cloned.1.call-done.refs_4_.refs_2_ = bf16[2048,2048]{1,0:T(8,128)(2,1)} async-done(((bf16[256,2048]{1,0:T(8,128)(2,1)}), bf16[2048,2048]{1,0:T(8,128)(2,1)}) %all-gather.5.cloned.1.call-update) | async-done | bytes 8388624 | tf_op jit(solution)/shard_map/all_gather | solution.py:506
  100.0 22.3 %conv_fwd.1 = (bf16[2048,512]{1,0:T(8,128)(2,1)}, bf16[2048,512]{1,0:T(8,128)(2,1)}, bf16[2048,512]{1,0:T(8,128)(2,1)}, bf16[2048,512]{1,0:T(8,128)(2,1)}) custom-call(s32[2,8]{1,0:T(2,128)} %dynamic-slice_bitcast_fusion.places, bf16[512,2048]{1,0:T(8,128)(2,1)} %copy-done.20, bf16[512,2048]{1,0:T(8,128)(2,1)} %collective-permute-done.1.refs_1_.refs_3_, ...), custom_call_target="tpu_custom_call" | custom-call | flops 2576980480 | bytes 5034393 | tf_op jit(solution)/shard_map/conv_fwd/pallas_call | solution.py:136
  122.3 5.3 back.7
  141.2 33.7 %collective-permute-done.6 = bf16[512,2048]{1,0:T(8,128)(2,1)} collective-permute-done((bf16[512,2048]{1,0:T(8,128)(2,1)}, bf16[512,2048]{1,0:T(8,128)(2,1)}, u32[]{:S(2)}, u32[]{:S(2)}) %collective-permute-start.6) | collective-permute-done | bytes 2097184 | tf_op jit(solution)/shard_map/ppermute | solution.py:60
  181.3 21.8 %collective-permute-done.7 = bf16[256,2048]{1,0:T(8,128)(2,1)S(1)} collective-permute-done((bf16[256,2048]{1,0:T(8,128)(2,1)}, bf16[256,2048]{1,0:T(8,128)(2,1)S(1)}, u32[]{:S(2)}, u32[]{:S(2)}) %collective-permute-start.7) | collective-permute-done | bytes 1048608 | tf_op jit(solution)/shard_map/ppermute | solution.py:60
  213.2 19.5 %collective-permute-done.12 = bf16[256,2048]{1,0:T(8,128)(2,1)S(1)} collective-permute-done((bf16[256,2048]{1,0:T(8,128)(2,1)S(1)}, bf16[256,2048]{1,0:T(8,128)(2,1)S(1)}, u32[]{:S(2)}, u32[]{:S(2)}) %collective-permute-start.12) | collective-permute-done | bytes 1048608 | tf_op jit(solution)/shard_map/ppermute | solution.py:60
  240.3 19.2 %all-gather.9.cloned.1.call-done.refs_3_.refs_5_ = bf16[2048,2048]{1,0:T(8,128)(2,1)} async-done(((bf16[256,2048]{1,0:T(8,128)(2,1)}), bf16[2048,2048]{1,0:T(8,128)(2,1)}) %all-gather.9.cloned.1.call-update) | async-done | bytes 8388624 | tf_op jit(solution)/shard_map/all_gather | solution.py:506
  259.5 29.3 %ffn_gate.2 = (bf16[2048,2048]{1,0:T(8,128)(2,1)}, bf16[2048,2048]{1,0:T(8,128)(2,1)}, bf16[2048,2048]{1,0:T(8,128)(2,1)}) custom-call(bf16[512,2048]{1,0:T(8,128)(2,1)} %pad_maximum_fusion.3.refs_0_, bf16[512,2048]{1,0:T(8,128)(2,1)} %copy-done.11, bf16[2048,2048]{1,0:T(8,128)(2,1)} %all-gather.7.cloned.1.call-done.refs_2_.refs_4_, ...), custom_call_target="tpu_custom_call" | custom-call | flops 3435973888 | bytes 9227468 | tf_op jit(solution)/shard_map/ffn_gate/pallas_call | solution.py:136
  292.0 29.1 %ffn_gate.3 = (bf16[2048,2048]{1,0:T(8,128)(2,1)}, bf16[2048,2048]{1,0:T(8,128)(2,1)}, bf16[2048,2048]{1,0:T(8,128)(2,1)}) custom-call(bf16[512,2048]{1,0:T(8,128)(2,1)} %collective-permute-done.11.refs_0_.refs_1_, bf16[512,2048]{1,0:T(8,128)(2,1)} %collective-permute-done.13.refs_1_.refs_3_, ...), custom_call_target="tpu_custom_call", output_to_operand_aliasing={{0}: (4, {}), {1}: (5, {}), {2}: (6, {})} | custom-call | flops 137438953472 | bytes 570425344 | tf_op jit(solution)/shard_map/ffn_gate/pallas_call | solution.py:136
  321.1 13.9 %part_grad.2.refs_3_ = bf16[2048,2048]{1,0:T(8,128)(2,1)} custom-call(bf16[512,2048]{1,0:T(8,128)(2,1)} %constant_dynamic-update-slice_fusion.refs_0_, bf16[512,2048]{1,0:T(8,128)(2,1)} %constant_dynamic-update-slice_fusion.2.refs_1_.refs_2_, bf16[2048,2048]{1,0:T(8,128)(2,1)} %get-tuple-element.111.refs_2_.refs_0_.refs_1_.refs_3_), custom_call_target="tpu_custom_call" | custom-call | flops 1717986944 | bytes 4194304 | tf_op jit(solution)/shard_map/part_grad/pallas_call | solution.py:136
  339.6 15.3 %part_grad.3 = bf16[2048,2048]{1,0:T(8,128)(2,1)} custom-call(bf16[512,2048]{1,0:T(8,128)(2,1)} %copy-done.21, bf16[512,2048]{1,0:T(8,128)(2,1)} %copy-done.22, bf16[2048,2048]{1,0:T(8,128)(2,1)} %get-tuple-element.111.refs_2_.refs_0_.refs_1_.refs_3_, bf16[2048,2048]{1,0:T(8,128)(2,1)} %part_grad.2.refs_3_), custom_call_target="tpu_custom_call" | custom-call | flops 1717986944 | bytes 5872025 | tf_op jit(solution)/shard_map/part_grad/pallas_call | solution.py:136
  354.9 9.9 %reduce-scatter.7.cloned.1.call-start = ((), (), s32[]{:S(2)}) async-start(), calls=%async_computation.9 | async-start | bytes 9437184 | tf_op jit(solution)/shard_map/reduce_scatter | solution.py:507
  364.9 27.2 %ffn_slope.1 = (bf16[2048,2048]{1,0:T(8,128)(2,1)}, bf16[2048,2048]{1,0:T(8,128)(2,1)}) custom-call(bf16[512,2048]{1,0:T(8,128)(2,1)} %constant_dynamic-update-slice_fusion.refs_0_, bf16[512,2048]{1,0:T(8,128)(2,1)} %copy-done.21, bf16[512,2048]{1,0:T(8,128)(2,1)} %constant_dynamic-update-slice_fusion.2.refs_1_.refs_2_, bf16[512,2048]{1,0:T(8,128)(2,1)} %copy-done.22, ...), custom_call_target="tpu_custom_call" | custom-call | flops 3435973888 | bytes 10066329 | tf_op jit(solution)/shard_map/ffn_slope/pallas_call | solution.py:136
  392.0 23.9 %back.9 = (bf16[512,2048]{1,0:T(8,128)(2,1)}, bf16[512,2048]{1,0:T(8,128)(2,1)}) custom-call(bf16[2048,2048]{1,0:T(8,128)(2,1)} %get-tuple-element.104.refs_0_.refs_2_.refs_4_, bf16[2048,2048]{1,0:T(8,128)(2,1)} %get-tuple-element.102.refs_1_.refs_3_.refs_4_, bf16[2048,2048]{1,0:T(8,128)(2,1)} %get-tuple-element.104.refs_0_.refs_2_.refs_4_, ...), custom_call_target="tpu_custom_call" | custom-call | flops 3435973888 | bytes 10905190 | tf_op jit(solution)/shard_map/back/pallas_call | solution.py:136
  418.9 23.8 %back.10 = (bf16[512,2048]{1,0:T(8,128)(2,1)}, bf16[512,2048]{1,0:T(8,128)(2,1)}) custom-call(bf16[2048,2048]{1,0:T(8,128)(2,1)} %get-tuple-element.104.refs_0_.refs_2_.refs_4_, bf16[2048,2048]{1,0:T(8,128)(2,1)} %get-tuple-element.102.refs_1_.refs_3_.refs_4_, bf16[2048,2048]{1,0:T(8,128)(2,1)} %get-tuple-element.104.refs_0_.refs_2_.refs_4_, ...), custom_call_target="tpu_custom_call" | custom-call | flops 3435973888 | bytes 10905190 | tf_op jit(solution)/shard_map/back/pallas_call | solution.py:136
  442.7 23.8 %weight_grad.3 = bf16[2048,2048]{1,0:T(8,128)(2,1)} custom-call(bf16[512,2048]{1,0:T(8,128)(2,1)} %pad_maximum_fusion.3.refs_0_, bf16[512,2048]{1,0:T(8,128)(2,1)} %collective-permute-done.11.refs_0_.refs_1_, bf16[512,2048]{1,0:T(8,128)(2,1)} %copy-done.11, bf16[512,2048]{1,0:T(8,128)(2,1)} %collective-permute-done.13.refs_1_.refs_3_, ...), custom_call_target="tpu_custom_call" | custom-call | flops 3435973888 | bytes 5033164 | tf_op jit(solution)/shard_map/weight_grad/pallas_call | solution.py:136
  471.2 24.3 %back.11 = (bf16[512,2048]{1,0:T(8,128)(2,1)}, bf16[512,2048]{1,0:T(8,128)(2,1)}, bf16[512,2048]{1,0:T(8,128)(2,1)}, bf16[512,2048]{1,0:T(8,128)(2,1)}) custom-call(bf16[2048,2048]{1,0:T(8,128)(2,1)} %get-tuple-element.111.refs_2_.refs_0_.refs_1_.refs_3_, bf16[2048,2048]{1,0:T(8,128)(2,1)} %get-tuple-element.111.refs_2_.refs_0_.refs_1_.refs_3_, ...), custom_call_target="tpu_custom_call" | custom-call | flops 3435973888 | bytes 10066329 | tf_op jit(solution)/shard_map/back/pallas_call | solution.py:136
  510.6 20.4 %collective-permute-done.22 = bf16[256,2048]{1,0:T(8,128)(2,1)S(1)} collective-permute-done((bf16[256,2048]{1,0:T(8,128)(2,1)S(1)}, bf16[256,2048]{1,0:T(8,128)(2,1)S(1)}, u32[]{:S(2)}, u32[]{:S(2)}) %collective-permute-start.22) | collective-permute-done | bytes 1048608 | tf_op jit(solution)/shard_map/ppermute | solution.py:60
  535.3 23.8 %weight_grad.4 = bf16[2048,2048]{1,0:T(8,128)(2,1)} custom-call(bf16[512,2048]{1,0:T(8,128)(2,1)} %pad_maximum_fusion.3.refs_0_, bf16[512,2048]{1,0:T(8,128)(2,1)} %collective-permute-done.11.refs_0_.refs_1_, bf16[512,2048]{1,0:T(8,128)(2,1)} %copy-done.11, bf16[512,2048]{1,0:T(8,128)(2,1)} %collective-permute-done.13.refs_1_.refs_3_, ...), custom_call_target="tpu_custom_call" | custom-call | flops 3435973888 | bytes 5033164 | tf_op jit(solution)/shard_map/weight_grad/pallas_call | solution.py:136
  559.1 17.7 %collective-permute-done.23.refs_3_ = bf16[512,2048]{1,0:T(8,128)(2,1)} collective-permute-done((bf16[512,2048]{1,0:T(8,128)(2,1)S(1)}, bf16[512,2048]{1,0:T(8,128)(2,1)}, u32[]{:S(2)}, u32[]{:S(2)}) %collective-permute-start.23) | collective-permute-done | bytes 2097184 | tf_op jit(solution)/shard_map/ppermute | solution.py:60
  581.8 23.1 %conv_bwd.1 = (bf16[2048,1536]{1,0:T(8,128)(2,1)}, f32[3,512]{1,0:T(4,128)}, bf16[2048,2048]{1,0:T(8,128)(2,1)}) custom-call(s32[2,8]{1,0:T(2,128)} %dynamic-slice_bitcast_fusion.places, bf16[512,2048]{1,0:T(8,128)(2,1)} %pad_maximum_fusion.5.refs_0_, bf16[512,2048]{1,0:T(8,128)(2,1)} %collective-permute-done.21.refs_1_, bf16[512,2048]{1,0:T(8,128)(2,1)} %copy-done.32, ...), custom_call_target="tpu_custom_call" | custom-call | flops 151182852096 | bytes 701503872 | tf_op jit(solution)/shard_map/conv_bwd/pallas_call | solution.py:136
  604.9 11.2 %back.12 = (bf16[512,2048]{1,0:T(8,128)(2,1)}, bf16[512,2048]{1,0:T(8,128)(2,1)}, f32[1,2048]{1,0:T(1,128)}) custom-call(bf16[2048,1536]{1,0:T(8,128)(2,1)} %get-tuple-element.128.refs_0_.refs_1_.refs_4_, bf16[2048,1536]{1,0:T(8,128)(2,1)} %get-tuple-element.128.refs_0_.refs_1_.refs_4_, bf16[2048,2048]{1,0:T(8,128)(2,1)} %all-gather.5.cloned.1.call-done.refs_4_.refs_2_, ...), custom_call_target="tpu_custom_call" | custom-call | flops 1288490240 | bytes 5873664 | tf_op jit(solution)/shard_map/back/pallas_call | solution.py:136
  618.1 10.5 %collective-permute-done.24 = bf16[512,2048]{1,0:T(8,128)(2,1)} collective-permute-done((bf16[512,2048]{1,0:T(8,128)(2,1)}, bf16[512,2048]{1,0:T(8,128)(2,1)}, u32[]{:S(2)}, u32[]{:S(2)}) %collective-permute-start.24) | collective-permute-done | bytes 2097184 | tf_op jit(solution)/shard_map/ppermute | solution.py:60
  630.0 19.5 %weight_grad.5 = bf16[2048,2048]{1,0:T(8,128)(2,1)} custom-call(bf16[512,2048]{1,0:T(8,128)(2,1)} %copy-done.20, bf16[512,2048]{1,0:T(8,128)(2,1)} %collective-permute-done.1.refs_1_.refs_3_, bf16[512,2048]{1,0:T(8,128)(2,1)} %copy-done.19, bf16[512,2048]{1,0:T(8,128)(2,1)} %collective-permute-done.3.refs_3_.refs_4_, ...), custom_call_target="tpu_custom_call", output_to_operand_aliasing={{}: (5, {})} | custom-call | flops 2576980480 | bytes 6291456 | tf_op jit(solution)/shard_map/weight_grad/pallas_call | solution.py:136
  655.1 11.2 %back.13 = (bf16[512,2048]{1,0:T(8,128)(2,1)}, bf16[512,2048]{1,0:T(8,128)(2,1)}, f32[1,2048]{1,0:T(1,128)}) custom-call(bf16[2048,1536]{1,0:T(8,128)(2,1)} %get-tuple-element.128.refs_0_.refs_1_.refs_4_, bf16[2048,1536]{1,0:T(8,128)(2,1)} %get-tuple-element.128.refs_0_.refs_1_.refs_4_, bf16[2048,2048]{1,0:T(8,128)(2,1)} %all-gather.5.cloned.1.call-done.refs_4_.refs_2_, ...), custom_call_target="tpu_custom_call" | custom-call | flops 193273528320 | bytes 881049600 | tf_op jit(solution)/shard_map/back/pallas_call | solution.py:136
  677.5 6.2 collective-permute-done.33
  694.1 6.5 collective-permute-done.31
  706.0 8.8 %collective-permute-done.25 = bf16[256,2048]{1,0:T(8,128)(2,1)S(1)} collective-permute-done((bf16[256,2048]{1,0:T(8,128)(2,1)}, bf16[256,2048]{1,0:T(8,128)(2,1)S(1)}, u32[]{:S(2)}, u32[]{:S(2)}) %collective-permute-start.25) | collective-permute-done | bytes 1048608 | tf_op jit(solution)/shard_map/ppermute | solution.py:60
  719.6 5.6 fusion.6
  735.7 9.2 %reduce-scatter.11.cloned.1.call-done.src = bf16[256,2048]{1,0:T(8,128)(2,1)} async-done(((bf16[2048,2048]{1,0:T(8,128)(2,1)}), bf16[256,2048]{1,0:T(8,128)(2,1)}) %reduce-scatter.11.cloned.1.call-update) | async-done | bytes 1048592 | tf_op jit(solution)/shard_map/reduce_scatter | solution.py:507
  (263 shorter events, 151.5 us)
Async XLA Ops:
  7.2 87.8 %all-gather.5.cloned.1.call-start = ((), (), s32[]{:S(2)}) async-start(), calls=%async_computation.4 | async-start | bytes 9437184 | tf_op jit(solution)/shard_map/all_gather | solution.py:506
  9.7 169.5 %all-gather.7.cloned.1.call-start = ((), (), s32[]{:S(2)}) async-start(), calls=%async_computation.5 | async-start | bytes 9437184 | tf_op jit(solution)/shard_map/all_gather | solution.py:506
  11.7 26.2 %collective-permute-start.2 = (bf16[256,2048]{1,0:T(8,128)(2,1)S(1)}, bf16[256,2048]{1,0:T(8,128)(2,1)S(1)}, u32[]{:S(2)}, u32[]{:S(2)}) collective-permute-start(bf16[256,2048]{1,0:T(8,128)(2,1)S(1)} %get-tuple-element.158), channel_id=1, source_target_pairs={{0,2},{1,3},{2,0},{3,1},{4,6},{5,7},{6,4},{7,5},{8,10},{9,11},{10,... | collective-permute-start | bytes 3145736 | tf_op jit(solution)/shard_map/ppermute | solution.py:60
  38.2 47.1 %collective-permute-start.3 = (bf16[512,2048]{1,0:T(8,128)(2,1)S(1)}, bf16[512,2048]{1,0:T(8,128)(2,1)}, u32[]{:S(2)}, u32[]{:S(2)}) collective-permute-start(bf16[512,2048]{1,0:T(8,128)(2,1)S(1)} %pad_maximum_fusion.2.refs_2_.refs_4_), channel_id=1, source_target_pairs={{0,1},{1,0},{2,3},{3,2},{4,5},{5,4},{6,7},{7,6},{8,9},{9,8},{10,11... | collective-permute-start | bytes 6291464 | tf_op jit(solution)/shard_map/ppermute | solution.py:60
  40.2 46.5 %collective-permute-start.1 = (bf16[512,2048]{1,0:T(8,128)(2,1)S(1)}, bf16[512,2048]{1,0:T(8,128)(2,1)}, u32[]{:S(2)}, u32[]{:S(2)}) collective-permute-start(bf16[512,2048]{1,0:T(8,128)(2,1)S(1)} %pad_maximum_fusion.1.refs_0_.refs_3_), channel_id=1, source_target_pairs={{0,2},{1,3},{2,0},{3,1},{4,6},{5,7},{6,4},{7,5},{8,10},{9,11},{10,... | collective-permute-start | bytes 6291464 | tf_op jit(solution)/shard_map/ppermute | solution.py:60
  95.0 164.4 %all-gather.9.cloned.1.call-start = ((), (), s32[]{:S(2)}) async-start(), calls=%async_computation.6 | async-start | bytes 9437184 | tf_op jit(solution)/shard_map/all_gather | solution.py:506
  95.1 27.2 %collective-permute-start.4 = (bf16[256,2048]{1,0:T(8,128)(2,1)}, bf16[256,2048]{1,0:T(8,128)(2,1)}, u32[]{:S(2)}, u32[]{:S(2)}) collective-permute-start(bf16[256,2048]{1,0:T(8,128)(2,1)} %get-tuple-element.79), channel_id=1, source_target_pairs={{0,1},{1,0},{2,3},{3,2},{4,5},{5,4},{6,7},{7,6},{8,9},{9,8},{10,11... | collective-permute-start | bytes 3145736 | tf_op jit(solution)/shard_map/ppermute | solution.py:60
  96.7 25.7 %collective-permute-start.5 = (bf16[256,2048]{1,0:T(8,128)(2,1)S(1)}, bf16[256,2048]{1,0:T(8,128)(2,1)}, u32[]{:S(2)}, u32[]{:S(2)}) collective-permute-start(bf16[256,2048]{1,0:T(8,128)(2,1)S(1)} %get-tuple-element.80), channel_id=1, source_target_pairs={{0,2},{1,3},{2,0},{3,1},{4,6},{5,7},{6,4},{7,5},{8,10},{9,11},{10,... | collective-permute-start | bytes 3145736 | tf_op jit(solution)/shard_map/ppermute | solution.py:60
  127.6 47.3 %collective-permute-start.6 = (bf16[512,2048]{1,0:T(8,128)(2,1)}, bf16[512,2048]{1,0:T(8,128)(2,1)}, u32[]{:S(2)}, u32[]{:S(2)}) collective-permute-start(bf16[512,2048]{1,0:T(8,128)(2,1)} %get-tuple-element.82), channel_id=1, source_target_pairs={{0,2},{1,3},{2,0},{3,1},{4,6},{5,7},{6,4},{7,5},{8,10},{9,11},{10,... | collective-permute-start | bytes 6291464 | tf_op jit(solution)/shard_map/ppermute | solution.py:60
  128.5 46.7 %collective-permute-start.8 = (bf16[512,2048]{1,0:T(8,128)(2,1)}, bf16[512,2048]{1,0:T(8,128)(2,1)}, u32[]{:S(2)}, u32[]{:S(2)}) collective-permute-start(bf16[512,2048]{1,0:T(8,128)(2,1)} %get-tuple-element.87), channel_id=1, source_target_pairs={{0,1},{1,0},{2,3},{3,2},{4,5},{5,4},{6,7},{7,6},{8,9},{9,8},{10,11... | collective-permute-start | bytes 6291464 | tf_op jit(solution)/shard_map/ppermute | solution.py:60
  179.3 185.6 %all-gather.11.cloned.1.call-start = ((), (), s32[]{:S(2)}) async-start(), calls=%async_computation.7 | async-start | bytes 9437184 | tf_op jit(solution)/shard_map/all_gather | solution.py:506
  232.9 56.0 %collective-permute-start.13 = (bf16[512,2048]{1,0:T(8,128)(2,1)S(1)}, bf16[512,2048]{1,0:T(8,128)(2,1)}, u32[]{:S(2)}, u32[]{:S(2)}) collective-permute-start(bf16[512,2048]{1,0:T(8,128)(2,1)S(1)} %pad_maximum_fusion.4.refs_1_.refs_2_), channel_id=1, source_target_pairs={{0,1},{1,0},{2,3},{3,2},{4,5},{5,4},{6,7},{7,6},{8,9},{9,8},{10,11... | collective-permute-start | bytes 6291464 | tf_op jit(solution)/shard_map/ppermute | solution.py:60
  237.6 51.3 %collective-permute-start.11 = (bf16[512,2048]{1,0:T(8,128)(2,1)}, bf16[512,2048]{1,0:T(8,128)(2,1)}, u32[]{:S(2)}, u32[]{:S(2)}) collective-permute-start(bf16[512,2048]{1,0:T(8,128)(2,1)} %pad_maximum_fusion.3.refs_0_), channel_id=1, source_target_pairs={{0,2},{1,3},{2,0},{3,1},{4,6},{5,7},{6,4},{7,5},{8,10},{9,11},{10,... | collective-permute-start | bytes 6291464 | tf_op jit(solution)/shard_map/ppermute | solution.py:60
  259.5 210.5 %reduce-scatter.5.cloned.1.call-start = ((), (), s32[]{:S(2)}) async-start(), calls=%async_computation.8 | async-start | bytes 9437184 | tf_op jit(solution)/shard_map/reduce_scatter | solution.py:507
  288.9 48.1 %collective-permute-start.14 = (bf16[512,2048]{1,0:T(8,128)(2,1)}, bf16[512,2048]{1,0:T(8,128)(2,1)S(1)}, u32[]{:S(2)}, u32[]{:S(2)}) collective-permute-start(bf16[512,2048]{1,0:T(8,128)(2,1)} %constant_dynamic-update-slice_fusion.refs_0_), channel_id=1, source_target_pairs={{0,2},{1,3},{2,0},{3,1},{4,6},{5,7},{6,4},{7,5},{8,10},{9,11},{10,... | collective-permute-start | bytes 6291464 | tf_op jit(solution)/shard_map/ppermute | solution.py:60
  290.5 47.8 %collective-permute-start.15 = (bf16[512,2048]{1,0:T(8,128)(2,1)}, bf16[512,2048]{1,0:T(8,128)(2,1)S(1)}, u32[]{:S(2)}, u32[]{:S(2)}) collective-permute-start(bf16[512,2048]{1,0:T(8,128)(2,1)} %constant_dynamic-update-slice_fusion.2.refs_1_.refs_2_), channel_id=1, source_target_pairs={{0,1},{1,0},{2,3},{3,2},{4,5},{5,4},{6,7},{7,6},{8,9},{9,8},{10,11... | collective-permute-start | bytes 6291464 | tf_op jit(solution)/shard_map/ppermute | solution.py:60
  354.9 204.1 %reduce-scatter.7.cloned.1.call-start = ((), (), s32[]{:S(2)}) async-start(), calls=%async_computation.9 | async-start | bytes 9437184 | tf_op jit(solution)/shard_map/reduce_scatter | solution.py:507
  415.9 50.6 %collective-permute-start.16 = (bf16[512,2048]{1,0:T(8,128)(2,1)}, bf16[512,2048]{1,0:T(8,128)(2,1)}, u32[]{:S(2)}, u32[]{:S(2)}) collective-permute-start(bf16[512,2048]{1,0:T(8,128)(2,1)} %get-tuple-element.103), channel_id=1, source_target_pairs={{0,2},{1,3},{2,0},{3,1},{4,6},{5,7},{6,4},{7,5},{8,10},{9,11},{10,... | collective-permute-start | bytes 6291464 | tf_op jit(solution)/shard_map/ppermute | solution.py:60
  417.5 52.1 %collective-permute-start.17 = (bf16[512,2048]{1,0:T(8,128)(2,1)}, bf16[512,2048]{1,0:T(8,128)(2,1)S(1)}, u32[]{:S(2)}, u32[]{:S(2)}) collective-permute-start(bf16[512,2048]{1,0:T(8,128)(2,1)} %get-tuple-element.109), channel_id=1, source_target_pairs={{0,1},{1,0},{2,3},{3,2},{4,5},{5,4},{6,7},{7,6},{8,9},{9,8},{10,11... | collective-permute-start | bytes 6291464 | tf_op jit(solution)/shard_map/ppermute | solution.py:60
  470.0 185.1 %reduce-scatter.9.cloned.1.call-start = ((), (), s32[]{:S(2)}) async-start(), calls=%async_computation.10 | async-start | bytes 9437184 | tf_op jit(solution)/shard_map/reduce_scatter | solution.py:507
  470.1 25.5 %collective-permute-start.18 = (bf16[256,2048]{1,0:T(8,128)(2,1)}, bf16[256,2048]{1,0:T(8,128)(2,1)}, u32[]{:S(2)}, u32[]{:S(2)}) collective-permute-start(bf16[256,2048]{1,0:T(8,128)(2,1)} %add_convert_fusion.5), channel_id=1, source_target_pairs={{0,1},{1,0},{2,3},{3,2},{4,5},{5,4},{6,7},{7,6},{8,9},{9,8},{10,11... | collective-permute-start | bytes 3145736 | tf_op jit(solution)/shard_map/ppermute | solution.py:60
  470.8 27.1 %collective-permute-start.19 = (bf16[256,2048]{1,0:T(8,128)(2,1)S(1)}, bf16[256,2048]{1,0:T(8,128)(2,1)}, u32[]{:S(2)}, u32[]{:S(2)}) collective-permute-start(bf16[256,2048]{1,0:T(8,128)(2,1)S(1)} %add_convert_fusion.4), channel_id=1, source_target_pairs={{0,2},{1,3},{2,0},{3,1},{4,6},{5,7},{6,4},{7,5},{8,10},{9,11},{10,... | collective-permute-start | bytes 3145736 | tf_op jit(solution)/shard_map/ppermute | solution.py:60
  531.1 45.7 %collective-permute-start.23 = (bf16[512,2048]{1,0:T(8,128)(2,1)S(1)}, bf16[512,2048]{1,0:T(8,128)(2,1)}, u32[]{:S(2)}, u32[]{:S(2)}) collective-permute-start(bf16[512,2048]{1,0:T(8,128)(2,1)S(1)} %pad_maximum_fusion.6.refs_2_), channel_id=1, source_target_pairs={{0,1},{1,0},{2,3},{3,2},{4,5},{5,4},{6,7},{7,6},{8,9},{9,8},{10,11... | collective-permute-start | bytes 6291464 | tf_op jit(solution)/shard_map/ppermute | solution.py:60
  533.9 45.8 %collective-permute-start.21 = (bf16[512,2048]{1,0:T(8,128)(2,1)}, bf16[512,2048]{1,0:T(8,128)(2,1)}, u32[]{:S(2)}, u32[]{:S(2)}) collective-permute-start(bf16[512,2048]{1,0:T(8,128)(2,1)} %pad_maximum_fusion.5.refs_0_), channel_id=1, source_target_pairs={{0,2},{1,3},{2,0},{3,1},{4,6},{5,7},{6,4},{7,5},{8,10},{9,11},{10,... | collective-permute-start | bytes 6291464 | tf_op jit(solution)/shard_map/ppermute | solution.py:60
  559.1 185.8 %reduce-scatter.11.cloned.1.call-start = ((), (), s32[]{:S(2)}) async-start(), calls=%async_computation.11 | async-start | bytes 9437184 | tf_op jit(solution)/shard_map/reduce_scatter | solution.py:507
  579.7 48.9 %collective-permute-start.24 = (bf16[512,2048]{1,0:T(8,128)(2,1)}, bf16[512,2048]{1,0:T(8,128)(2,1)}, u32[]{:S(2)}, u32[]{:S(2)}) collective-permute-start(bf16[512,2048]{1,0:T(8,128)(2,1)} %get-tuple-element.115), channel_id=1, source_target_pairs={{0,2},{1,3},{2,0},{3,1},{4,6},{5,7},{6,4},{7,5},{8,10},{9,11},{10,... | collective-permute-start | bytes 6291464 | tf_op jit(solution)/shard_map/ppermute | solution.py:60
  581.1 48.9 %collective-permute-start.26 = (bf16[512,2048]{1,0:T(8,128)(2,1)}, bf16[512,2048]{1,0:T(8,128)(2,1)}, u32[]{:S(2)}, u32[]{:S(2)}) collective-permute-start(bf16[512,2048]{1,0:T(8,128)(2,1)} %get-tuple-element.118), channel_id=1, source_target_pairs={{0,1},{1,0},{2,3},{3,2},{4,5},{5,4},{6,7},{7,6},{8,9},{9,8},{10,11... | collective-permute-start | bytes 6291464 | tf_op jit(solution)/shard_map/ppermute | solution.py:60
  616.1 52.3 %collective-permute-start.28 = (bf16[512,2048]{1,0:T(8,128)(2,1)}, bf16[512,2048]{1,0:T(8,128)(2,1)}, u32[]{:S(2)}, u32[]{:S(2)}) collective-permute-start(bf16[512,2048]{1,0:T(8,128)(2,1)} %get-tuple-element.125), channel_id=1, source_target_pairs={{0,2},{1,3},{2,0},{3,1},{4,6},{5,7},{6,4},{7,5},{8,10},{9,11},{10,... | collective-permute-start | bytes 6291464 | tf_op jit(solution)/shard_map/ppermute | solution.py:60
  617.4 55.4 %collective-permute-start.30 = (bf16[512,2048]{1,0:T(8,128)(2,1)}, bf16[512,2048]{1,0:T(8,128)(2,1)}, u32[]{:S(2)}, u32[]{:S(2)}) collective-permute-start(bf16[512,2048]{1,0:T(8,128)(2,1)} %get-tuple-element.131), channel_id=1, source_target_pairs={{0,1},{1,0},{2,3},{3,2},{4,5},{5,4},{6,7},{7,6},{8,9},{9,8},{10,11... | collective-permute-start | bytes 6291464 | tf_op jit(solution)/shard_map/ppermute | solution.py:60
  687.0 27.8 %collective-permute-start.25 = (bf16[256,2048]{1,0:T(8,128)(2,1)}, bf16[256,2048]{1,0:T(8,128)(2,1)S(1)}, u32[]{:S(2)}, u32[]{:S(2)}) collective-permute-start(bf16[256,2048]{1,0:T(8,128)(2,1)} %add_convert_fusion.3), channel_id=1, source_target_pairs={{0,1},{1,0},{2,3},{3,2},{4,5},{5,4},{6,7},{7,6},{8,9},{9,8},{10,11... | collective-permute-start | bytes 3145736 | tf_op jit(solution)/shard_map/ppermute | solution.py:60
  688.4 36.8 %collective-permute-start.27 = (bf16[256,2048]{1,0:T(8,128)(2,1)S(1)}, bf16[256,2048]{1,0:T(8,128)(2,1)S(1)}, u32[]{:S(2)}, u32[]{:S(2)}) collective-permute-start(bf16[256,2048]{1,0:T(8,128)(2,1)S(1)} %copy-done.37), channel_id=1, source_target_pairs={{0,2},{1,3},{2,0},{3,1},{4,6},{5,7},{6,4},{7,5},{8,10},{9,11},{10,... | collective-permute-start | bytes 3145736 | tf_op jit(solution)/shard_map/ppermute | solution.py:60
  700.6 26.4 %collective-permute-start.35 = (f32[8,2048]{1,0:T(8,128)S(1)}, f32[8,2048]{1,0:T(8,128)S(1)}, u32[]{:S(2)}, u32[]{:S(2)}) collective-permute-start(f32[8,2048]{1,0:T(8,128)S(1)} %add.186), channel_id=1, source_target_pairs={{0,1},{1,0},{2,3},{3,2},{4,5},{5,4},{6,7},{7,6},{8,9},{9,8},{10,11... | collective-permute-start | bytes 196616 | tf_op jit(solution)/shard_map/ppermute | solution.py:123
  (71 other events, 657.9 us)
Sparse Core Ops, SparseCore 0:
  10.2 84.7 all-gather.4
  96.6 80.5 all-gather.6
  179.4 79.9 all-gather.8
  261.5 80.5 all-gather.10
  355.1 88.5 reduce-scatter.4
  470.1 86.7 reduce-scatter.6
  559.3 88.4 reduce-scatter.8
  655.2 89.6 reduce-scatter.10
